TPU v7x, 32 devices: a whole 2x2x4 slice. The times are simulated.
32 devices in a mesh: seq: 16 (over z, y, x), chan: 2 (over core).
Axes of the slice: x: 2, y: 2, z: 4, core: 2. Of those that a mesh axis runs over, the one named last changes fastest.
Arguments:
- gate_acts: bfloat16 [16384, 2048], P('seq', 'chan'), may hold values from -40 to 40
- value_acts: bfloat16 [16384, 2048], P('seq', 'chan'), may hold values from -6 to 6
- kernel: bfloat16 [32, 2048], P('chan'), may hold values from -0.125 to 0.125
- norm_gain: float32 [2048], P('chan'), may hold values from 0.1 to 1.9
- out_grad: bfloat16 [16384, 2048], P('seq', 'chan'), may hold values from -30 to 30
Outputs:
- normed: bfloat16 [16384, 2048], P('seq', 'chan')
- gate_grad: bfloat16 [16384, 2048], P('seq', 'chan')
- value_grad: bfloat16 [16384, 2048], P('seq', 'chan')
- kernel_grad: float32 [32, 2048], P('chan')
- gain_grad: float32 [2048], P('chan')
All inputs are finite; a program needn't handle non-finite values.
Results may differ from a plain program's by a relative error of at most 0.0085.
Values may be sent and summed in bfloat16 or wider, within the bound.
No kernel may reach another device: no remote copies, remote signals or barrier semaphores. Data moves between devices by JAX's collectives and lax.ppermute only.
A program may use at most 256 MiB of HBM per device.

v0:
```python
import functools
import math

import jax
import jax.numpy as jnp
from jax import lax
from jax.experimental import pallas as pl
from jax.experimental.pallas import tpu as pltpu
from jax.sharding import PartitionSpec as P

norm_eps = 1e-06
TILE = 256
LANES = 128
HEAD = 64
CHUNKS = 4
MIB = 1 << 20


def params(mib):
    return pltpu.CompilerParams(
        vmem_limit_bytes=mib * MIB, dimension_semantics=("arbitrary",)
    )


def cost(flops, moved):
    return pl.CostEstimate(flops=flops, bytes_accessed=moved, transcendentals=0)


def lane_iota(rows):
    return lax.broadcasted_iota(jnp.int32, (rows, LANES), 1)


def slab(pair):
    return pl.ds(pl.multiple_of(pair * LANES, LANES), LANES)


def odd_device():
    return lax.axis_index("seq") % 2 == 1


def own_row(chunk):
    row = jnp.where(odd_device(), (CHUNKS - 1 - chunk) * TILE, chunk * TILE)
    return pl.multiple_of(row, TILE)


VMEM = pl.BlockSpec(memory_space=pltpu.VMEM)


def held(*arrays):
    return [pltpu.with_memory_space_constraint(array, pltpu.VMEM) for array in arrays]


def after(value, *others):
    return lax.optimization_barrier((value, *others))[0]


def band_body(row_ref, band_ref):
    tiles = row_ref.shape[2] // LANES
    step = pl.program_id(0)
    upper = lane_iota(LANES) >= lax.broadcasted_iota(jnp.int32, (LANES, LANES), 0)
    for half in range(2):
        head = 2 * step + half
        before = jnp.zeros((LANES, LANES), jnp.float32)
        band_ref[head, :, :LANES] = before.astype(band_ref.dtype)
        for tile in range(tiles):
            segment = row_ref[step, half : half + 1, tile * LANES : (tile + 1) * LANES]
            turned = pltpu.roll(
                jnp.broadcast_to(segment, (LANES, LANES)), 0, 1, stride=1, stride_axis=0
            )
            cell = jnp.where(upper, turned, before)
            band_ref[head, :, (tile + 1) * LANES : (tile + 2) * LANES] = cell.astype(
                band_ref.dtype
            )
            before = turned


def band_rows(taps, low, high):
    heads = taps.shape[0]
    return jnp.pad(taps, ((0, 0), (low, high))).reshape(heads // 2, 2, -1)


def bands(rows):
    heads, length = 2 * rows.shape[0], rows.shape[2]
    return pl.pallas_call(
        band_body,
        grid=(heads // 2,),
        in_specs=[VMEM],
        out_specs=VMEM,
        out_shape=pltpu.VMEM((heads, LANES, length + LANES), jnp.bfloat16),
        compiler_params=params(4),
        cost_estimate=cost(heads * LANES * length, 2 * heads * LANES * length),
        name="bands",
    )(*held(rows))


def natural(chunks):
    return [jnp.where(odd_device(), *pair) for pair in zip(chunks[::-1], chunks)]


def extended(own, near, far):
    if len(far) < CHUNKS:
        far = [*far, jnp.zeros_like(near[0])]
    odd = odd_device()
    left = [jnp.where(odd, n, f) for n, f in zip(near, far[::-1])]
    right = [jnp.where(odd, f, n) for n, f in zip(near[::-1], far)]
    return left + own + right


def at_pair(refs, pair):
    return [ref[:, slab(pair)] for ref in refs]


def rows_of(ref, pair):
    return [ref[at : at + TILE, slab(pair)] for at in range(0, ref.shape[0], TILE)]


def layout_scratch(rows, lag):
    wide = (rows + 2 * lag) // TILE * HEAD
    return [
        pltpu.VMEM((2, TILE, wide), jnp.bfloat16),
        pltpu.VMEM((2, TILE, wide - LANES), jnp.bfloat16),
    ]


def lay_out(blocks, even_ref, odd_ref):
    low = lane_iota(TILE) < HEAD
    turned = [pltpu.roll(block, HEAD, 1) for block in blocks]
    for tile in range(len(blocks) // 2):
        cols = slice(tile * LANES, (tile + 1) * LANES)
        first, second = 2 * tile, 2 * tile + 1
        even_ref[0, :, cols] = jnp.where(low, blocks[first], turned[second])
        even_ref[1, :, cols] = jnp.where(low, turned[first], blocks[second])
        if odd_ref is not None and second + 1 < len(blocks):
            odd_ref[0, :, cols] = jnp.where(low, blocks[second], turned[second + 1])
            odd_ref[1, :, cols] = jnp.where(low, turned[second], blocks[second + 1])


def window(even_ref, odd_ref, head, start, width):
    if start % 2 == 0:
        return even_ref[head, :, start * HEAD : start * HEAD + width]
    return odd_ref[head, :, (start - 1) * HEAD : (start - 1) * HEAD + width]


def band_product(band_ref, band_head, even_ref, odd_ref, head, slots, width):
    span = slots * TILE
    tile = jnp.concatenate(
        [band_ref[band_head, :, LANES : LANES + span], band_ref[band_head, :, :span]], axis=0
    )
    data = jnp.concatenate(
        [window(even_ref, odd_ref, head, slot, width) for slot in range(slots)], axis=0
    )
    return jnp.dot(tile, data, preferred_element_type=jnp.float32)


def token_blocks(first, second):
    low = lane_iota(TILE) < HEAD
    blocks = []
    for tile in range(first.shape[1] // LANES):
        cols = slice(tile * LANES, (tile + 1) * LANES)
        one, two = first[:, cols], second[:, cols]
        blocks.append(jnp.where(low, one, pltpu.roll(two, HEAD, 1)))
        blocks.append(jnp.where(low, pltpu.roll(one, HEAD, 1), two))
    return blocks


def last_term(band_ref, pair, last):
    low = lane_iota(TILE) < HEAD
    at = jnp.where(odd_device(), band_ref.shape[2] - LANES - TILE, 0)
    parts = []
    for half in range(2):
        head = 2 * pair + half
        tile = jnp.concatenate(
            [
                band_ref[head, :, pl.ds(pl.multiple_of(at + LANES, LANES), TILE)],
                band_ref[head, :, pl.ds(pl.multiple_of(at, LANES), TILE)],
            ],
            axis=0,
        )
        parts.append(jnp.dot(tile, last, preferred_element_type=jnp.float32))
    return jnp.where(low, *parts)


def split_body(value_ref, *refs):
    chunk_refs, sems = refs[:CHUNKS], refs[CHUNKS]
    copies = []
    for chunk, ref in enumerate(chunk_refs):
        copies.append(
            pltpu.make_async_copy(
                value_ref.at[pl.ds(own_row(chunk), TILE), :], ref, sems.at[chunk]
            )
        )
        copies[-1].start()
    for copy in copies:
        copy.wait()


def split(value):
    rows, width = value.shape
    return pl.pallas_call(
        split_body,
        in_specs=[pl.BlockSpec(memory_space=pltpu.HBM)],
        out_specs=[VMEM] * CHUNKS,
        out_shape=[pltpu.VMEM((TILE, width), value.dtype)] * CHUNKS,
        scratch_shapes=[pltpu.SemaphoreType.DMA((CHUNKS,))],
        compiler_params=pltpu.CompilerParams(vmem_limit_bytes=2 * MIB),
        cost_estimate=cost(0, 4 * rows * width),
        name="split",
    )(pltpu.with_memory_space_constraint(value, pltpu.HBM))


def product_flops(rows, width, lag):
    return 2 * (width // HEAD) * TILE * (TILE + 2 * lag) * rows // TILE * HEAD


def token_sums(square_ref, inner_ref, sums_ref, start):
    for at in range(0, square_ref.shape[0], LANES):
        rows = slice(at, at + LANES)
        cols = pl.ds(pl.multiple_of(start + at, LANES), LANES)
        sums_ref[0:1, cols] = jnp.sum(square_ref[rows, :].T, axis=0, keepdims=True)
        sums_ref[1:2, cols] = jnp.sum(inner_ref[rows, :].T, axis=0, keepdims=True)


def add_sums(mixed, gate, grad, gain, square_ref, inner_ref, at):
    hidden = gate.astype(jnp.float32) * mixed
    square_ref[at, :] += hidden * hidden
    inner_ref[at, :] += gain * grad.astype(jnp.float32) * hidden


def forward_body(slots, band_ref, own_ref, gate_ref, grad_ref, gain_ref, *refs):
    near_refs, far_refs, refs = refs[:CHUNKS], refs[CHUNKS : 2 * CHUNKS - 1], refs[2 * CHUNKS - 1 :]
    mixed_ref, sums_ref, even_ref, odd_ref, square_ref, inner_ref = refs
    pair = pl.program_id(0)

    @pl.when(pair == 0)
    def _():
        square_ref[...] = jnp.zeros_like(square_ref)
        inner_ref[...] = jnp.zeros_like(inner_ref)

    blocks = extended(rows_of(own_ref, pair), at_pair(near_refs, pair), at_pair(far_refs, pair))
    lay_out(blocks, even_ref, odd_ref)
    width = mixed_ref.shape[0] // TILE * HEAD
    results = [
        band_product(band_ref, 2 * pair + half, even_ref, odd_ref, half, slots, width)
        for half in range(2)
    ]
    lanes = slab(pair)
    for index, mixed in enumerate(token_blocks(*results)):
        at = slice(index * TILE, (index + 1) * TILE)
        mixed_ref[at, lanes] = mixed
        add_sums(
            mixed, gate_ref[at, lanes], grad_ref[at, lanes], gain_ref[:, lanes], square_ref, inner_ref, at
        )

    @pl.when(pair == pl.num_programs(0) - 1)
    def _():
        token_sums(square_ref, inner_ref, sums_ref, 0)


def forward(band, own, near, far, gate, grad, gain, lag):
    rows, width = gate.shape
    slots = 1 + 2 * lag // TILE
    operands = held(band, own, gate, grad, gain, *near, *far)
    return pl.pallas_call(
        functools.partial(forward_body, slots),
        grid=(width // LANES,),
        in_specs=[VMEM] * len(operands),
        out_specs=[VMEM] * 2,
        out_shape=[
            pltpu.VMEM((rows, width), jnp.float32),
            pltpu.VMEM((2, rows), jnp.float32),
        ],
        scratch_shapes=layout_scratch(rows, lag)
        + [pltpu.VMEM((rows, LANES), jnp.float32)] * 2,
        compiler_params=params(10),
        cost_estimate=cost(product_flops(rows, width, lag), 16 * rows * width),
        name="forward",
    )(*operands)


def forward_last_body(band_ref, last_ref, gate_ref, grad_ref, gain_ref, mixed_ref, sums_ref, *refs):
    first_ref, out_ref, square_ref, inner_ref = refs
    pair = pl.program_id(0)

    @pl.when(pair == 0)
    def _():
        square_ref[...] = jnp.zeros_like(square_ref)
        inner_ref[...] = jnp.zeros_like(inner_ref)
        out_ref[...] = sums_ref[...]

    lanes, rows = slab(pair), pl.ds(own_row(0), TILE)
    mixed = mixed_ref[rows, lanes] + last_term(band_ref, pair, last_ref[:, lanes])
    first_ref[:, lanes] = mixed
    add_sums(
        mixed,
        gate_ref[rows, lanes],
        grad_ref[rows, lanes],
        gain_ref[:, lanes],
        square_ref,
        inner_ref,
        slice(None),
    )

    @pl.when(pair == pl.num_programs(0) - 1)
    def _():
        token_sums(square_ref, inner_ref, out_ref, own_row(0))


def forward_last(band, last, gate, grad, gain, mixed, sums):
    rows, width = gate.shape
    operands = held(band, last, gate, grad, gain, mixed, sums)
    return pl.pallas_call(
        forward_last_body,
        grid=(width // LANES,),
        in_specs=[VMEM] * len(operands),
        out_specs=[VMEM] * 2,
        out_shape=[
            pltpu.VMEM((TILE, width), jnp.float32),
            pltpu.VMEM((2, rows), jnp.float32),
        ],
        scratch_shapes=[pltpu.VMEM((TILE, LANES), jnp.float32)] * 2,
        compiler_params=params(6),
        cost_estimate=cost(8 * TILE * TILE * width, 6 * TILE * width),
        name="forward_last",
    )(*operands)


def token_columns(full_width, sums_ref, tokens):
    scale = lax.rsqrt(sums_ref[0:1, tokens] / full_width + norm_eps)
    pull = scale * scale * sums_ref[1:2, tokens] / full_width
    return (
        jnp.broadcast_to(scale, (LANES, LANES)).T,
        jnp.broadcast_to(pull, (LANES, LANES)).T,
    )


def mix_grad_body(full_width, sums_ref, mixed_ref, first_ref, gate_ref, grad_ref, gain_ref, *refs):
    out_refs, gain_grad_ref, total_ref = refs[:-2], refs[-2], refs[-1]
    total_ref[...] = jnp.zeros_like(total_ref)
    for chunk, out_ref in enumerate(out_refs):
        for at in range(0, TILE, LANES):
            tokens = pl.ds(pl.multiple_of(own_row(chunk) + at, LANES), LANES)
            rows = slice(at, at + LANES)
            scale, pull = token_columns(full_width, sums_ref, tokens)
            for lane in range(0, mixed_ref.shape[1], LANES):
                cols = slice(lane, lane + LANES)
                gate = gate_ref[tokens, cols].astype(jnp.float32)
                grad = grad_ref[tokens, cols].astype(jnp.float32)
                mixed = mixed_ref[tokens, cols] if chunk else first_ref[rows, cols]
                hidden = gate * mixed
                hidden_grad = scale * (gain_ref[:, cols] * grad - hidden * pull)
                out_ref[rows, cols] = (hidden_grad * gate).astype(out_ref.dtype)
                total_ref[:, cols] += jnp.sum(
                    (grad * (hidden * scale)).reshape(LANES // 8, 8, LANES), axis=0
                )
    gain_grad_ref[...] = jnp.sum(total_ref[...], axis=0, keepdims=True)


def mix_grad_of(full_width, *operands):
    rows, width = operands[1].shape
    operands = held(*operands)
    *chunks, gain_sums = pl.pallas_call(
        functools.partial(mix_grad_body, full_width),
        in_specs=[VMEM] * len(operands),
        out_specs=[VMEM] * (CHUNKS + 1),
        out_shape=[pltpu.VMEM((TILE, width), jnp.bfloat16)] * CHUNKS
        + [pltpu.VMEM((1, width), jnp.float32)],
        scratch_shapes=[pltpu.VMEM((8, width), jnp.float32)],
        compiler_params=pltpu.CompilerParams(vmem_limit_bytes=4 * MIB),
        cost_estimate=cost(14 * rows * width, 10 * rows * width),
        name="mix_grad",
    )(*operands)
    return chunks, gain_sums


def norm_body(full_width, sums_ref, mixed_ref, first_ref, gate_ref, grad_ref, gain_ref, *refs):
    normed_ref, gate_grad_ref = refs
    start = pl.program_id(0) * LANES
    tokens = pl.ds(pl.multiple_of(start, LANES), LANES)
    within = pl.ds(pl.multiple_of(lax.rem(start, TILE), LANES), LANES)
    first = start // TILE == own_row(0) // TILE
    scale, pull = token_columns(full_width, sums_ref, tokens)
    for lane in range(0, mixed_ref.shape[1], LANES):
        cols = slice(lane, lane + LANES)
        gain = gain_ref[:, cols]
        gate = gate_ref[tokens, cols].astype(jnp.float32)
        mixed = jnp.where(first, first_ref[within, cols], mixed_ref[tokens, cols])
        grad = grad_ref[tokens, cols].astype(jnp.float32)
        hidden = gate * mixed
        normed_ref[:, cols] = (hidden * scale * gain).astype(normed_ref.dtype)
        hidden_grad = scale * (gain * grad - hidden * pull)
        gate_grad_ref[:, cols] = (hidden_grad * mixed).astype(gate_grad_ref.dtype)


def norm(full_width, *operands):
    rows, width = operands[1].shape
    operands = held(*operands)
    big = jax.ShapeDtypeStruct((rows, width), jnp.bfloat16)
    return pl.pallas_call(
        functools.partial(norm_body, full_width),
        grid=(rows // LANES,),
        in_specs=[VMEM] * len(operands),
        out_specs=[pl.BlockSpec((LANES, width), lambda g: (g, 0))] * 2,
        out_shape=[big, big],
        compiler_params=params(6),
        cost_estimate=cost(14 * rows * width, 12 * rows * width),
        name="norm",
    )(*operands)


def kernel_grad_body(slots, gain_ref, own_ref, *refs):
    near_refs, far_refs, refs = refs[:CHUNKS], refs[CHUNKS : 2 * CHUNKS], refs[2 * CHUNKS :]
    mix_refs, (out_ref, even_ref, odd_ref, mix_even_ref, cells_ref) = refs[:CHUNKS], refs[CHUNKS:]
    pair = pl.program_id(0)
    blocks = extended(rows_of(own_ref, pair), at_pair(near_refs, pair), at_pair(far_refs, pair))
    lay_out(blocks, even_ref, odd_ref)
    blocks = natural(at_pair(mix_refs, pair))
    lay_out(blocks, mix_even_ref, None)
    width = len(blocks) * HEAD
    span = cells_ref.shape[1]
    lags = span - LANES
    gains = gain_ref[:, slab(pair)]
    for half in range(2):
        mix = mix_even_ref[half]
        carry = None
        for lag_slot in range(slots):
            cross = lax.dot_general(
                window(even_ref, odd_ref, half, slots - 1 - lag_slot, width),
                mix,
                (((1,), (1,)), ((), ())),
                preferred_element_type=jnp.float32,
            )
            at = 2 * lag_slot * LANES
            upper, lower = cross[:LANES], cross[LANES:]
            if carry is not None:
                cells_ref[:, at - LANES : at] = carry + lower[:, :LANES]
            cells_ref[:, at : at + LANES] = upper[:, :LANES] + lower[:, LANES:]
            carry = upper[:, LANES:]
        total = cells_ref[0:8, :]
        for group in range(1, LANES // 8):
            total += pltpu.roll(cells_ref[8 * group : 8 * group + 8, :], span - 8 * group, 1)
        row = lax.broadcasted_iota(jnp.int32, (8, span), 0)
        for bit in (1, 2, 4):
            total = jnp.where((row & bit) != 0, pltpu.roll(total, span - bit, 1), total)
        sums = jnp.concatenate(
            [
                jnp.sum(total, axis=0, keepdims=True)[:, :lags],
                gains if half == 0 else pltpu.roll(gains, HEAD, 1),
            ],
            axis=1,
        )
        tall = min(8, out_ref.shape[0])
        row = 2 * pair + half
        group = pl.ds(pl.multiple_of(row // tall * tall, tall), tall)
        here = lax.broadcasted_iota(jnp.int32, (tall, out_ref.shape[1]), 0) == lax.rem(row, tall)
        out_ref[group, :] = jnp.where(here, sums, out_ref[group, :])


def kernel_grad_local(gain_sums, own, near, far, mix_grad, lag):
    rows, width = own.shape
    pairs = width // LANES
    slots = 1 + 2 * lag // TILE
    operands = held(gain_sums, own, *near, *far, *mix_grad)
    return pl.pallas_call(
        functools.partial(kernel_grad_body, slots),
        grid=(pairs,),
        in_specs=[VMEM] * len(operands),
        out_specs=VMEM,
        out_shape=pltpu.VMEM((2 * pairs, 2 * lag + LANES), jnp.float32),
        scratch_shapes=layout_scratch(rows, lag)
        + [
            pltpu.VMEM((2, TILE, rows // TILE * HEAD), jnp.bfloat16),
            pltpu.VMEM((LANES, 2 * lag + LANES), jnp.float32),
        ],
        compiler_params=params(10),
        cost_estimate=cost(product_flops(rows, width, lag), 8 * rows * width),
        name="kernel_grad",
    )(*operands)


def value_grad_body(slots, band_ref, *refs):
    own_refs, near_refs, refs = refs[:CHUNKS], refs[CHUNKS : 2 * CHUNKS], refs[2 * CHUNKS :]
    far_refs, (out_ref, first_ref, even_ref, odd_ref) = refs[: CHUNKS - 1], refs[CHUNKS - 1 :]
    pair = pl.program_id(0)
    own = natural(at_pair(own_refs, pair))
    blocks = extended(own, at_pair(near_refs, pair), at_pair(far_refs, pair))
    lay_out(blocks, even_ref, odd_ref)
    width = len(own) * HEAD
    results = [
        band_product(band_ref, 2 * pair + half, even_ref, odd_ref, half, slots, width)
        for half in range(2)
    ]
    blocks = token_blocks(*results)
    first_ref[:, slab(pair)] = jnp.where(odd_device(), blocks[-1], blocks[0])
    for index, block in enumerate(blocks):
        out_ref[index * TILE : (index + 1) * TILE, :] = block.astype(out_ref.dtype)


def value_grad_of(band, own, near, far, lag):
    rows, width = len(own) * TILE, own[0].shape[1]
    slots = 1 + 2 * lag // TILE
    operands = held(band, *own, *near, *far)
    return pl.pallas_call(
        functools.partial(value_grad_body, slots),
        grid=(width // LANES,),
        in_specs=[VMEM] * len(operands),
        out_specs=[pl.BlockSpec((rows, LANES), lambda g: (0, g)), VMEM],
        out_shape=[
            jax.ShapeDtypeStruct((rows, width), jnp.bfloat16),
            pltpu.VMEM((TILE, width), jnp.float32),
        ],
        scratch_shapes=layout_scratch(rows, lag),
        compiler_params=params(10),
        cost_estimate=cost(product_flops(rows, width, lag), 12 * rows * width),
        name="value_grad",
    )(*operands)


def value_grad_last_body(band_ref, last_ref, first_ref, rest_ref, out_ref, block_ref, sem):
    pair = pl.program_id(0)
    lanes = slab(pair)
    block = first_ref[:, lanes] + last_term(band_ref, pair, last_ref[:, lanes])
    block_ref[:, lanes] = block.astype(block_ref.dtype)

    @pl.when(pair == pl.num_programs(0) - 1)
    def _():
        copy = pltpu.make_async_copy(block_ref, out_ref.at[pl.ds(own_row(0), TILE), :], sem)
        copy.start()
        copy.wait()


def value_grad_last(band, last, first, rest):
    width = first.shape[1]
    operands = held(band, last, first)
    return pl.pallas_call(
        value_grad_last_body,
        grid=(width // LANES,),
        in_specs=[VMEM] * len(operands) + [pl.BlockSpec(memory_space=pl.ANY)],
        out_specs=pl.BlockSpec(memory_space=pl.ANY),
        out_shape=jax.ShapeDtypeStruct(rest.shape, rest.dtype),
        input_output_aliases={len(operands): 0},
        scratch_shapes=[pltpu.VMEM((TILE, width), jnp.bfloat16), pltpu.SemaphoreType.DMA(())],
        compiler_params=params(6),
        cost_estimate=cost(8 * TILE * TILE * width, 6 * TILE * width),
        name="value_grad_last",
    )(*operands, rest)


def swapped(chunk):
    count = lax.axis_size("seq")
    return lax.ppermute(chunk, "seq", [(i, i ^ 1) for i in range(count)])


def relayed(chunk):
    count = lax.axis_size("seq")
    pairs = [(i, i + 2) if i % 2 == 0 else (i, i - 2) for i in range(count)]
    return lax.ppermute(chunk, "seq", [(i, j) for i, j in pairs if 0 <= j < count])


def sum_over_bits(value, bits):
    count = lax.axis_size("seq")
    total = value
    for mask in range(1, 1 << len(bits)):
        flip = sum(1 << bit for at, bit in enumerate(bits) if mask >> at & 1)
        total += lax.ppermute(value, "seq", [(i, i ^ flip) for i in range(count)])
    return total


def sum_over(value, axis):
    count = lax.axis_size(axis)
    if count & (count - 1):
        return lax.psum(value, axis)
    for bit in range(count.bit_length() - 1):
        value += lax.ppermute(value, axis, [(i, i ^ (1 << bit)) for i in range(count)])
    return value


def on_device(gate_acts, value_acts, kernel, norm_gain, out_grad):
    rows, width = value_acts.shape
    heads = kernel.shape[0]
    lag = kernel.shape[1] // 2
    count = lax.axis_size("seq")
    assert width == heads * HEAD and rows == lag == CHUNKS * TILE
    assert count & (count - 1) == 0
    full_width = width * lax.axis_size("chan")
    gain = norm_gain.reshape(1, width)
    taps = kernel.astype(jnp.float32)

    ahead, behind = lax.optimization_barrier(
        (band_rows(taps[:, ::-1], 1, TILE - 1), band_rows(taps, 0, TILE))
    )
    band = bands(ahead)
    *chunks, last = split(value_acts)
    near = [swapped(chunk) for chunk in [*chunks, after(last, band)]]
    far = [relayed(chunk) for chunk in near]
    mixed, sums = forward(band, value_acts, near, far[:-1], gate_acts, out_grad, gain, lag)
    first, sums = forward_last(band, far[-1], gate_acts, out_grad, gain, mixed, sums)
    sums = sum_over(sums, "chan")
    args = (mixed, first, gate_acts, out_grad, gain)
    mix_grad, gain_sums = mix_grad_of(full_width, sums, *args)

    grad_near = [swapped(chunk) for chunk in mix_grad]
    totals = kernel_grad_local(gain_sums, value_acts, near, far, mix_grad, lag)
    bits = list(range(count.bit_length() - 1))
    grad_near[0], totals = lax.optimization_barrier((grad_near[0], totals))
    back_band = bands(after(behind, grad_near[0]))
    normed, gate_grad = norm(full_width, after(sums, grad_near[1]), *args)
    for bit in bits[2:]:
        totals = sum_over_bits(totals, [bit])
    grad_near[1], totals = lax.optimization_barrier((grad_near[1], totals))
    grad_far = [relayed(chunk) for chunk in grad_near]
    totals, *grad_far[:2] = lax.optimization_barrier((totals, *grad_far[:2]))
    totals = sum_over_bits(totals, bits[:2])
    grad_far[0], normed, gate_grad = lax.optimization_barrier((grad_far[0], normed, gate_grad))
    value_grad, first = value_grad_of(back_band, mix_grad, grad_near, grad_far[:-1], lag)
    value_grad = value_grad_last(back_band, grad_far[-1], first, value_grad)
    tokens = rows * count
    kernel_grad = totals[:, : 2 * lag] / math.sqrt(tokens * HEAD)
    gain_grad = totals[:, 2 * lag : 2 * lag + HEAD].reshape(width) / math.sqrt(tokens)
    return (normed, gate_grad, value_grad, kernel_grad, gain_grad)


def solution(mesh):
    placed = (P("seq", "chan"), P("seq", "chan"), P("chan", None), P("chan"), P("seq", "chan"))
    return jax.shard_map(
        on_device,
        mesh=mesh,
        in_specs=placed,
        out_specs=(
            P("seq", "chan"),
            P("seq", "chan"),
            P("seq", "chan"),
            P("chan", None),
            P("chan"),
        ),
        check_vma=False,
    )
```

profile of v0, /device:TPU:0, one launch (start us, length us, event | category | flops | bytes accessed | tf_op | source)
XLA Modules:
  0.0 152.6 jit_solution(8448161383760555964)
XLA Ops:
  3.0 3.0 %collective-permute-start.2 = (bf16[256,1024]{1,0:T(8,128)(2,1)}, bf16[256,1024]{1,0:T(8,128)(2,1)S(1)}, u32[]{:S(2)}, u32[]{:S(2)}) collective-permute-start(bf16[256,1024]{1,0:T(8,128)(2,1)} %get-tuple-element.40), channel_id=1, source_target_pairs={{0,2},{2,0},{4,6},{6,4},{8,10},{10,8},{12,14},{14,12},{16,18},{18,... | collective-permute-start | bytes 1572872 | tf_op jit(solution)/shard_map/ppermute | solution.py:550
  11.2 3.1 %bands.2.band_ref = bf16[16,128,2432]{2,1,0:T(8,128)(2,1)S(1)} custom-call(f32[8,2,2304]{2,1,0:T(2,128)S(1)} %reshape.22.row_ref), custom_call_target="tpu_custom_call" | custom-call | flops 4718592 | bytes 9437184 | tf_op jit(solution)/shard_map/bands/pallas_call | solution.py:84
  14.4 4.6 %collective-permute-done.2.refs_0_ = bf16[256,1024]{1,0:T(8,128)(2,1)S(1)} collective-permute-done((bf16[256,1024]{1,0:T(8,128)(2,1)}, bf16[256,1024]{1,0:T(8,128)(2,1)S(1)}, u32[]{:S(2)}, u32[]{:S(2)}) %collective-permute-start.2) | collective-permute-done | bytes 524320 | tf_op jit(solution)/shard_map/ppermute | solution.py:550
  19.0 4.0 %collective-permute-start.5 = (bf16[256,1024]{1,0:T(8,128)(2,1)S(1)}, bf16[256,1024]{1,0:T(8,128)(2,1)S(1)}, u32[]{:S(2)}, u32[]{:S(2)}) collective-permute-start(bf16[256,1024]{1,0:T(8,128)(2,1)S(1)} %collective-permute-done.2.refs_0_), channel_id=1, source_target_pairs={{0,4},{4,8},{6,2},{8,12},{10,6},{12,16},{14,10},{16,20},{18,14},{2... | collective-permute-start | bytes 1572872 | tf_op jit(solution)/shard_map/ppermute | solution.py:556
  23.0 7.2 %collective-permute-done.3.refs_1_ = bf16[256,1024]{1,0:T(8,128)(2,1)S(1)} collective-permute-done((bf16[256,1024]{1,0:T(8,128)(2,1)S(1)}, bf16[256,1024]{1,0:T(8,128)(2,1)S(1)}, u32[]{:S(2)}, u32[]{:S(2)}) %collective-permute-start.3) | collective-permute-done | bytes 524320 | tf_op jit(solution)/shard_map/ppermute | solution.py:550
  30.2 4.0 %collective-permute-start.6 = (bf16[256,1024]{1,0:T(8,128)(2,1)S(1)}, bf16[256,1024]{1,0:T(8,128)(2,1)S(1)}, u32[]{:S(2)}, u32[]{:S(2)}) collective-permute-start(bf16[256,1024]{1,0:T(8,128)(2,1)S(1)} %collective-permute-done.3.refs_1_), channel_id=1, source_target_pairs={{0,4},{4,8},{6,2},{8,12},{10,6},{12,16},{14,10},{16,20},{18,14},{2... | collective-permute-start | bytes 1572872 | tf_op jit(solution)/shard_map/ppermute | solution.py:556
  34.3 7.2 %collective-permute-done.4.refs_2_ = bf16[256,1024]{1,0:T(8,128)(2,1)S(1)} collective-permute-done((bf16[256,1024]{1,0:T(8,128)(2,1)S(1)}, bf16[256,1024]{1,0:T(8,128)(2,1)S(1)}, u32[]{:S(2)}, u32[]{:S(2)}) %collective-permute-start.4) | collective-permute-done | bytes 524320 | tf_op jit(solution)/shard_map/ppermute | solution.py:550
  41.5 4.0 %collective-permute-start.7 = (bf16[256,1024]{1,0:T(8,128)(2,1)S(1)}, bf16[256,1024]{1,0:T(8,128)(2,1)S(1)}, u32[]{:S(2)}, u32[]{:S(2)}) collective-permute-start(bf16[256,1024]{1,0:T(8,128)(2,1)S(1)} %collective-permute-done.4.refs_2_), channel_id=1, source_target_pairs={{0,4},{4,8},{6,2},{8,12},{10,6},{12,16},{14,10},{16,20},{18,14},{2... | collective-permute-start | bytes 1572872 | tf_op jit(solution)/shard_map/ppermute | solution.py:556
  45.5 6.4 %collective-permute-done.refs_3_ = bf16[256,1024]{1,0:T(8,128)(2,1)S(1)} collective-permute-done((bf16[256,1024]{1,0:T(8,128)(2,1)S(1)}, bf16[256,1024]{1,0:T(8,128)(2,1)S(1)}, u32[]{:S(2)}, u32[]{:S(2)}) %collective-permute-start) | collective-permute-done | bytes 524320 | tf_op jit(solution)/shard_map/ppermute | solution.py:550
  51.9 3.7 %collective-permute-start.1 = (bf16[256,1024]{1,0:T(8,128)(2,1)S(1)}, bf16[256,1024]{1,0:T(8,128)(2,1)S(1)}, u32[]{:S(2)}, u32[]{:S(2)}) collective-permute-start(bf16[256,1024]{1,0:T(8,128)(2,1)S(1)} %collective-permute-done.refs_3_), channel_id=1, source_target_pairs={{0,4},{4,8},{6,2},{8,12},{10,6},{12,16},{14,10},{16,20},{18,14},{2... | collective-permute-start | bytes 1572872 | tf_op jit(solution)/shard_map/ppermute | solution.py:556
  55.7 10.9 %forward.1 = (f32[1024,1024]{1,0:T(8,128)S(1)}, f32[2,1024]{1,0:T(2,128)S(1)}) custom-call(bf16[16,128,2432]{2,1,0:T(8,128)(2,1)S(1)} %bands.2.band_ref, bf16[1024,1024]{1,0:T(8,128)(2,1)S(1)} %copy-done.2, bf16[1024,1024]{1,0:T(8,128)(2,1)S(1)} %copy-done, bf16[1024,1024]{1,0:T(8,128)(2,1)S(1)} %copy-done.1, f32[1,1024]{1,0:T(1,128)S(1)} %bitcast.1, ...), custom_call_target="tpu_custom_call" | custom-call | flops 4831838208 | bytes 16777216 | tf_op jit(solution)/shard_map/forward/pallas_call | solution.py:263
  75.5 12.8 %kernel_grad.1 = f32[16,2176]{1,0:T(8,128)S(1)} custom-call(f32[1,1024]{1,0:T(1,128)S(1)} %get-tuple-element.49.gain_ref, bf16[1024,1024]{1,0:T(8,128)(2,1)S(1)} %copy-done.2, bf16[256,1024]{1,0:T(8,128)(2,1)S(1)} %collective-permute-done.2.refs_0_, bf16[256,1024]{1,0:T(8,128)(2,1)S(1)} %collective-permute-done.3.refs_1_, ...), custom_call_target="tpu_custom_call" | custom-call | flops 4831838208 | bytes 8388608 | tf_op jit(solution)/shard_map/kernel_grad/pallas_call | solution.py:463
  90.0 3.5 %collective-permute-done.11 = f32[16,2176]{1,0:T(8,128)S(1)} collective-permute-done((f32[16,2176]{1,0:T(8,128)S(1)}, f32[16,2176]{1,0:T(8,128)S(1)}, u32[]{:S(2)}, u32[]{:S(2)}) %collective-permute-start.11) | collective-permute-done | bytes 139296 | tf_op jit(solution)/shard_map/ppermute | solution.py:564
  93.5 2.7 %collective-permute-start.12 = (f32[16,2176]{1,0:T(8,128)S(1)}, f32[16,2176]{1,0:T(8,128)S(1)}, u32[]{:S(2)}, u32[]{:S(2)}) collective-permute-start(f32[16,2176]{1,0:T(8,128)S(1)} %add.23), channel_id=1, source_target_pairs={{0,16},{2,18},{4,20},{6,22},{8,24},{10,26},{12,28},{14,30},{16,0},... | collective-permute-start | bytes 417800 | tf_op jit(solution)/shard_map/ppermute | solution.py:564
  97.6 3.1 %collective-permute-start.13 = (bf16[256,1024]{1,0:T(8,128)(2,1)S(1)}, bf16[256,1024]{1,0:T(8,128)(2,1)S(1)}, u32[]{:S(2)}, u32[]{:S(2)}) collective-permute-start(bf16[256,1024]{1,0:T(8,128)(2,1)S(1)} %collective-permute-done.10.refs_4_), channel_id=1, source_target_pairs={{0,4},{4,8},{6,2},{8,12},{10,6},{12,16},{14,10},{16,20},{18,14},{2... | collective-permute-start | bytes 1572872 | tf_op jit(solution)/shard_map/ppermute | solution.py:556
  101.5 4.3 %collective-permute-start.14 = (bf16[256,1024]{1,0:T(8,128)(2,1)S(1)}, bf16[256,1024]{1,0:T(8,128)(2,1)S(1)}, u32[]{:S(2)}, u32[]{:S(2)}) collective-permute-start(bf16[256,1024]{1,0:T(8,128)(2,1)S(1)} %collective-permute-done.9.refs_5_), channel_id=1, source_target_pairs={{0,4},{4,8},{6,2},{8,12},{10,6},{12,16},{14,10},{16,20},{18,14},{2... | collective-permute-start | bytes 1572872 | tf_op jit(solution)/shard_map/ppermute | solution.py:556
  105.9 3.2 %collective-permute-done.17.refs_6_ = bf16[256,1024]{1,0:T(8,128)(2,1)S(1)} collective-permute-done((bf16[256,1024]{1,0:T(8,128)(2,1)S(1)}, bf16[256,1024]{1,0:T(8,128)(2,1)S(1)}, u32[]{:S(2)}, u32[]{:S(2)}) %collective-permute-start.17) | collective-permute-done | bytes 524320 | tf_op jit(solution)/shard_map/ppermute | solution.py:550
  109.1 4.0 %collective-permute-start.18 = (bf16[256,1024]{1,0:T(8,128)(2,1)S(1)}, bf16[256,1024]{1,0:T(8,128)(2,1)S(1)}, u32[]{:S(2)}, u32[]{:S(2)}) collective-permute-start(bf16[256,1024]{1,0:T(8,128)(2,1)S(1)} %collective-permute-done.17.refs_6_), channel_id=1, source_target_pairs={{0,4},{4,8},{6,2},{8,12},{10,6},{12,16},{14,10},{16,20},{18,14},{2... | collective-permute-start | bytes 1572872 | tf_op jit(solution)/shard_map/ppermute | solution.py:556
  113.0 6.5 %collective-permute-done.15.refs_7_ = bf16[256,1024]{1,0:T(8,128)(2,1)S(1)} collective-permute-done((bf16[256,1024]{1,0:T(8,128)(2,1)S(1)}, bf16[256,1024]{1,0:T(8,128)(2,1)S(1)}, u32[]{:S(2)}, u32[]{:S(2)}) %collective-permute-start.15) | collective-permute-done | bytes 524320 | tf_op jit(solution)/shard_map/ppermute | solution.py:550
  119.5 4.3 %collective-permute-start.16 = (bf16[256,1024]{1,0:T(8,128)(2,1)S(1)}, bf16[256,1024]{1,0:T(8,128)(2,1)S(1)}, u32[]{:S(2)}, u32[]{:S(2)}) collective-permute-start(bf16[256,1024]{1,0:T(8,128)(2,1)S(1)} %collective-permute-done.15.refs_7_), channel_id=1, source_target_pairs={{0,4},{4,8},{6,2},{8,12},{10,6},{12,16},{14,10},{16,20},{18,14},{2... | collective-permute-start | bytes 1572872 | tf_op jit(solution)/shard_map/ppermute | solution.py:556
  123.8 3.1 %bands.3.band_ref = bf16[16,128,2432]{2,1,0:T(8,128)(2,1)S(1)} custom-call(f32[8,2,2304]{2,1,0:T(2,128)S(1)} %reshape.23.row_ref), custom_call_target="tpu_custom_call" | custom-call | flops 4718592 | bytes 9437184 | tf_op jit(solution)/shard_map/bands/pallas_call | solution.py:84
  126.9 4.6 %norm.1 = (bf16[1024,1024]{1,0:T(8,128)(2,1)}, bf16[1024,1024]{1,0:T(8,128)(2,1)}) custom-call(f32[2,1024]{1,0:T(2,128)S(1)} %add.22.sums_ref, f32[1024,1024]{1,0:T(8,128)S(1)} %get-tuple-element.43.mixed_ref, f32[256,1024]{1,0:T(8,128)S(1)} %get-tuple-element.46.first_ref, bf16[1024,1024]{1,0:T(8,128)(2,1)S(1)} %copy-done, ...), custom_call_target="tpu_custom_call" | custom-call | flops 14680064 | bytes 12582912 | tf_op jit(solution)/shard_map/norm/pallas_call | solution.py:398
  135.1 3.3 %collective-permute-done.18.refs_10_ = bf16[256,1024]{1,0:T(8,128)(2,1)S(1)} collective-permute-done((bf16[256,1024]{1,0:T(8,128)(2,1)S(1)}, bf16[256,1024]{1,0:T(8,128)(2,1)S(1)}, u32[]{:S(2)}, u32[]{:S(2)}) %collective-permute-start.18) | collective-permute-done | bytes 524320 | tf_op jit(solution)/shard_map/ppermute | solution.py:556
  138.4 10.3 %value_grad.1 = (bf16[1024,1024]{1,0:T(8,128)(2,1)}, f32[256,1024]{1,0:T(8,128)S(1)}) custom-call(bf16[16,128,2432]{2,1,0:T(8,128)(2,1)S(1)} %bands.3.band_ref, bf16[256,1024]{1,0:T(8,128)(2,1)S(1)} %get-tuple-element.48.refs_8_.refs_0_, bf16[256,1024]{1,0:T(8,128)(2,1)S(1)} %get-tuple-element.47.refs_9_.refs_1_, ...), custom_call_target="tpu_custom_call" | custom-call | flops 4831838208 | bytes 12582912 | tf_op jit(solution)/shard_map/value_grad/pallas_call | solution.py:502
  (52 shorter events, 27.9 us)
Async XLA Ops:
  3.0 16.0 %collective-permute-start.2 = (bf16[256,1024]{1,0:T(8,128)(2,1)}, bf16[256,1024]{1,0:T(8,128)(2,1)S(1)}, u32[]{:S(2)}, u32[]{:S(2)}) collective-permute-start(bf16[256,1024]{1,0:T(8,128)(2,1)} %get-tuple-element.40), channel_id=1, source_target_pairs={{0,2},{2,0},{4,6},{6,4},{8,10},{10,8},{12,14},{14,12},{16,18},{18,... | collective-permute-start | bytes 1572872 | tf_op jit(solution)/shard_map/ppermute | solution.py:550
  6.0 24.2 %collective-permute-start.3 = (bf16[256,1024]{1,0:T(8,128)(2,1)S(1)}, bf16[256,1024]{1,0:T(8,128)(2,1)S(1)}, u32[]{:S(2)}, u32[]{:S(2)}) collective-permute-start(bf16[256,1024]{1,0:T(8,128)(2,1)S(1)} %get-tuple-element.41), channel_id=1, source_target_pairs={{0,2},{2,0},{4,6},{6,4},{8,10},{10,8},{12,14},{14,12},{16,18},{18,... | collective-permute-start | bytes 1572872 | tf_op jit(solution)/shard_map/ppermute | solution.py:550
  6.1 35.4 %collective-permute-start.4 = (bf16[256,1024]{1,0:T(8,128)(2,1)S(1)}, bf16[256,1024]{1,0:T(8,128)(2,1)S(1)}, u32[]{:S(2)}, u32[]{:S(2)}) collective-permute-start(bf16[256,1024]{1,0:T(8,128)(2,1)S(1)} %get-tuple-element.42), channel_id=1, source_target_pairs={{0,2},{2,0},{4,6},{6,4},{8,10},{10,8},{12,14},{14,12},{16,18},{18,... | collective-permute-start | bytes 1572872 | tf_op jit(solution)/shard_map/ppermute | solution.py:550
  11.1 44.5 %copy-start = (bf16[1024,1024]{1,0:T(8,128)(2,1)S(1)}, bf16[1024,1024]{1,0:T(8,128)(2,1)}, u32[]{:S(2)}) copy-start(bf16[1024,1024]{1,0:T(8,128)(2,1)} %gate_ref.7) | copy-start | bytes 6291460
  11.1 44.5 %copy-start.1 = (bf16[1024,1024]{1,0:T(8,128)(2,1)S(1)}, bf16[1024,1024]{1,0:T(8,128)(2,1)}, u32[]{:S(2)}) copy-start(bf16[1024,1024]{1,0:T(8,128)(2,1)} %grad_ref.7) | copy-start | bytes 6291460
  14.3 37.6 %collective-permute-start = (bf16[256,1024]{1,0:T(8,128)(2,1)S(1)}, bf16[256,1024]{1,0:T(8,128)(2,1)S(1)}, u32[]{:S(2)}, u32[]{:S(2)}) collective-permute-start(bf16[256,1024]{1,0:T(8,128)(2,1)S(1)} %get-tuple-element.39), channel_id=1, source_target_pairs={{0,2},{2,0},{4,6},{6,4},{8,10},{10,8},{12,14},{14,12},{16,18},{18,... | collective-permute-start | bytes 1572872 | tf_op jit(solution)/shard_map/ppermute | solution.py:550
  19.0 36.6 %collective-permute-start.5 = (bf16[256,1024]{1,0:T(8,128)(2,1)S(1)}, bf16[256,1024]{1,0:T(8,128)(2,1)S(1)}, u32[]{:S(2)}, u32[]{:S(2)}) collective-permute-start(bf16[256,1024]{1,0:T(8,128)(2,1)S(1)} %collective-permute-done.2.refs_0_), channel_id=1, source_target_pairs={{0,4},{4,8},{6,2},{8,12},{10,6},{12,16},{14,10},{16,20},{18,14},{2... | collective-permute-start | bytes 1572872 | tf_op jit(solution)/shard_map/ppermute | solution.py:556
  30.2 25.4 %collective-permute-start.6 = (bf16[256,1024]{1,0:T(8,128)(2,1)S(1)}, bf16[256,1024]{1,0:T(8,128)(2,1)S(1)}, u32[]{:S(2)}, u32[]{:S(2)}) collective-permute-start(bf16[256,1024]{1,0:T(8,128)(2,1)S(1)} %collective-permute-done.3.refs_1_), channel_id=1, source_target_pairs={{0,4},{4,8},{6,2},{8,12},{10,6},{12,16},{14,10},{16,20},{18,14},{2... | collective-permute-start | bytes 1572872 | tf_op jit(solution)/shard_map/ppermute | solution.py:556
  41.5 14.1 %collective-permute-start.7 = (bf16[256,1024]{1,0:T(8,128)(2,1)S(1)}, bf16[256,1024]{1,0:T(8,128)(2,1)S(1)}, u32[]{:S(2)}, u32[]{:S(2)}) collective-permute-start(bf16[256,1024]{1,0:T(8,128)(2,1)S(1)} %collective-permute-done.4.refs_2_), channel_id=1, source_target_pairs={{0,4},{4,8},{6,2},{8,12},{10,6},{12,16},{14,10},{16,20},{18,14},{2... | collective-permute-start | bytes 1572872 | tf_op jit(solution)/shard_map/ppermute | solution.py:556
  51.9 14.7 %collective-permute-start.1 = (bf16[256,1024]{1,0:T(8,128)(2,1)S(1)}, bf16[256,1024]{1,0:T(8,128)(2,1)S(1)}, u32[]{:S(2)}, u32[]{:S(2)}) collective-permute-start(bf16[256,1024]{1,0:T(8,128)(2,1)S(1)} %collective-permute-done.refs_3_), channel_id=1, source_target_pairs={{0,4},{4,8},{6,2},{8,12},{10,6},{12,16},{14,10},{16,20},{18,14},{2... | collective-permute-start | bytes 1572872 | tf_op jit(solution)/shard_map/ppermute | solution.py:556
  68.7 1.2 collective-permute-start.8
  71.8 16.6 %collective-permute-start.10 = (bf16[256,1024]{1,0:T(8,128)(2,1)S(1)}, bf16[256,1024]{1,0:T(8,128)(2,1)S(1)}, u32[]{:S(2)}, u32[]{:S(2)}) collective-permute-start(bf16[256,1024]{1,0:T(8,128)(2,1)S(1)} %get-tuple-element.48.refs_8_.refs_0_), channel_id=1, source_target_pairs={{0,2},{2,0},{4,6},{6,4},{8,10},{10,8},{12,14},{14,12},{16,18},{18,... | collective-permute-start | bytes 1572872 | tf_op jit(solution)/shard_map/ppermute | solution.py:550
  73.5 28.0 %collective-permute-start.9 = (bf16[256,1024]{1,0:T(8,128)(2,1)S(1)}, bf16[256,1024]{1,0:T(8,128)(2,1)S(1)}, u32[]{:S(2)}, u32[]{:S(2)}) collective-permute-start(bf16[256,1024]{1,0:T(8,128)(2,1)S(1)} %get-tuple-element.47.refs_9_.refs_1_), channel_id=1, source_target_pairs={{0,2},{2,0},{4,6},{6,4},{8,10},{10,8},{12,14},{14,12},{16,18},{18,... | collective-permute-start | bytes 1572872 | tf_op jit(solution)/shard_map/ppermute | solution.py:550
  73.8 35.2 %collective-permute-start.17 = (bf16[256,1024]{1,0:T(8,128)(2,1)S(1)}, bf16[256,1024]{1,0:T(8,128)(2,1)S(1)}, u32[]{:S(2)}, u32[]{:S(2)}) collective-permute-start(bf16[256,1024]{1,0:T(8,128)(2,1)S(1)} %get-tuple-element.50.refs_10_.refs_2_), channel_id=1, source_target_pairs={{0,2},{2,0},{4,6},{6,4},{8,10},{10,8},{12,14},{14,12},{16,18},{18,... | collective-permute-start | bytes 1572872 | tf_op jit(solution)/shard_map/ppermute | solution.py:550
  88.4 5.1 %collective-permute-start.11 = (f32[16,2176]{1,0:T(8,128)S(1)}, f32[16,2176]{1,0:T(8,128)S(1)}, u32[]{:S(2)}, u32[]{:S(2)}) collective-permute-start(f32[16,2176]{1,0:T(8,128)S(1)} %kernel_grad.1), channel_id=1, source_target_pairs={{0,8},{2,10},{4,12},{6,14},{8,0},{10,2},{12,4},{14,6},{16,24},{18,... | collective-permute-start | bytes 417800 | tf_op jit(solution)/shard_map/ppermute | solution.py:564
  93.5 8.0 %collective-permute-start.12 = (f32[16,2176]{1,0:T(8,128)S(1)}, f32[16,2176]{1,0:T(8,128)S(1)}, u32[]{:S(2)}, u32[]{:S(2)}) collective-permute-start(f32[16,2176]{1,0:T(8,128)S(1)} %add.23), channel_id=1, source_target_pairs={{0,16},{2,18},{4,20},{6,22},{8,24},{10,26},{12,28},{14,30},{16,0},... | collective-permute-start | bytes 417800 | tf_op jit(solution)/shard_map/ppermute | solution.py:564
  96.2 23.3 %collective-permute-start.15 = (bf16[256,1024]{1,0:T(8,128)(2,1)S(1)}, bf16[256,1024]{1,0:T(8,128)(2,1)S(1)}, u32[]{:S(2)}, u32[]{:S(2)}) collective-permute-start(bf16[256,1024]{1,0:T(8,128)(2,1)S(1)} %get-tuple-element.51.refs_11_.refs_3_), channel_id=1, source_target_pairs={{0,2},{2,0},{4,6},{6,4},{8,10},{10,8},{12,14},{14,12},{16,18},{18,... | collective-permute-start | bytes 1572872 | tf_op jit(solution)/shard_map/ppermute | solution.py:550
  97.6 33.9 %collective-permute-start.13 = (bf16[256,1024]{1,0:T(8,128)(2,1)S(1)}, bf16[256,1024]{1,0:T(8,128)(2,1)S(1)}, u32[]{:S(2)}, u32[]{:S(2)}) collective-permute-start(bf16[256,1024]{1,0:T(8,128)(2,1)S(1)} %collective-permute-done.10.refs_4_), channel_id=1, source_target_pairs={{0,4},{4,8},{6,2},{8,12},{10,6},{12,16},{14,10},{16,20},{18,14},{2... | collective-permute-start | bytes 1572872 | tf_op jit(solution)/shard_map/ppermute | solution.py:556
  101.5 30.0 %collective-permute-start.14 = (bf16[256,1024]{1,0:T(8,128)(2,1)S(1)}, bf16[256,1024]{1,0:T(8,128)(2,1)S(1)}, u32[]{:S(2)}, u32[]{:S(2)}) collective-permute-start(bf16[256,1024]{1,0:T(8,128)(2,1)S(1)} %collective-permute-done.9.refs_5_), channel_id=1, source_target_pairs={{0,4},{4,8},{6,2},{8,12},{10,6},{12,16},{14,10},{16,20},{18,14},{2... | collective-permute-start | bytes 1572872 | tf_op jit(solution)/shard_map/ppermute | solution.py:556
  109.1 29.3 %collective-permute-start.18 = (bf16[256,1024]{1,0:T(8,128)(2,1)S(1)}, bf16[256,1024]{1,0:T(8,128)(2,1)S(1)}, u32[]{:S(2)}, u32[]{:S(2)}) collective-permute-start(bf16[256,1024]{1,0:T(8,128)(2,1)S(1)} %collective-permute-done.17.refs_6_), channel_id=1, source_target_pairs={{0,4},{4,8},{6,2},{8,12},{10,6},{12,16},{14,10},{16,20},{18,14},{2... | collective-permute-start | bytes 1572872 | tf_op jit(solution)/shard_map/ppermute | solution.py:556
  119.5 29.1 %collective-permute-start.16 = (bf16[256,1024]{1,0:T(8,128)(2,1)S(1)}, bf16[256,1024]{1,0:T(8,128)(2,1)S(1)}, u32[]{:S(2)}, u32[]{:S(2)}) collective-permute-start(bf16[256,1024]{1,0:T(8,128)(2,1)S(1)} %collective-permute-done.15.refs_7_), channel_id=1, source_target_pairs={{0,4},{4,8},{6,2},{8,12},{10,6},{12,16},{14,10},{16,20},{18,14},{2... | collective-permute-start | bytes 1572872 | tf_op jit(solution)/shard_map/ppermute | solution.py:556
  131.5 19.7 %collective-permute-start.21 = (f32[16,2176]{1,0:T(8,128)S(1)}, f32[16,2176]{1,0:T(8,128)S(1)}, u32[]{:S(2)}, u32[]{:S(2)}) collective-permute-start(f32[16,2176]{1,0:T(8,128)S(1)} %add.24), channel_id=1, source_target_pairs={{0,6},{2,4},{4,2},{6,0},{8,14},{10,12},{12,10},{14,8},{16,22},{18,... | collective-permute-start | bytes 417800 | tf_op jit(solution)/shard_map/ppermute | solution.py:564
  132.7 18.5 %collective-permute-start.20 = (f32[16,2176]{1,0:T(8,128)S(1)}, f32[16,2176]{1,0:T(8,128)S(1)}, u32[]{:S(2)}, u32[]{:S(2)}) collective-permute-start(f32[16,2176]{1,0:T(8,128)S(1)} %add.24), channel_id=1, source_target_pairs={{0,4},{2,6},{4,0},{6,2},{8,12},{10,14},{12,8},{14,10},{16,20},{18,... | collective-permute-start | bytes 417800 | tf_op jit(solution)/shard_map/ppermute | solution.py:564
  133.4 17.9 %collective-permute-start.19 = (f32[16,2176]{1,0:T(8,128)S(1)}, f32[16,2176]{1,0:T(8,128)S(1)}, u32[]{:S(2)}, u32[]{:S(2)}) collective-permute-start(f32[16,2176]{1,0:T(8,128)S(1)} %add.24), channel_id=1, source_target_pairs={{0,2},{2,0},{4,6},{6,4},{8,10},{10,8},{12,14},{14,12},{16,18},{18,... | collective-permute-start | bytes 417800 | tf_op jit(solution)/shard_map/ppermute | solution.py:564
  (3 other events, 96.4 us)
where the time goes:
time: 154 us; the launch traced here: 153 us
  Pallas kernels  53.7 us (35%)
  starting transfers between devices  49.7 us (32%)
  waiting for transfers between devices  43.8 us (28%)
  local copies, waits for them, and re-layouts  3.71 us (2%)
    ppermute x8, waiting for transfers between devices, swapped(): return lax.ppermute(chunk, 'seq', [(i, i ^ 1) for i in range(count)])  35.1 us
    ppermute x8, starting transfers between devices, relayed(): lax.ppermute(chunk, 'seq', [(i, j) for i, j in pairs if 0 <= j < count])  31.4 us
    pallas_call x1, Pallas kernels, kernel_grad_local(): pl.pallas_call(functools.partial(kernel_grad_body, slots), grid=(pairs,),...  12.8 us
    pallas_call x1, Pallas kernels, forward(): pl.pallas_call(functools.partial(forward_body, slots), grid=(width // LAN...  10.9 us
    ppermute x8, starting transfers between devices, swapped(): return lax.ppermute(chunk, 'seq', [(i, i ^ 1) for i in range(count)])  10.3 us
    pallas_call x1, Pallas kernels, value_grad_of(): pl.pallas_call(functools.partial(value_grad_body, slots), grid=(width //...  10.3 us
    ppermute x5, starting transfers between devices, sum_over_bits(): total += lax.ppermute(value, 'seq', [(i, i ^ flip) for i in range(count)])  7.86 us
    pallas_call x2, Pallas kernels, bands(): pl.pallas_call(band_body, grid=(heads // 2,), in_specs=[VMEM], out_specs=...  6.21 us
  transfers between devices with their start and end apart: 22, of which 10 were waited for; matrix products, arithmetic and copies ran while one was open for 2% of the time, Pallas kernels for 31%

commit v1 on v0

--- a/solution.py
+++ b/solution.py
@@ -556,13 +556,13 @@
     return lax.ppermute(chunk, "seq", [(i, j) for i, j in pairs if 0 <= j < count])
 
 
-def sum_over_bits(value, bits):
+def terms_over_bits(value, bits):
     count = lax.axis_size("seq")
-    total = value
+    terms = []
     for mask in range(1, 1 << len(bits)):
         flip = sum(1 << bit for at, bit in enumerate(bits) if mask >> at & 1)
-        total += lax.ppermute(value, "seq", [(i, i ^ flip) for i in range(count)])
-    return total
+        terms.append(lax.ppermute(value, "seq", [(i, i ^ flip) for i in range(count)]))
+    return terms
 
 
 def sum_over(value, axis):
@@ -598,21 +598,26 @@
     args = (mixed, first, gate_acts, out_grad, gain)
     mix_grad, gain_sums = mix_grad_of(full_width, sums, *args)
 
-    grad_near = [swapped(chunk) for chunk in mix_grad]
+    grad_near = [swapped(part) for part in mix_grad]
     totals = kernel_grad_local(gain_sums, value_acts, near, far, mix_grad, lag)
+    normed, gate_grad = norm(full_width, after(sums, grad_near[0]), *args)
+    back_band = bands(after(behind, grad_near[1]))
+    grad_near[0], totals = lax.optimization_barrier((grad_near[0], totals))
+    grad_near[3], normed, gate_grad, back_band = lax.optimization_barrier(
+        (grad_near[3], normed, gate_grad, back_band)
+    )
     bits = list(range(count.bit_length() - 1))
-    grad_near[0], totals = lax.optimization_barrier((grad_near[0], totals))
-    back_band = bands(after(behind, grad_near[0]))
-    normed, gate_grad = norm(full_width, after(sums, grad_near[1]), *args)
     for bit in bits[2:]:
-        totals = sum_over_bits(totals, [bit])
-    grad_near[1], totals = lax.optimization_barrier((grad_near[1], totals))
+        totals += terms_over_bits(totals, [bit])[0]
+        if bit == 2:
+            grad_near[1], totals = lax.optimization_barrier((grad_near[1], totals))
     grad_far = [relayed(chunk) for chunk in grad_near]
     totals, *grad_far[:2] = lax.optimization_barrier((totals, *grad_far[:2]))
-    totals = sum_over_bits(totals, bits[:2])
-    grad_far[0], normed, gate_grad = lax.optimization_barrier((grad_far[0], normed, gate_grad))
+    terms = [totals] + terms_over_bits(totals, bits[:2])
     value_grad, first = value_grad_of(back_band, mix_grad, grad_near, grad_far[:-1], lag)
     value_grad = value_grad_last(back_band, grad_far[-1], first, value_grad)
+    value_grad, *terms = lax.optimization_barrier((value_grad, *terms))
+    totals = sum(terms[1:], terms[0])
     tokens = rows * count
     kernel_grad = totals[:, : 2 * lag] / math.sqrt(tokens * HEAD)
     gain_grad = totals[:, 2 * lag : 2 * lag + HEAD].reshape(width) / math.sqrt(tokens)

time: 154 us -> 155 us (level)
  starting transfers between devices: 49.7 us -> 58.5 us
  waiting for transfers between devices: 43.8 us -> 37.2 us
    ppermute x5, starting transfers between devices: 7.86 us -> 17.4 us  [terms_over_bits(): lax.ppermute(value, 'seq', [(i, i ^ flip) for i in range(count)])]
    ppermute x5, waiting for transfers between devices: 4.29 us -> 0.01 us  [terms_over_bits(): lax.ppermute(value, 'seq', [(i, i ^ flip) for i in range(count)])]
    ppermute x8, waiting for transfers between devices: 3.31 us -> 0.02 us  [relayed(): lax.ppermute(chunk, 'seq', [(i, j) for i, j in pairs if 0 <= j < count])]
  transfers between devices with their start and end apart: 22 -> 22, of which waited for: 10 -> 7; matrix products, arithmetic and copies ran while one was open for 2% -> 2% of each run, Pallas kernels for 31% -> 31%
where the time goes in v1:
time: 155 us
  starting transfers between devices  58.5 us (38%)
  Pallas kernels  53.7 us (35%)
  waiting for transfers between devices  37.2 us (24%)
  local copies, waits for them, and re-layouts  3.71 us (2%)
    ppermute x8, waiting for transfers between devices, swapped(): return lax.ppermute(chunk, 'seq', [(i, i ^ 1) for i in range(count)])  36 us
    ppermute x8, starting transfers between devices, relayed(): lax.ppermute(chunk, 'seq', [(i, j) for i, j in pairs if 0 <= j < count])  30.6 us
    ppermute x5, starting transfers between devices, terms_over_bits(): lax.ppermute(value, 'seq', [(i, i ^ flip) for i in range(count)])  17.4 us
    pallas_call x1, Pallas kernels, kernel_grad_local(): pl.pallas_call(functools.partial(kernel_grad_body, slots), grid=(pairs,),...  12.8 us
    pallas_call x1, Pallas kernels, forward(): pl.pallas_call(functools.partial(forward_body, slots), grid=(width // LAN...  10.9 us
    ppermute x8, starting transfers between devices, swapped(): return lax.ppermute(chunk, 'seq', [(i, i ^ 1) for i in range(count)])  10.4 us
    pallas_call x1, Pallas kernels, value_grad_of(): pl.pallas_call(functools.partial(value_grad_body, slots), grid=(width //...  10.3 us
    pallas_call x2, Pallas kernels, bands(): pl.pallas_call(band_body, grid=(heads // 2,), in_specs=[VMEM], out_specs=...  6.2 us
  transfers between devices with their start and end apart: 22, of which 7 were waited for; matrix products, arithmetic and copies ran while one was open for 2% of the time, Pallas kernels for 31%

profile of v1, /device:TPU:0, one launch (start us, length us, event | category | flops | bytes accessed | tf_op | source)
XLA Modules:
  0.0 154.9 jit_solution(12484314593065662063)
XLA Ops:
  3.0 3.0 %collective-permute-start.2 = (bf16[256,1024]{1,0:T(8,128)(2,1)}, bf16[256,1024]{1,0:T(8,128)(2,1)S(1)}, u32[]{:S(2)}, u32[]{:S(2)}) collective-permute-start(bf16[256,1024]{1,0:T(8,128)(2,1)} %get-tuple-element.46), channel_id=1, source_target_pairs={{0,2},{2,0},{4,6},{6,4},{8,10},{10,8},{12,14},{14,12},{16,18},{18,... | collective-permute-start | bytes 1572872 | tf_op jit(solution)/shard_map/ppermute | solution.py:550
  11.2 3.1 %bands.2.band_ref = bf16[16,128,2432]{2,1,0:T(8,128)(2,1)S(1)} custom-call(f32[8,2,2304]{2,1,0:T(2,128)S(1)} %reshape.22.row_ref), custom_call_target="tpu_custom_call" | custom-call | flops 4718592 | bytes 9437184 | tf_op jit(solution)/shard_map/bands/pallas_call | solution.py:84
  14.4 4.6 %collective-permute-done.2.refs_0_ = bf16[256,1024]{1,0:T(8,128)(2,1)S(1)} collective-permute-done((bf16[256,1024]{1,0:T(8,128)(2,1)}, bf16[256,1024]{1,0:T(8,128)(2,1)S(1)}, u32[]{:S(2)}, u32[]{:S(2)}) %collective-permute-start.2) | collective-permute-done | bytes 524320 | tf_op jit(solution)/shard_map/ppermute | solution.py:550
  19.0 4.0 %collective-permute-start.5 = (bf16[256,1024]{1,0:T(8,128)(2,1)S(1)}, bf16[256,1024]{1,0:T(8,128)(2,1)S(1)}, u32[]{:S(2)}, u32[]{:S(2)}) collective-permute-start(bf16[256,1024]{1,0:T(8,128)(2,1)S(1)} %collective-permute-done.2.refs_0_), channel_id=1, source_target_pairs={{0,4},{4,8},{6,2},{8,12},{10,6},{12,16},{14,10},{16,20},{18,14},{2... | collective-permute-start | bytes 1572872 | tf_op jit(solution)/shard_map/ppermute | solution.py:556
  23.0 7.2 %collective-permute-done.3.refs_1_ = bf16[256,1024]{1,0:T(8,128)(2,1)S(1)} collective-permute-done((bf16[256,1024]{1,0:T(8,128)(2,1)S(1)}, bf16[256,1024]{1,0:T(8,128)(2,1)S(1)}, u32[]{:S(2)}, u32[]{:S(2)}) %collective-permute-start.3) | collective-permute-done | bytes 524320 | tf_op jit(solution)/shard_map/ppermute | solution.py:550
  30.2 4.0 %collective-permute-start.6 = (bf16[256,1024]{1,0:T(8,128)(2,1)S(1)}, bf16[256,1024]{1,0:T(8,128)(2,1)S(1)}, u32[]{:S(2)}, u32[]{:S(2)}) collective-permute-start(bf16[256,1024]{1,0:T(8,128)(2,1)S(1)} %collective-permute-done.3.refs_1_), channel_id=1, source_target_pairs={{0,4},{4,8},{6,2},{8,12},{10,6},{12,16},{14,10},{16,20},{18,14},{2... | collective-permute-start | bytes 1572872 | tf_op jit(solution)/shard_map/ppermute | solution.py:556
  34.3 7.2 %collective-permute-done.4.refs_2_ = bf16[256,1024]{1,0:T(8,128)(2,1)S(1)} collective-permute-done((bf16[256,1024]{1,0:T(8,128)(2,1)S(1)}, bf16[256,1024]{1,0:T(8,128)(2,1)S(1)}, u32[]{:S(2)}, u32[]{:S(2)}) %collective-permute-start.4) | collective-permute-done | bytes 524320 | tf_op jit(solution)/shard_map/ppermute | solution.py:550
  41.5 4.0 %collective-permute-start.7 = (bf16[256,1024]{1,0:T(8,128)(2,1)S(1)}, bf16[256,1024]{1,0:T(8,128)(2,1)S(1)}, u32[]{:S(2)}, u32[]{:S(2)}) collective-permute-start(bf16[256,1024]{1,0:T(8,128)(2,1)S(1)} %collective-permute-done.4.refs_2_), channel_id=1, source_target_pairs={{0,4},{4,8},{6,2},{8,12},{10,6},{12,16},{14,10},{16,20},{18,14},{2... | collective-permute-start | bytes 1572872 | tf_op jit(solution)/shard_map/ppermute | solution.py:556
  45.5 6.4 %collective-permute-done.refs_3_ = bf16[256,1024]{1,0:T(8,128)(2,1)S(1)} collective-permute-done((bf16[256,1024]{1,0:T(8,128)(2,1)S(1)}, bf16[256,1024]{1,0:T(8,128)(2,1)S(1)}, u32[]{:S(2)}, u32[]{:S(2)}) %collective-permute-start) | collective-permute-done | bytes 524320 | tf_op jit(solution)/shard_map/ppermute | solution.py:550
  51.9 3.7 %collective-permute-start.1 = (bf16[256,1024]{1,0:T(8,128)(2,1)S(1)}, bf16[256,1024]{1,0:T(8,128)(2,1)S(1)}, u32[]{:S(2)}, u32[]{:S(2)}) collective-permute-start(bf16[256,1024]{1,0:T(8,128)(2,1)S(1)} %collective-permute-done.refs_3_), channel_id=1, source_target_pairs={{0,4},{4,8},{6,2},{8,12},{10,6},{12,16},{14,10},{16,20},{18,14},{2... | collective-permute-start | bytes 1572872 | tf_op jit(solution)/shard_map/ppermute | solution.py:556
  55.7 10.9 %forward.1 = (f32[1024,1024]{1,0:T(8,128)S(1)}, f32[2,1024]{1,0:T(2,128)S(1)}) custom-call(bf16[16,128,2432]{2,1,0:T(8,128)(2,1)S(1)} %bands.2.band_ref, bf16[1024,1024]{1,0:T(8,128)(2,1)S(1)} %copy-done.2, bf16[1024,1024]{1,0:T(8,128)(2,1)S(1)} %copy-done, bf16[1024,1024]{1,0:T(8,128)(2,1)S(1)} %copy-done.1, f32[1,1024]{1,0:T(1,128)S(1)} %bitcast.1, ...), custom_call_target="tpu_custom_call" | custom-call | flops 4831838208 | bytes 16777216 | tf_op jit(solution)/shard_map/forward/pallas_call | solution.py:263
  75.5 12.8 %kernel_grad.1 = f32[16,2176]{1,0:T(8,128)S(1)} custom-call(f32[1,1024]{1,0:T(1,128)S(1)} %get-tuple-element.66.gain_ref, bf16[1024,1024]{1,0:T(8,128)(2,1)S(1)} %copy-done.2, bf16[256,1024]{1,0:T(8,128)(2,1)S(1)} %collective-permute-done.2.refs_0_, bf16[256,1024]{1,0:T(8,128)(2,1)S(1)} %collective-permute-done.3.refs_1_, ...), custom_call_target="tpu_custom_call" | custom-call | flops 4831838208 | bytes 8388608 | tf_op jit(solution)/shard_map/kernel_grad/pallas_call | solution.py:463
  91.4 3.0 %collective-permute-start.16 = (bf16[256,1024]{1,0:T(8,128)(2,1)S(1)}, bf16[256,1024]{1,0:T(8,128)(2,1)S(1)}, u32[]{:S(2)}, u32[]{:S(2)}) collective-permute-start(bf16[256,1024]{1,0:T(8,128)(2,1)S(1)} %collective-permute-done.10.refs_4_), channel_id=1, source_target_pairs={{0,4},{4,8},{6,2},{8,12},{10,6},{12,16},{14,10},{16,20},{18,14},{2... | collective-permute-start | bytes 1572872 | tf_op jit(solution)/shard_map/ppermute | solution.py:556
  94.5 3.4 %collective-permute-done.11.refs_5_ = bf16[256,1024]{1,0:T(8,128)(2,1)S(1)} collective-permute-done((bf16[256,1024]{1,0:T(8,128)(2,1)S(1)}, bf16[256,1024]{1,0:T(8,128)(2,1)S(1)}, u32[]{:S(2)}, u32[]{:S(2)}) %collective-permute-start.11) | collective-permute-done | bytes 524320 | tf_op jit(solution)/shard_map/ppermute | solution.py:550
  97.8 4.0 %collective-permute-start.17 = (bf16[256,1024]{1,0:T(8,128)(2,1)S(1)}, bf16[256,1024]{1,0:T(8,128)(2,1)S(1)}, u32[]{:S(2)}, u32[]{:S(2)}) collective-permute-start(bf16[256,1024]{1,0:T(8,128)(2,1)S(1)} %collective-permute-done.11.refs_5_), channel_id=1, source_target_pairs={{0,4},{4,8},{6,2},{8,12},{10,6},{12,16},{14,10},{16,20},{18,14},{2... | collective-permute-start | bytes 1572872 | tf_op jit(solution)/shard_map/ppermute | solution.py:556
  101.8 7.3 %collective-permute-done.14.refs_6_ = bf16[256,1024]{1,0:T(8,128)(2,1)S(1)} collective-permute-done((bf16[256,1024]{1,0:T(8,128)(2,1)S(1)}, bf16[256,1024]{1,0:T(8,128)(2,1)S(1)}, u32[]{:S(2)}, u32[]{:S(2)}) %collective-permute-start.14) | collective-permute-done | bytes 524320 | tf_op jit(solution)/shard_map/ppermute | solution.py:550
  109.1 4.0 %collective-permute-start.18 = (bf16[256,1024]{1,0:T(8,128)(2,1)S(1)}, bf16[256,1024]{1,0:T(8,128)(2,1)S(1)}, u32[]{:S(2)}, u32[]{:S(2)}) collective-permute-start(bf16[256,1024]{1,0:T(8,128)(2,1)S(1)} %collective-permute-done.14.refs_6_), channel_id=1, source_target_pairs={{0,4},{4,8},{6,2},{8,12},{10,6},{12,16},{14,10},{16,20},{18,14},{2... | collective-permute-start | bytes 1572872 | tf_op jit(solution)/shard_map/ppermute | solution.py:556
  113.0 2.6 %collective-permute-start.15 = (f32[16,2176]{1,0:T(8,128)S(1)}, f32[16,2176]{1,0:T(8,128)S(1)}, u32[]{:S(2)}, u32[]{:S(2)}) collective-permute-start(f32[16,2176]{1,0:T(8,128)S(1)} %add.23), channel_id=1, source_target_pairs={{0,16},{2,18},{4,20},{6,22},{8,24},{10,26},{12,28},{14,30},{16,0},... | collective-permute-start | bytes 417800 | tf_op jit(solution)/shard_map/ppermute | solution.py:564
  115.7 3.1 %bands.3.band_ref = bf16[16,128,2432]{2,1,0:T(8,128)(2,1)S(1)} custom-call(f32[8,2,2304]{2,1,0:T(2,128)S(1)} %reshape.23.row_ref), custom_call_target="tpu_custom_call" | custom-call | flops 4718592 | bytes 9437184 | tf_op jit(solution)/shard_map/bands/pallas_call | solution.py:84
  118.8 4.6 %norm.1 = (bf16[1024,1024]{1,0:T(8,128)(2,1)}, bf16[1024,1024]{1,0:T(8,128)(2,1)}) custom-call(f32[2,1024]{1,0:T(2,128)S(1)} %add.22.sums_ref, f32[1024,1024]{1,0:T(8,128)S(1)} %get-tuple-element.49.mixed_ref, f32[256,1024]{1,0:T(8,128)S(1)} %get-tuple-element.52.first_ref, bf16[1024,1024]{1,0:T(8,128)(2,1)S(1)} %copy-done, ...), custom_call_target="tpu_custom_call" | custom-call | flops 14680064 | bytes 12582912 | tf_op jit(solution)/shard_map/norm/pallas_call | solution.py:398
  123.3 4.0 %collective-permute-start.12 = (bf16[256,1024]{1,0:T(8,128)(2,1)S(1)}, bf16[256,1024]{1,0:T(8,128)(2,1)S(1)}, u32[]{:S(2)}, u32[]{:S(2)}) collective-permute-start(bf16[256,1024]{1,0:T(8,128)(2,1)S(1)} %collective-permute-done.9.refs_7_), channel_id=1, source_target_pairs={{0,4},{4,8},{6,2},{8,12},{10,6},{12,16},{14,10},{16,20},{18,14},{2... | collective-permute-start | bytes 1572872 | tf_op jit(solution)/shard_map/ppermute | solution.py:556
  128.8 11.8 %collective-permute-start.20 = (f32[16,2176]{1,0:T(8,128)S(1)}, f32[16,2176]{1,0:T(8,128)S(1)}, u32[]{:S(2)}, u32[]{:S(2)}) collective-permute-start(f32[16,2176]{1,0:T(8,128)S(1)} %add.24), channel_id=1, source_target_pairs={{0,4},{2,6},{4,0},{6,2},{8,12},{10,14},{12,8},{14,10},{16,20},{18,... | collective-permute-start | bytes 417800 | tf_op jit(solution)/shard_map/ppermute | solution.py:564
  140.6 10.3 %value_grad.1 = (bf16[1024,1024]{1,0:T(8,128)(2,1)}, f32[256,1024]{1,0:T(8,128)S(1)}) custom-call(bf16[16,128,2432]{2,1,0:T(8,128)(2,1)S(1)} %bands.3.band_ref, bf16[256,1024]{1,0:T(8,128)(2,1)S(1)} %get-tuple-element.54.refs_8_.refs_0_, bf16[256,1024]{1,0:T(8,128)(2,1)S(1)} %get-tuple-element.59.refs_9_.refs_1_, ...), custom_call_target="tpu_custom_call" | custom-call | flops 4831838208 | bytes 12582912 | tf_op jit(solution)/shard_map/value_grad/pallas_call | solution.py:502
  150.9 2.6 %value_grad_last.1 = bf16[1024,1024]{1,0:T(8,128)(2,1)} custom-call(bf16[16,128,2432]{2,1,0:T(8,128)(2,1)S(1)} %bands.3.band_ref, bf16[256,1024]{1,0:T(8,128)(2,1)S(1)} %collective-permute-done.12.last_ref, f32[256,1024]{1,0:T(8,128)S(1)} %get-tuple-element.73.first_ref, bf16[1024,1024]{1,0:T(8,128)(2,1)} %get-tuple-element.74.rest_ref), custom_call_target="tpu_custom_call", output_to_operand_aliasing={{}: (3, {})} | custom-call | flops 536870912 | bytes 1572864 | tf_op jit(solution)/shard_map/value_grad_last/pallas_call | solution.py:534
  (52 shorter events, 22.4 us)
Async XLA Ops:
  3.0 16.0 %collective-permute-start.2 = (bf16[256,1024]{1,0:T(8,128)(2,1)}, bf16[256,1024]{1,0:T(8,128)(2,1)S(1)}, u32[]{:S(2)}, u32[]{:S(2)}) collective-permute-start(bf16[256,1024]{1,0:T(8,128)(2,1)} %get-tuple-element.46), channel_id=1, source_target_pairs={{0,2},{2,0},{4,6},{6,4},{8,10},{10,8},{12,14},{14,12},{16,18},{18,... | collective-permute-start | bytes 1572872 | tf_op jit(solution)/shard_map/ppermute | solution.py:550
  6.0 24.2 %collective-permute-start.3 = (bf16[256,1024]{1,0:T(8,128)(2,1)S(1)}, bf16[256,1024]{1,0:T(8,128)(2,1)S(1)}, u32[]{:S(2)}, u32[]{:S(2)}) collective-permute-start(bf16[256,1024]{1,0:T(8,128)(2,1)S(1)} %get-tuple-element.47), channel_id=1, source_target_pairs={{0,2},{2,0},{4,6},{6,4},{8,10},{10,8},{12,14},{14,12},{16,18},{18,... | collective-permute-start | bytes 1572872 | tf_op jit(solution)/shard_map/ppermute | solution.py:550
  6.1 35.4 %collective-permute-start.4 = (bf16[256,1024]{1,0:T(8,128)(2,1)S(1)}, bf16[256,1024]{1,0:T(8,128)(2,1)S(1)}, u32[]{:S(2)}, u32[]{:S(2)}) collective-permute-start(bf16[256,1024]{1,0:T(8,128)(2,1)S(1)} %get-tuple-element.48), channel_id=1, source_target_pairs={{0,2},{2,0},{4,6},{6,4},{8,10},{10,8},{12,14},{14,12},{16,18},{18,... | collective-permute-start | bytes 1572872 | tf_op jit(solution)/shard_map/ppermute | solution.py:550
  11.1 44.5 %copy-start = (bf16[1024,1024]{1,0:T(8,128)(2,1)S(1)}, bf16[1024,1024]{1,0:T(8,128)(2,1)}, u32[]{:S(2)}) copy-start(bf16[1024,1024]{1,0:T(8,128)(2,1)} %gate_ref.7) | copy-start | bytes 6291460
  11.1 44.5 %copy-start.1 = (bf16[1024,1024]{1,0:T(8,128)(2,1)S(1)}, bf16[1024,1024]{1,0:T(8,128)(2,1)}, u32[]{:S(2)}) copy-start(bf16[1024,1024]{1,0:T(8,128)(2,1)} %grad_ref.7) | copy-start | bytes 6291460
  14.3 37.6 %collective-permute-start = (bf16[256,1024]{1,0:T(8,128)(2,1)S(1)}, bf16[256,1024]{1,0:T(8,128)(2,1)S(1)}, u32[]{:S(2)}, u32[]{:S(2)}) collective-permute-start(bf16[256,1024]{1,0:T(8,128)(2,1)S(1)} %get-tuple-element.45), channel_id=1, source_target_pairs={{0,2},{2,0},{4,6},{6,4},{8,10},{10,8},{12,14},{14,12},{16,18},{18,... | collective-permute-start | bytes 1572872 | tf_op jit(solution)/shard_map/ppermute | solution.py:550
  19.0 36.6 %collective-permute-start.5 = (bf16[256,1024]{1,0:T(8,128)(2,1)S(1)}, bf16[256,1024]{1,0:T(8,128)(2,1)S(1)}, u32[]{:S(2)}, u32[]{:S(2)}) collective-permute-start(bf16[256,1024]{1,0:T(8,128)(2,1)S(1)} %collective-permute-done.2.refs_0_), channel_id=1, source_target_pairs={{0,4},{4,8},{6,2},{8,12},{10,6},{12,16},{14,10},{16,20},{18,14},{2... | collective-permute-start | bytes 1572872 | tf_op jit(solution)/shard_map/ppermute | solution.py:556
  30.2 25.4 %collective-permute-start.6 = (bf16[256,1024]{1,0:T(8,128)(2,1)S(1)}, bf16[256,1024]{1,0:T(8,128)(2,1)S(1)}, u32[]{:S(2)}, u32[]{:S(2)}) collective-permute-start(bf16[256,1024]{1,0:T(8,128)(2,1)S(1)} %collective-permute-done.3.refs_1_), channel_id=1, source_target_pairs={{0,4},{4,8},{6,2},{8,12},{10,6},{12,16},{14,10},{16,20},{18,14},{2... | collective-permute-start | bytes 1572872 | tf_op jit(solution)/shard_map/ppermute | solution.py:556
  41.5 14.1 %collective-permute-start.7 = (bf16[256,1024]{1,0:T(8,128)(2,1)S(1)}, bf16[256,1024]{1,0:T(8,128)(2,1)S(1)}, u32[]{:S(2)}, u32[]{:S(2)}) collective-permute-start(bf16[256,1024]{1,0:T(8,128)(2,1)S(1)} %collective-permute-done.4.refs_2_), channel_id=1, source_target_pairs={{0,4},{4,8},{6,2},{8,12},{10,6},{12,16},{14,10},{16,20},{18,14},{2... | collective-permute-start | bytes 1572872 | tf_op jit(solution)/shard_map/ppermute | solution.py:556
  51.9 14.7 %collective-permute-start.1 = (bf16[256,1024]{1,0:T(8,128)(2,1)S(1)}, bf16[256,1024]{1,0:T(8,128)(2,1)S(1)}, u32[]{:S(2)}, u32[]{:S(2)}) collective-permute-start(bf16[256,1024]{1,0:T(8,128)(2,1)S(1)} %collective-permute-done.refs_3_), channel_id=1, source_target_pairs={{0,4},{4,8},{6,2},{8,12},{10,6},{12,16},{14,10},{16,20},{18,14},{2... | collective-permute-start | bytes 1572872 | tf_op jit(solution)/shard_map/ppermute | solution.py:556
  68.7 1.2 collective-permute-start.8
  71.8 16.6 %collective-permute-start.10 = (bf16[256,1024]{1,0:T(8,128)(2,1)S(1)}, bf16[256,1024]{1,0:T(8,128)(2,1)S(1)}, u32[]{:S(2)}, u32[]{:S(2)}) collective-permute-start(bf16[256,1024]{1,0:T(8,128)(2,1)S(1)} %get-tuple-element.54.refs_8_.refs_0_), channel_id=1, source_target_pairs={{0,2},{2,0},{4,6},{6,4},{8,10},{10,8},{12,14},{14,12},{16,18},{18,... | collective-permute-start | bytes 1572872 | tf_op jit(solution)/shard_map/ppermute | solution.py:550
  73.5 24.3 %collective-permute-start.11 = (bf16[256,1024]{1,0:T(8,128)(2,1)S(1)}, bf16[256,1024]{1,0:T(8,128)(2,1)S(1)}, u32[]{:S(2)}, u32[]{:S(2)}) collective-permute-start(bf16[256,1024]{1,0:T(8,128)(2,1)S(1)} %get-tuple-element.59.refs_9_.refs_1_), channel_id=1, source_target_pairs={{0,2},{2,0},{4,6},{6,4},{8,10},{10,8},{12,14},{14,12},{16,18},{18,... | collective-permute-start | bytes 1572872 | tf_op jit(solution)/shard_map/ppermute | solution.py:550
  73.8 35.2 %collective-permute-start.14 = (bf16[256,1024]{1,0:T(8,128)(2,1)S(1)}, bf16[256,1024]{1,0:T(8,128)(2,1)S(1)}, u32[]{:S(2)}, u32[]{:S(2)}) collective-permute-start(bf16[256,1024]{1,0:T(8,128)(2,1)S(1)} %get-tuple-element.65.refs_10_.refs_2_), channel_id=1, source_target_pairs={{0,2},{2,0},{4,6},{6,4},{8,10},{10,8},{12,14},{14,12},{16,18},{18,... | collective-permute-start | bytes 1572872 | tf_op jit(solution)/shard_map/ppermute | solution.py:550
  88.4 6.1 %collective-permute-start.13 = (f32[16,2176]{1,0:T(8,128)S(1)}, f32[16,2176]{1,0:T(8,128)S(1)}, u32[]{:S(2)}, u32[]{:S(2)}) collective-permute-start(f32[16,2176]{1,0:T(8,128)S(1)} %kernel_grad.1), channel_id=1, source_target_pairs={{0,8},{2,10},{4,12},{6,14},{8,0},{10,2},{12,4},{14,6},{16,24},{18,... | collective-permute-start | bytes 417800 | tf_op jit(solution)/shard_map/ppermute | solution.py:564
  90.0 33.3 %collective-permute-start.9 = (bf16[256,1024]{1,0:T(8,128)(2,1)S(1)}, bf16[256,1024]{1,0:T(8,128)(2,1)S(1)}, u32[]{:S(2)}, u32[]{:S(2)}) collective-permute-start(bf16[256,1024]{1,0:T(8,128)(2,1)S(1)} %get-tuple-element.53.refs_11_.refs_3_), channel_id=1, source_target_pairs={{0,2},{2,0},{4,6},{6,4},{8,10},{10,8},{12,14},{14,12},{16,18},{18,... | collective-permute-start | bytes 1572872 | tf_op jit(solution)/shard_map/ppermute | solution.py:550
  91.4 36.0 %collective-permute-start.16 = (bf16[256,1024]{1,0:T(8,128)(2,1)S(1)}, bf16[256,1024]{1,0:T(8,128)(2,1)S(1)}, u32[]{:S(2)}, u32[]{:S(2)}) collective-permute-start(bf16[256,1024]{1,0:T(8,128)(2,1)S(1)} %collective-permute-done.10.refs_4_), channel_id=1, source_target_pairs={{0,4},{4,8},{6,2},{8,12},{10,6},{12,16},{14,10},{16,20},{18,14},{2... | collective-permute-start | bytes 1572872 | tf_op jit(solution)/shard_map/ppermute | solution.py:556
  97.8 29.6 %collective-permute-start.17 = (bf16[256,1024]{1,0:T(8,128)(2,1)S(1)}, bf16[256,1024]{1,0:T(8,128)(2,1)S(1)}, u32[]{:S(2)}, u32[]{:S(2)}) collective-permute-start(bf16[256,1024]{1,0:T(8,128)(2,1)S(1)} %collective-permute-done.11.refs_5_), channel_id=1, source_target_pairs={{0,4},{4,8},{6,2},{8,12},{10,6},{12,16},{14,10},{16,20},{18,14},{2... | collective-permute-start | bytes 1572872 | tf_op jit(solution)/shard_map/ppermute | solution.py:556
  109.1 31.5 %collective-permute-start.18 = (bf16[256,1024]{1,0:T(8,128)(2,1)S(1)}, bf16[256,1024]{1,0:T(8,128)(2,1)S(1)}, u32[]{:S(2)}, u32[]{:S(2)}) collective-permute-start(bf16[256,1024]{1,0:T(8,128)(2,1)S(1)} %collective-permute-done.14.refs_6_), channel_id=1, source_target_pairs={{0,4},{4,8},{6,2},{8,12},{10,6},{12,16},{14,10},{16,20},{18,14},{2... | collective-permute-start | bytes 1572872 | tf_op jit(solution)/shard_map/ppermute | solution.py:556
  113.0 14.3 %collective-permute-start.15 = (f32[16,2176]{1,0:T(8,128)S(1)}, f32[16,2176]{1,0:T(8,128)S(1)}, u32[]{:S(2)}, u32[]{:S(2)}) collective-permute-start(f32[16,2176]{1,0:T(8,128)S(1)} %add.23), channel_id=1, source_target_pairs={{0,16},{2,18},{4,20},{6,22},{8,24},{10,26},{12,28},{14,30},{16,0},... | collective-permute-start | bytes 417800 | tf_op jit(solution)/shard_map/ppermute | solution.py:564
  123.3 27.5 %collective-permute-start.12 = (bf16[256,1024]{1,0:T(8,128)(2,1)S(1)}, bf16[256,1024]{1,0:T(8,128)(2,1)S(1)}, u32[]{:S(2)}, u32[]{:S(2)}) collective-permute-start(bf16[256,1024]{1,0:T(8,128)(2,1)S(1)} %collective-permute-done.9.refs_7_), channel_id=1, source_target_pairs={{0,4},{4,8},{6,2},{8,12},{10,6},{12,16},{14,10},{16,20},{18,14},{2... | collective-permute-start | bytes 1572872 | tf_op jit(solution)/shard_map/ppermute | solution.py:556
  127.4 26.0 %collective-permute-start.21 = (f32[16,2176]{1,0:T(8,128)S(1)}, f32[16,2176]{1,0:T(8,128)S(1)}, u32[]{:S(2)}, u32[]{:S(2)}) collective-permute-start(f32[16,2176]{1,0:T(8,128)S(1)} %add.24), channel_id=1, source_target_pairs={{0,6},{2,4},{4,2},{6,0},{8,14},{10,12},{12,10},{14,8},{16,22},{18,... | collective-permute-start | bytes 417800 | tf_op jit(solution)/shard_map/ppermute | solution.py:564
  128.8 24.7 %collective-permute-start.20 = (f32[16,2176]{1,0:T(8,128)S(1)}, f32[16,2176]{1,0:T(8,128)S(1)}, u32[]{:S(2)}, u32[]{:S(2)}) collective-permute-start(f32[16,2176]{1,0:T(8,128)S(1)} %add.24), channel_id=1, source_target_pairs={{0,4},{2,6},{4,0},{6,2},{8,12},{10,14},{12,8},{14,10},{16,20},{18,... | collective-permute-start | bytes 417800 | tf_op jit(solution)/shard_map/ppermute | solution.py:564
  140.6 12.9 %collective-permute-start.19 = (f32[16,2176]{1,0:T(8,128)S(1)}, f32[16,2176]{1,0:T(8,128)S(1)}, u32[]{:S(2)}, u32[]{:S(2)}) collective-permute-start(f32[16,2176]{1,0:T(8,128)S(1)} %add.24), channel_id=1, source_target_pairs={{0,2},{2,0},{4,6},{6,4},{8,10},{10,8},{12,14},{14,12},{16,18},{18,... | collective-permute-start | bytes 417800 | tf_op jit(solution)/shard_map/ppermute | solution.py:564
  (3 other events, 96.4 us)

commit v2 on v1

--- a/solution.py
+++ b/solution.py
@@ -607,14 +607,20 @@
         (grad_near[3], normed, gate_grad, back_band)
     )
     bits = list(range(count.bit_length() - 1))
+    term = jnp.zeros_like(totals)
     for bit in bits[2:]:
-        totals += terms_over_bits(totals, [bit])[0]
+        totals += term
+        term = terms_over_bits(totals, [bit])[0]
         if bit == 2:
+            totals += term
+            term = jnp.zeros_like(totals)
             grad_near[1], totals = lax.optimization_barrier((grad_near[1], totals))
+            grad_near[2], totals = lax.optimization_barrier((grad_near[2], totals))
     grad_far = [relayed(chunk) for chunk in grad_near]
-    totals, *grad_far[:2] = lax.optimization_barrier((totals, *grad_far[:2]))
+    value_grad, first = value_grad_of(back_band, mix_grad, grad_near, grad_far[:-1], lag)
+    totals, term, first = lax.optimization_barrier((totals, term, first))
+    totals += term
     terms = [totals] + terms_over_bits(totals, bits[:2])
-    value_grad, first = value_grad_of(back_band, mix_grad, grad_near, grad_far[:-1], lag)
     value_grad = value_grad_last(back_band, grad_far[-1], first, value_grad)
     value_grad, *terms = lax.optimization_barrier((value_grad, *terms))
     totals = sum(terms[1:], terms[0])

time: 155 us -> 156 us (level)
  waiting for transfers between devices: 37.2 us -> 41.6 us
  starting transfers between devices: 58.5 us -> 55.2 us
    ppermute x5, starting transfers between devices: 17.4 us -> 14.2 us  [terms_over_bits(): lax.ppermute(value, 'seq', [(i, i ^ flip) for i in range(count)])]
    ppermute x5, waiting for transfers between devices: 0.01 us -> 2.48 us  [terms_over_bits(): lax.ppermute(value, 'seq', [(i, i ^ flip) for i in range(count)])]
    ppermute x8, waiting for transfers between devices: 0.02 us -> 1.9 us  [relayed(): lax.ppermute(chunk, 'seq', [(i, j) for i, j in pairs if 0 <= j < count])]
  transfers between devices with their start and end apart: 22 -> 22, of which waited for: 7 -> 10; matrix products, arithmetic and copies ran while one was open for 2% -> 2% of each run, Pallas kernels for 31% -> 30%
where the time goes in v2:
time: 156 us
  starting transfers between devices  55.2 us (35%)
  Pallas kernels  53.7 us (34%)
  waiting for transfers between devices  41.6 us (27%)
  local copies, waits for them, and re-layouts  3.71 us (2%)
    ppermute x8, waiting for transfers between devices, swapped(): return lax.ppermute(chunk, 'seq', [(i, i ^ 1) for i in range(count)])  36 us
    ppermute x8, starting transfers between devices, relayed(): lax.ppermute(chunk, 'seq', [(i, j) for i, j in pairs if 0 <= j < count])  30.6 us
    ppermute x5, starting transfers between devices, terms_over_bits(): lax.ppermute(value, 'seq', [(i, i ^ flip) for i in range(count)])  14.2 us
    pallas_call x1, Pallas kernels, kernel_grad_local(): pl.pallas_call(functools.partial(kernel_grad_body, slots), grid=(pairs,),...  12.8 us
    pallas_call x1, Pallas kernels, forward(): pl.pallas_call(functools.partial(forward_body, slots), grid=(width // LAN...  10.9 us
    ppermute x8, starting transfers between devices, swapped(): return lax.ppermute(chunk, 'seq', [(i, i ^ 1) for i in range(count)])  10.4 us
    pallas_call x1, Pallas kernels, value_grad_of(): pl.pallas_call(functools.partial(value_grad_body, slots), grid=(width //...  10.3 us
    pallas_call x2, Pallas kernels, bands(): pl.pallas_call(band_body, grid=(heads // 2,), in_specs=[VMEM], out_specs=...  6.21 us
  transfers between devices with their start and end apart: 22, of which 10 were waited for; matrix products, arithmetic and copies ran while one was open for 2% of the time, Pallas kernels for 30%

profile of v2, /device:TPU:0, one launch (start us, length us, event | category | flops | bytes accessed | tf_op | source)
XLA Modules:
  0.0 155.9 jit_solution(3026219905923865894)
XLA Ops:
  3.0 3.0 %collective-permute-start.2 = (bf16[256,1024]{1,0:T(8,128)(2,1)}, bf16[256,1024]{1,0:T(8,128)(2,1)S(1)}, u32[]{:S(2)}, u32[]{:S(2)}) collective-permute-start(bf16[256,1024]{1,0:T(8,128)(2,1)} %get-tuple-element.48), channel_id=1, source_target_pairs={{0,2},{2,0},{4,6},{6,4},{8,10},{10,8},{12,14},{14,12},{16,18},{18,... | collective-permute-start | bytes 1572872 | tf_op jit(solution)/shard_map/ppermute | solution.py:550
  11.2 3.1 %bands.2.band_ref = bf16[16,128,2432]{2,1,0:T(8,128)(2,1)S(1)} custom-call(f32[8,2,2304]{2,1,0:T(2,128)S(1)} %reshape.22.row_ref), custom_call_target="tpu_custom_call" | custom-call | flops 4718592 | bytes 9437184 | tf_op jit(solution)/shard_map/bands/pallas_call | solution.py:84
  14.4 4.6 %collective-permute-done.2.refs_0_ = bf16[256,1024]{1,0:T(8,128)(2,1)S(1)} collective-permute-done((bf16[256,1024]{1,0:T(8,128)(2,1)}, bf16[256,1024]{1,0:T(8,128)(2,1)S(1)}, u32[]{:S(2)}, u32[]{:S(2)}) %collective-permute-start.2) | collective-permute-done | bytes 524320 | tf_op jit(solution)/shard_map/ppermute | solution.py:550
  19.0 4.0 %collective-permute-start.5 = (bf16[256,1024]{1,0:T(8,128)(2,1)S(1)}, bf16[256,1024]{1,0:T(8,128)(2,1)S(1)}, u32[]{:S(2)}, u32[]{:S(2)}) collective-permute-start(bf16[256,1024]{1,0:T(8,128)(2,1)S(1)} %collective-permute-done.2.refs_0_), channel_id=1, source_target_pairs={{0,4},{4,8},{6,2},{8,12},{10,6},{12,16},{14,10},{16,20},{18,14},{2... | collective-permute-start | bytes 1572872 | tf_op jit(solution)/shard_map/ppermute | solution.py:556
  23.0 7.2 %collective-permute-done.3.refs_1_ = bf16[256,1024]{1,0:T(8,128)(2,1)S(1)} collective-permute-done((bf16[256,1024]{1,0:T(8,128)(2,1)S(1)}, bf16[256,1024]{1,0:T(8,128)(2,1)S(1)}, u32[]{:S(2)}, u32[]{:S(2)}) %collective-permute-start.3) | collective-permute-done | bytes 524320 | tf_op jit(solution)/shard_map/ppermute | solution.py:550
  30.2 4.0 %collective-permute-start.6 = (bf16[256,1024]{1,0:T(8,128)(2,1)S(1)}, bf16[256,1024]{1,0:T(8,128)(2,1)S(1)}, u32[]{:S(2)}, u32[]{:S(2)}) collective-permute-start(bf16[256,1024]{1,0:T(8,128)(2,1)S(1)} %collective-permute-done.3.refs_1_), channel_id=1, source_target_pairs={{0,4},{4,8},{6,2},{8,12},{10,6},{12,16},{14,10},{16,20},{18,14},{2... | collective-permute-start | bytes 1572872 | tf_op jit(solution)/shard_map/ppermute | solution.py:556
  34.3 7.2 %collective-permute-done.4.refs_2_ = bf16[256,1024]{1,0:T(8,128)(2,1)S(1)} collective-permute-done((bf16[256,1024]{1,0:T(8,128)(2,1)S(1)}, bf16[256,1024]{1,0:T(8,128)(2,1)S(1)}, u32[]{:S(2)}, u32[]{:S(2)}) %collective-permute-start.4) | collective-permute-done | bytes 524320 | tf_op jit(solution)/shard_map/ppermute | solution.py:550
  41.5 4.0 %collective-permute-start.7 = (bf16[256,1024]{1,0:T(8,128)(2,1)S(1)}, bf16[256,1024]{1,0:T(8,128)(2,1)S(1)}, u32[]{:S(2)}, u32[]{:S(2)}) collective-permute-start(bf16[256,1024]{1,0:T(8,128)(2,1)S(1)} %collective-permute-done.4.refs_2_), channel_id=1, source_target_pairs={{0,4},{4,8},{6,2},{8,12},{10,6},{12,16},{14,10},{16,20},{18,14},{2... | collective-permute-start | bytes 1572872 | tf_op jit(solution)/shard_map/ppermute | solution.py:556
  45.5 6.4 %collective-permute-done.refs_3_ = bf16[256,1024]{1,0:T(8,128)(2,1)S(1)} collective-permute-done((bf16[256,1024]{1,0:T(8,128)(2,1)S(1)}, bf16[256,1024]{1,0:T(8,128)(2,1)S(1)}, u32[]{:S(2)}, u32[]{:S(2)}) %collective-permute-start) | collective-permute-done | bytes 524320 | tf_op jit(solution)/shard_map/ppermute | solution.py:550
  51.9 3.7 %collective-permute-start.1 = (bf16[256,1024]{1,0:T(8,128)(2,1)S(1)}, bf16[256,1024]{1,0:T(8,128)(2,1)S(1)}, u32[]{:S(2)}, u32[]{:S(2)}) collective-permute-start(bf16[256,1024]{1,0:T(8,128)(2,1)S(1)} %collective-permute-done.refs_3_), channel_id=1, source_target_pairs={{0,4},{4,8},{6,2},{8,12},{10,6},{12,16},{14,10},{16,20},{18,14},{2... | collective-permute-start | bytes 1572872 | tf_op jit(solution)/shard_map/ppermute | solution.py:556
  55.7 10.9 %forward.1 = (f32[1024,1024]{1,0:T(8,128)S(1)}, f32[2,1024]{1,0:T(2,128)S(1)}) custom-call(bf16[16,128,2432]{2,1,0:T(8,128)(2,1)S(1)} %bands.2.band_ref, bf16[1024,1024]{1,0:T(8,128)(2,1)S(1)} %copy-done.2, bf16[1024,1024]{1,0:T(8,128)(2,1)S(1)} %copy-done, bf16[1024,1024]{1,0:T(8,128)(2,1)S(1)} %copy-done.1, f32[1,1024]{1,0:T(1,128)S(1)} %bitcast.1, ...), custom_call_target="tpu_custom_call" | custom-call | flops 4831838208 | bytes 16777216 | tf_op jit(solution)/shard_map/forward/pallas_call | solution.py:263
  75.5 12.8 %kernel_grad.1 = f32[16,2176]{1,0:T(8,128)S(1)} custom-call(f32[1,1024]{1,0:T(1,128)S(1)} %get-tuple-element.68.gain_ref, bf16[1024,1024]{1,0:T(8,128)(2,1)S(1)} %copy-done.2, bf16[256,1024]{1,0:T(8,128)(2,1)S(1)} %collective-permute-done.2.refs_0_, bf16[256,1024]{1,0:T(8,128)(2,1)S(1)} %collective-permute-done.3.refs_1_, ...), custom_call_target="tpu_custom_call" | custom-call | flops 4831838208 | bytes 8388608 | tf_op jit(solution)/shard_map/kernel_grad/pallas_call | solution.py:463
  91.4 3.0 %collective-permute-start.16 = (bf16[256,1024]{1,0:T(8,128)(2,1)S(1)}, bf16[256,1024]{1,0:T(8,128)(2,1)S(1)}, u32[]{:S(2)}, u32[]{:S(2)}) collective-permute-start(bf16[256,1024]{1,0:T(8,128)(2,1)S(1)} %collective-permute-done.10.refs_4_), channel_id=1, source_target_pairs={{0,4},{4,8},{6,2},{8,12},{10,6},{12,16},{14,10},{16,20},{18,14},{2... | collective-permute-start | bytes 1572872 | tf_op jit(solution)/shard_map/ppermute | solution.py:556
  94.5 3.4 %collective-permute-done.11.refs_5_ = bf16[256,1024]{1,0:T(8,128)(2,1)S(1)} collective-permute-done((bf16[256,1024]{1,0:T(8,128)(2,1)S(1)}, bf16[256,1024]{1,0:T(8,128)(2,1)S(1)}, u32[]{:S(2)}, u32[]{:S(2)}) %collective-permute-start.11) | collective-permute-done | bytes 524320 | tf_op jit(solution)/shard_map/ppermute | solution.py:550
  97.8 4.0 %collective-permute-start.17 = (bf16[256,1024]{1,0:T(8,128)(2,1)S(1)}, bf16[256,1024]{1,0:T(8,128)(2,1)S(1)}, u32[]{:S(2)}, u32[]{:S(2)}) collective-permute-start(bf16[256,1024]{1,0:T(8,128)(2,1)S(1)} %collective-permute-done.11.refs_5_), channel_id=1, source_target_pairs={{0,4},{4,8},{6,2},{8,12},{10,6},{12,16},{14,10},{16,20},{18,14},{2... | collective-permute-start | bytes 1572872 | tf_op jit(solution)/shard_map/ppermute | solution.py:556
  101.8 7.3 %collective-permute-done.13.refs_6_ = bf16[256,1024]{1,0:T(8,128)(2,1)S(1)} collective-permute-done((bf16[256,1024]{1,0:T(8,128)(2,1)S(1)}, bf16[256,1024]{1,0:T(8,128)(2,1)S(1)}, u32[]{:S(2)}, u32[]{:S(2)}) %collective-permute-start.13) | collective-permute-done | bytes 524320 | tf_op jit(solution)/shard_map/ppermute | solution.py:550
  109.1 4.0 %collective-permute-start.18 = (bf16[256,1024]{1,0:T(8,128)(2,1)S(1)}, bf16[256,1024]{1,0:T(8,128)(2,1)S(1)}, u32[]{:S(2)}, u32[]{:S(2)}) collective-permute-start(bf16[256,1024]{1,0:T(8,128)(2,1)S(1)} %collective-permute-done.13.refs_6_), channel_id=1, source_target_pairs={{0,4},{4,8},{6,2},{8,12},{10,6},{12,16},{14,10},{16,20},{18,14},{2... | collective-permute-start | bytes 1572872 | tf_op jit(solution)/shard_map/ppermute | solution.py:556
  113.0 3.1 %bands.3.band_ref = bf16[16,128,2432]{2,1,0:T(8,128)(2,1)S(1)} custom-call(f32[8,2,2304]{2,1,0:T(2,128)S(1)} %reshape.23.row_ref), custom_call_target="tpu_custom_call" | custom-call | flops 4718592 | bytes 9437184 | tf_op jit(solution)/shard_map/bands/pallas_call | solution.py:84
  116.1 4.6 %norm.1 = (bf16[1024,1024]{1,0:T(8,128)(2,1)}, bf16[1024,1024]{1,0:T(8,128)(2,1)}) custom-call(f32[2,1024]{1,0:T(2,128)S(1)} %add.22.sums_ref, f32[1024,1024]{1,0:T(8,128)S(1)} %get-tuple-element.51.mixed_ref, f32[256,1024]{1,0:T(8,128)S(1)} %get-tuple-element.54.first_ref, bf16[1024,1024]{1,0:T(8,128)(2,1)S(1)} %copy-done, ...), custom_call_target="tpu_custom_call" | custom-call | flops 14680064 | bytes 12582912 | tf_op jit(solution)/shard_map/norm/pallas_call | solution.py:398
  120.7 4.0 %collective-permute-start.12 = (bf16[256,1024]{1,0:T(8,128)(2,1)S(1)}, bf16[256,1024]{1,0:T(8,128)(2,1)S(1)}, u32[]{:S(2)}, u32[]{:S(2)}) collective-permute-start(bf16[256,1024]{1,0:T(8,128)(2,1)S(1)} %collective-permute-done.9.refs_7_), channel_id=1, source_target_pairs={{0,4},{4,8},{6,2},{8,12},{10,6},{12,16},{14,10},{16,20},{18,14},{2... | collective-permute-start | bytes 1572872 | tf_op jit(solution)/shard_map/ppermute | solution.py:556
  124.7 2.6 %collective-permute-start.15 = (f32[16,2176]{1,0:T(8,128)S(1)}, f32[16,2176]{1,0:T(8,128)S(1)}, u32[]{:S(2)}, u32[]{:S(2)}) collective-permute-start(f32[16,2176]{1,0:T(8,128)S(1)} %add.23), channel_id=1, source_target_pairs={{0,16},{2,18},{4,20},{6,22},{8,24},{10,26},{12,28},{14,30},{16,0},... | collective-permute-start | bytes 417800 | tf_op jit(solution)/shard_map/ppermute | solution.py:564
  129.2 10.3 %value_grad.1 = (bf16[1024,1024]{1,0:T(8,128)(2,1)}, f32[256,1024]{1,0:T(8,128)S(1)}) custom-call(bf16[16,128,2432]{2,1,0:T(8,128)(2,1)S(1)} %bands.3.band_ref, bf16[256,1024]{1,0:T(8,128)(2,1)S(1)} %get-tuple-element.56.refs_8_.refs_0_, bf16[256,1024]{1,0:T(8,128)(2,1)S(1)} %get-tuple-element.61.refs_9_.refs_1_, ...), custom_call_target="tpu_custom_call" | custom-call | flops 4831838208 | bytes 12582912 | tf_op jit(solution)/shard_map/value_grad/pallas_call | solution.py:502
  139.6 4.8 %collective-permute-start.21 = (f32[16,2176]{1,0:T(8,128)S(1)}, f32[16,2176]{1,0:T(8,128)S(1)}, u32[]{:S(2)}, u32[]{:S(2)}) collective-permute-start(f32[16,2176]{1,0:T(8,128)S(1)} %add.24), channel_id=1, source_target_pairs={{0,6},{2,4},{4,2},{6,0},{8,14},{10,12},{12,10},{14,8},{16,22},{18,... | collective-permute-start | bytes 417800 | tf_op jit(solution)/shard_map/ppermute | solution.py:564
  144.4 5.1 %collective-permute-start.20 = (f32[16,2176]{1,0:T(8,128)S(1)}, f32[16,2176]{1,0:T(8,128)S(1)}, u32[]{:S(2)}, u32[]{:S(2)}) collective-permute-start(f32[16,2176]{1,0:T(8,128)S(1)} %add.24), channel_id=1, source_target_pairs={{0,4},{2,6},{4,0},{6,2},{8,12},{10,14},{12,8},{14,10},{16,20},{18,... | collective-permute-start | bytes 417800 | tf_op jit(solution)/shard_map/ppermute | solution.py:564
  (52 shorter events, 27.9 us)
Async XLA Ops:
  3.0 16.0 %collective-permute-start.2 = (bf16[256,1024]{1,0:T(8,128)(2,1)}, bf16[256,1024]{1,0:T(8,128)(2,1)S(1)}, u32[]{:S(2)}, u32[]{:S(2)}) collective-permute-start(bf16[256,1024]{1,0:T(8,128)(2,1)} %get-tuple-element.48), channel_id=1, source_target_pairs={{0,2},{2,0},{4,6},{6,4},{8,10},{10,8},{12,14},{14,12},{16,18},{18,... | collective-permute-start | bytes 1572872 | tf_op jit(solution)/shard_map/ppermute | solution.py:550
  6.0 24.2 %collective-permute-start.3 = (bf16[256,1024]{1,0:T(8,128)(2,1)S(1)}, bf16[256,1024]{1,0:T(8,128)(2,1)S(1)}, u32[]{:S(2)}, u32[]{:S(2)}) collective-permute-start(bf16[256,1024]{1,0:T(8,128)(2,1)S(1)} %get-tuple-element.49), channel_id=1, source_target_pairs={{0,2},{2,0},{4,6},{6,4},{8,10},{10,8},{12,14},{14,12},{16,18},{18,... | collective-permute-start | bytes 1572872 | tf_op jit(solution)/shard_map/ppermute | solution.py:550
  6.1 35.4 %collective-permute-start.4 = (bf16[256,1024]{1,0:T(8,128)(2,1)S(1)}, bf16[256,1024]{1,0:T(8,128)(2,1)S(1)}, u32[]{:S(2)}, u32[]{:S(2)}) collective-permute-start(bf16[256,1024]{1,0:T(8,128)(2,1)S(1)} %get-tuple-element.50), channel_id=1, source_target_pairs={{0,2},{2,0},{4,6},{6,4},{8,10},{10,8},{12,14},{14,12},{16,18},{18,... | collective-permute-start | bytes 1572872 | tf_op jit(solution)/shard_map/ppermute | solution.py:550
  11.1 44.5 %copy-start = (bf16[1024,1024]{1,0:T(8,128)(2,1)S(1)}, bf16[1024,1024]{1,0:T(8,128)(2,1)}, u32[]{:S(2)}) copy-start(bf16[1024,1024]{1,0:T(8,128)(2,1)} %gate_ref.7) | copy-start | bytes 6291460
  11.1 44.5 %copy-start.1 = (bf16[1024,1024]{1,0:T(8,128)(2,1)S(1)}, bf16[1024,1024]{1,0:T(8,128)(2,1)}, u32[]{:S(2)}) copy-start(bf16[1024,1024]{1,0:T(8,128)(2,1)} %grad_ref.7) | copy-start | bytes 6291460
  14.3 37.6 %collective-permute-start = (bf16[256,1024]{1,0:T(8,128)(2,1)S(1)}, bf16[256,1024]{1,0:T(8,128)(2,1)S(1)}, u32[]{:S(2)}, u32[]{:S(2)}) collective-permute-start(bf16[256,1024]{1,0:T(8,128)(2,1)S(1)} %get-tuple-element.47), channel_id=1, source_target_pairs={{0,2},{2,0},{4,6},{6,4},{8,10},{10,8},{12,14},{14,12},{16,18},{18,... | collective-permute-start | bytes 1572872 | tf_op jit(solution)/shard_map/ppermute | solution.py:550
  19.0 36.6 %collective-permute-start.5 = (bf16[256,1024]{1,0:T(8,128)(2,1)S(1)}, bf16[256,1024]{1,0:T(8,128)(2,1)S(1)}, u32[]{:S(2)}, u32[]{:S(2)}) collective-permute-start(bf16[256,1024]{1,0:T(8,128)(2,1)S(1)} %collective-permute-done.2.refs_0_), channel_id=1, source_target_pairs={{0,4},{4,8},{6,2},{8,12},{10,6},{12,16},{14,10},{16,20},{18,14},{2... | collective-permute-start | bytes 1572872 | tf_op jit(solution)/shard_map/ppermute | solution.py:556
  30.2 25.4 %collective-permute-start.6 = (bf16[256,1024]{1,0:T(8,128)(2,1)S(1)}, bf16[256,1024]{1,0:T(8,128)(2,1)S(1)}, u32[]{:S(2)}, u32[]{:S(2)}) collective-permute-start(bf16[256,1024]{1,0:T(8,128)(2,1)S(1)} %collective-permute-done.3.refs_1_), channel_id=1, source_target_pairs={{0,4},{4,8},{6,2},{8,12},{10,6},{12,16},{14,10},{16,20},{18,14},{2... | collective-permute-start | bytes 1572872 | tf_op jit(solution)/shard_map/ppermute | solution.py:556
  41.5 14.1 %collective-permute-start.7 = (bf16[256,1024]{1,0:T(8,128)(2,1)S(1)}, bf16[256,1024]{1,0:T(8,128)(2,1)S(1)}, u32[]{:S(2)}, u32[]{:S(2)}) collective-permute-start(bf16[256,1024]{1,0:T(8,128)(2,1)S(1)} %collective-permute-done.4.refs_2_), channel_id=1, source_target_pairs={{0,4},{4,8},{6,2},{8,12},{10,6},{12,16},{14,10},{16,20},{18,14},{2... | collective-permute-start | bytes 1572872 | tf_op jit(solution)/shard_map/ppermute | solution.py:556
  51.9 14.7 %collective-permute-start.1 = (bf16[256,1024]{1,0:T(8,128)(2,1)S(1)}, bf16[256,1024]{1,0:T(8,128)(2,1)S(1)}, u32[]{:S(2)}, u32[]{:S(2)}) collective-permute-start(bf16[256,1024]{1,0:T(8,128)(2,1)S(1)} %collective-permute-done.refs_3_), channel_id=1, source_target_pairs={{0,4},{4,8},{6,2},{8,12},{10,6},{12,16},{14,10},{16,20},{18,14},{2... | collective-permute-start | bytes 1572872 | tf_op jit(solution)/shard_map/ppermute | solution.py:556
  68.7 1.2 collective-permute-start.8
  71.8 16.6 %collective-permute-start.10 = (bf16[256,1024]{1,0:T(8,128)(2,1)S(1)}, bf16[256,1024]{1,0:T(8,128)(2,1)S(1)}, u32[]{:S(2)}, u32[]{:S(2)}) collective-permute-start(bf16[256,1024]{1,0:T(8,128)(2,1)S(1)} %get-tuple-element.56.refs_8_.refs_0_), channel_id=1, source_target_pairs={{0,2},{2,0},{4,6},{6,4},{8,10},{10,8},{12,14},{14,12},{16,18},{18,... | collective-permute-start | bytes 1572872 | tf_op jit(solution)/shard_map/ppermute | solution.py:550
  73.5 24.3 %collective-permute-start.11 = (bf16[256,1024]{1,0:T(8,128)(2,1)S(1)}, bf16[256,1024]{1,0:T(8,128)(2,1)S(1)}, u32[]{:S(2)}, u32[]{:S(2)}) collective-permute-start(bf16[256,1024]{1,0:T(8,128)(2,1)S(1)} %get-tuple-element.61.refs_9_.refs_1_), channel_id=1, source_target_pairs={{0,2},{2,0},{4,6},{6,4},{8,10},{10,8},{12,14},{14,12},{16,18},{18,... | collective-permute-start | bytes 1572872 | tf_op jit(solution)/shard_map/ppermute | solution.py:550
  73.8 35.2 %collective-permute-start.13 = (bf16[256,1024]{1,0:T(8,128)(2,1)S(1)}, bf16[256,1024]{1,0:T(8,128)(2,1)S(1)}, u32[]{:S(2)}, u32[]{:S(2)}) collective-permute-start(bf16[256,1024]{1,0:T(8,128)(2,1)S(1)} %get-tuple-element.67.refs_10_.refs_2_), channel_id=1, source_target_pairs={{0,2},{2,0},{4,6},{6,4},{8,10},{10,8},{12,14},{14,12},{16,18},{18,... | collective-permute-start | bytes 1572872 | tf_op jit(solution)/shard_map/ppermute | solution.py:550
  88.4 6.1 %collective-permute-start.14 = (f32[16,2176]{1,0:T(8,128)S(1)}, f32[16,2176]{1,0:T(8,128)S(1)}, u32[]{:S(2)}, u32[]{:S(2)}) collective-permute-start(f32[16,2176]{1,0:T(8,128)S(1)} %kernel_grad.1), channel_id=1, source_target_pairs={{0,8},{2,10},{4,12},{6,14},{8,0},{10,2},{12,4},{14,6},{16,24},{18,... | collective-permute-start | bytes 417800 | tf_op jit(solution)/shard_map/ppermute | solution.py:564
  90.0 30.7 %collective-permute-start.9 = (bf16[256,1024]{1,0:T(8,128)(2,1)S(1)}, bf16[256,1024]{1,0:T(8,128)(2,1)S(1)}, u32[]{:S(2)}, u32[]{:S(2)}) collective-permute-start(bf16[256,1024]{1,0:T(8,128)(2,1)S(1)} %get-tuple-element.55.refs_11_.refs_3_), channel_id=1, source_target_pairs={{0,2},{2,0},{4,6},{6,4},{8,10},{10,8},{12,14},{14,12},{16,18},{18,... | collective-permute-start | bytes 1572872 | tf_op jit(solution)/shard_map/ppermute | solution.py:550
  91.4 35.9 %collective-permute-start.16 = (bf16[256,1024]{1,0:T(8,128)(2,1)S(1)}, bf16[256,1024]{1,0:T(8,128)(2,1)S(1)}, u32[]{:S(2)}, u32[]{:S(2)}) collective-permute-start(bf16[256,1024]{1,0:T(8,128)(2,1)S(1)} %collective-permute-done.10.refs_4_), channel_id=1, source_target_pairs={{0,4},{4,8},{6,2},{8,12},{10,6},{12,16},{14,10},{16,20},{18,14},{2... | collective-permute-start | bytes 1572872 | tf_op jit(solution)/shard_map/ppermute | solution.py:556
  97.8 29.5 %collective-permute-start.17 = (bf16[256,1024]{1,0:T(8,128)(2,1)S(1)}, bf16[256,1024]{1,0:T(8,128)(2,1)S(1)}, u32[]{:S(2)}, u32[]{:S(2)}) collective-permute-start(bf16[256,1024]{1,0:T(8,128)(2,1)S(1)} %collective-permute-done.11.refs_5_), channel_id=1, source_target_pairs={{0,4},{4,8},{6,2},{8,12},{10,6},{12,16},{14,10},{16,20},{18,14},{2... | collective-permute-start | bytes 1572872 | tf_op jit(solution)/shard_map/ppermute | solution.py:556
  109.1 20.2 %collective-permute-start.18 = (bf16[256,1024]{1,0:T(8,128)(2,1)S(1)}, bf16[256,1024]{1,0:T(8,128)(2,1)S(1)}, u32[]{:S(2)}, u32[]{:S(2)}) collective-permute-start(bf16[256,1024]{1,0:T(8,128)(2,1)S(1)} %collective-permute-done.13.refs_6_), channel_id=1, source_target_pairs={{0,4},{4,8},{6,2},{8,12},{10,6},{12,16},{14,10},{16,20},{18,14},{2... | collective-permute-start | bytes 1572872 | tf_op jit(solution)/shard_map/ppermute | solution.py:556
  120.7 28.7 %collective-permute-start.12 = (bf16[256,1024]{1,0:T(8,128)(2,1)S(1)}, bf16[256,1024]{1,0:T(8,128)(2,1)S(1)}, u32[]{:S(2)}, u32[]{:S(2)}) collective-permute-start(bf16[256,1024]{1,0:T(8,128)(2,1)S(1)} %collective-permute-done.9.refs_7_), channel_id=1, source_target_pairs={{0,4},{4,8},{6,2},{8,12},{10,6},{12,16},{14,10},{16,20},{18,14},{2... | collective-permute-start | bytes 1572872 | tf_op jit(solution)/shard_map/ppermute | solution.py:556
  124.7 14.8 %collective-permute-start.15 = (f32[16,2176]{1,0:T(8,128)S(1)}, f32[16,2176]{1,0:T(8,128)S(1)}, u32[]{:S(2)}, u32[]{:S(2)}) collective-permute-start(f32[16,2176]{1,0:T(8,128)S(1)} %add.23), channel_id=1, source_target_pairs={{0,16},{2,18},{4,20},{6,22},{8,24},{10,26},{12,28},{14,30},{16,0},... | collective-permute-start | bytes 417800 | tf_op jit(solution)/shard_map/ppermute | solution.py:564
  139.6 12.5 %collective-permute-start.21 = (f32[16,2176]{1,0:T(8,128)S(1)}, f32[16,2176]{1,0:T(8,128)S(1)}, u32[]{:S(2)}, u32[]{:S(2)}) collective-permute-start(f32[16,2176]{1,0:T(8,128)S(1)} %add.24), channel_id=1, source_target_pairs={{0,6},{2,4},{4,2},{6,0},{8,14},{10,12},{12,10},{14,8},{16,22},{18,... | collective-permute-start | bytes 417800 | tf_op jit(solution)/shard_map/ppermute | solution.py:564
  144.4 8.1 %collective-permute-start.20 = (f32[16,2176]{1,0:T(8,128)S(1)}, f32[16,2176]{1,0:T(8,128)S(1)}, u32[]{:S(2)}, u32[]{:S(2)}) collective-permute-start(f32[16,2176]{1,0:T(8,128)S(1)} %add.24), channel_id=1, source_target_pairs={{0,4},{2,6},{4,0},{6,2},{8,12},{10,14},{12,8},{14,10},{16,20},{18,... | collective-permute-start | bytes 417800 | tf_op jit(solution)/shard_map/ppermute | solution.py:564
  149.5 5.1 %collective-permute-start.19 = (f32[16,2176]{1,0:T(8,128)S(1)}, f32[16,2176]{1,0:T(8,128)S(1)}, u32[]{:S(2)}, u32[]{:S(2)}) collective-permute-start(f32[16,2176]{1,0:T(8,128)S(1)} %add.24), channel_id=1, source_target_pairs={{0,2},{2,0},{4,6},{6,4},{8,10},{10,8},{12,14},{14,12},{16,18},{18,... | collective-permute-start | bytes 417800 | tf_op jit(solution)/shard_map/ppermute | solution.py:564
  (3 other events, 96.4 us)

commit v3 on v1

--- a/solution.py
+++ b/solution.py
@@ -420,13 +420,12 @@
     lags = span - LANES
     gains = gain_ref[:, slab(pair)]
     for half in range(2):
-        mix = mix_even_ref[half]
+        mix = mix_even_ref[half].T
         carry = None
         for lag_slot in range(slots):
-            cross = lax.dot_general(
+            cross = jnp.dot(
                 window(even_ref, odd_ref, half, slots - 1 - lag_slot, width),
                 mix,
-                (((1,), (1,)), ((), ())),
                 preferred_element_type=jnp.float32,
             )
             at = 2 * lag_slot * LANES
@@ -609,8 +608,7 @@
     bits = list(range(count.bit_length() - 1))
     for bit in bits[2:]:
         totals += terms_over_bits(totals, [bit])[0]
-        if bit == 2:
-            grad_near[1], totals = lax.optimization_barrier((grad_near[1], totals))
+    grad_near[1], totals = lax.optimization_barrier((grad_near[1], totals))
     grad_far = [relayed(chunk) for chunk in grad_near]
     totals, *grad_far[:2] = lax.optimization_barrier((totals, *grad_far[:2]))
     terms = [totals] + terms_over_bits(totals, bits[:2])

time: 155 us -> 154 us (level)
  starting transfers between devices: 58.5 us -> 51.8 us
  waiting for transfers between devices: 37.2 us -> 41.9 us
    ppermute x8, waiting for transfers between devices: 0.02 us -> 7.89 us  [relayed(): lax.ppermute(chunk, 'seq', [(i, j) for i, j in pairs if 0 <= j < count])]
    ppermute x8, waiting for transfers between devices: 36 us -> 28.6 us  [swapped(): return lax.ppermute(chunk, 'seq', [(i, i ^ 1) for i in range(count)])]
    ppermute x5, starting transfers between devices: 17.4 us -> 10.2 us  [terms_over_bits(): lax.ppermute(value, 'seq', [(i, i ^ flip) for i in range(count)])]
    ppermute x5, waiting for transfers between devices: 0.01 us -> 4.27 us  [terms_over_bits(): lax.ppermute(value, 'seq', [(i, i ^ flip) for i in range(count)])]
  transfers between devices with their start and end apart: 22 -> 22, of which waited for: 7 -> 9; matrix products, arithmetic and copies ran while one was open for 2% -> 2% of each run, Pallas kernels for 31% -> 31%
where the time goes in v3:
time: 154 us; the launch traced here: 153 us
  Pallas kernels  53.7 us (35%)
  starting transfers between devices  51.8 us (34%)
  waiting for transfers between devices  41.9 us (27%)
  local copies, waits for them, and re-layouts  3.71 us (2%)
    ppermute x8, starting transfers between devices, relayed(): lax.ppermute(chunk, 'seq', [(i, j) for i, j in pairs if 0 <= j < count])  31.1 us
    ppermute x8, waiting for transfers between devices, swapped(): return lax.ppermute(chunk, 'seq', [(i, i ^ 1) for i in range(count)])  28.6 us
    pallas_call x1, Pallas kernels, kernel_grad_local(): pl.pallas_call(functools.partial(kernel_grad_body, slots), grid=(pairs,),...  12.8 us
    pallas_call x1, Pallas kernels, forward(): pl.pallas_call(functools.partial(forward_body, slots), grid=(width // LAN...  10.9 us
    ppermute x8, starting transfers between devices, swapped(): return lax.ppermute(chunk, 'seq', [(i, i ^ 1) for i in range(count)])  10.4 us
    pallas_call x1, Pallas kernels, value_grad_of(): pl.pallas_call(functools.partial(value_grad_body, slots), grid=(width //...  10.3 us
    ppermute x5, starting transfers between devices, terms_over_bits(): lax.ppermute(value, 'seq', [(i, i ^ flip) for i in range(count)])  10.2 us
    ppermute x8, waiting for transfers between devices, relayed(): lax.ppermute(chunk, 'seq', [(i, j) for i, j in pairs if 0 <= j < count])  7.89 us
  transfers between devices with their start and end apart: 22, of which 9 were waited for; matrix products, arithmetic and copies ran while one was open for 2% of the time, Pallas kernels for 31%

profile of v3, /device:TPU:0, one launch (start us, length us, event | category | flops | bytes accessed | tf_op | source)
XLA Modules:
  0.0 152.8 jit_solution(2955364048891202683)
XLA Ops:
  3.0 3.0 %collective-permute-start.2 = (bf16[256,1024]{1,0:T(8,128)(2,1)}, bf16[256,1024]{1,0:T(8,128)(2,1)S(1)}, u32[]{:S(2)}, u32[]{:S(2)}) collective-permute-start(bf16[256,1024]{1,0:T(8,128)(2,1)} %get-tuple-element.46), channel_id=1, source_target_pairs={{0,2},{2,0},{4,6},{6,4},{8,10},{10,8},{12,14},{14,12},{16,18},{18,... | collective-permute-start | bytes 1572872 | tf_op jit(solution)/shard_map/ppermute | solution.py:549
  11.2 3.1 %bands.2.band_ref = bf16[16,128,2432]{2,1,0:T(8,128)(2,1)S(1)} custom-call(f32[8,2,2304]{2,1,0:T(2,128)S(1)} %reshape.22.row_ref), custom_call_target="tpu_custom_call" | custom-call | flops 4718592 | bytes 9437184 | tf_op jit(solution)/shard_map/bands/pallas_call | solution.py:84
  14.4 4.6 %collective-permute-done.2.refs_0_ = bf16[256,1024]{1,0:T(8,128)(2,1)S(1)} collective-permute-done((bf16[256,1024]{1,0:T(8,128)(2,1)}, bf16[256,1024]{1,0:T(8,128)(2,1)S(1)}, u32[]{:S(2)}, u32[]{:S(2)}) %collective-permute-start.2) | collective-permute-done | bytes 524320 | tf_op jit(solution)/shard_map/ppermute | solution.py:549
  19.0 4.0 %collective-permute-start.5 = (bf16[256,1024]{1,0:T(8,128)(2,1)S(1)}, bf16[256,1024]{1,0:T(8,128)(2,1)S(1)}, u32[]{:S(2)}, u32[]{:S(2)}) collective-permute-start(bf16[256,1024]{1,0:T(8,128)(2,1)S(1)} %collective-permute-done.2.refs_0_), channel_id=1, source_target_pairs={{0,4},{4,8},{6,2},{8,12},{10,6},{12,16},{14,10},{16,20},{18,14},{2... | collective-permute-start | bytes 1572872 | tf_op jit(solution)/shard_map/ppermute | solution.py:555
  23.0 7.2 %collective-permute-done.3.refs_1_ = bf16[256,1024]{1,0:T(8,128)(2,1)S(1)} collective-permute-done((bf16[256,1024]{1,0:T(8,128)(2,1)S(1)}, bf16[256,1024]{1,0:T(8,128)(2,1)S(1)}, u32[]{:S(2)}, u32[]{:S(2)}) %collective-permute-start.3) | collective-permute-done | bytes 524320 | tf_op jit(solution)/shard_map/ppermute | solution.py:549
  30.2 4.0 %collective-permute-start.6 = (bf16[256,1024]{1,0:T(8,128)(2,1)S(1)}, bf16[256,1024]{1,0:T(8,128)(2,1)S(1)}, u32[]{:S(2)}, u32[]{:S(2)}) collective-permute-start(bf16[256,1024]{1,0:T(8,128)(2,1)S(1)} %collective-permute-done.3.refs_1_), channel_id=1, source_target_pairs={{0,4},{4,8},{6,2},{8,12},{10,6},{12,16},{14,10},{16,20},{18,14},{2... | collective-permute-start | bytes 1572872 | tf_op jit(solution)/shard_map/ppermute | solution.py:555
  34.3 7.2 %collective-permute-done.4.refs_2_ = bf16[256,1024]{1,0:T(8,128)(2,1)S(1)} collective-permute-done((bf16[256,1024]{1,0:T(8,128)(2,1)S(1)}, bf16[256,1024]{1,0:T(8,128)(2,1)S(1)}, u32[]{:S(2)}, u32[]{:S(2)}) %collective-permute-start.4) | collective-permute-done | bytes 524320 | tf_op jit(solution)/shard_map/ppermute | solution.py:549
  41.5 4.0 %collective-permute-start.7 = (bf16[256,1024]{1,0:T(8,128)(2,1)S(1)}, bf16[256,1024]{1,0:T(8,128)(2,1)S(1)}, u32[]{:S(2)}, u32[]{:S(2)}) collective-permute-start(bf16[256,1024]{1,0:T(8,128)(2,1)S(1)} %collective-permute-done.4.refs_2_), channel_id=1, source_target_pairs={{0,4},{4,8},{6,2},{8,12},{10,6},{12,16},{14,10},{16,20},{18,14},{2... | collective-permute-start | bytes 1572872 | tf_op jit(solution)/shard_map/ppermute | solution.py:555
  45.5 6.4 %collective-permute-done.refs_3_ = bf16[256,1024]{1,0:T(8,128)(2,1)S(1)} collective-permute-done((bf16[256,1024]{1,0:T(8,128)(2,1)S(1)}, bf16[256,1024]{1,0:T(8,128)(2,1)S(1)}, u32[]{:S(2)}, u32[]{:S(2)}) %collective-permute-start) | collective-permute-done | bytes 524320 | tf_op jit(solution)/shard_map/ppermute | solution.py:549
  51.9 3.7 %collective-permute-start.1 = (bf16[256,1024]{1,0:T(8,128)(2,1)S(1)}, bf16[256,1024]{1,0:T(8,128)(2,1)S(1)}, u32[]{:S(2)}, u32[]{:S(2)}) collective-permute-start(bf16[256,1024]{1,0:T(8,128)(2,1)S(1)} %collective-permute-done.refs_3_), channel_id=1, source_target_pairs={{0,4},{4,8},{6,2},{8,12},{10,6},{12,16},{14,10},{16,20},{18,14},{2... | collective-permute-start | bytes 1572872 | tf_op jit(solution)/shard_map/ppermute | solution.py:555
  55.7 10.9 %forward.1 = (f32[1024,1024]{1,0:T(8,128)S(1)}, f32[2,1024]{1,0:T(2,128)S(1)}) custom-call(bf16[16,128,2432]{2,1,0:T(8,128)(2,1)S(1)} %bands.2.band_ref, bf16[1024,1024]{1,0:T(8,128)(2,1)S(1)} %copy-done.2, bf16[1024,1024]{1,0:T(8,128)(2,1)S(1)} %copy-done, bf16[1024,1024]{1,0:T(8,128)(2,1)S(1)} %copy-done.1, f32[1,1024]{1,0:T(1,128)S(1)} %bitcast.1, ...), custom_call_target="tpu_custom_call" | custom-call | flops 4831838208 | bytes 16777216 | tf_op jit(solution)/shard_map/forward/pallas_call | solution.py:263
  75.5 12.8 %kernel_grad.1 = f32[16,2176]{1,0:T(8,128)S(1)} custom-call(f32[1,1024]{1,0:T(1,128)S(1)} %get-tuple-element.66.gain_ref, bf16[1024,1024]{1,0:T(8,128)(2,1)S(1)} %copy-done.2, bf16[256,1024]{1,0:T(8,128)(2,1)S(1)} %collective-permute-done.2.refs_0_, bf16[256,1024]{1,0:T(8,128)(2,1)S(1)} %collective-permute-done.3.refs_1_, ...), custom_call_target="tpu_custom_call" | custom-call | flops 4831838208 | bytes 8388608 | tf_op jit(solution)/shard_map/kernel_grad/pallas_call | solution.py:462
  90.0 3.5 %collective-permute-done.13 = f32[16,2176]{1,0:T(8,128)S(1)} collective-permute-done((f32[16,2176]{1,0:T(8,128)S(1)}, f32[16,2176]{1,0:T(8,128)S(1)}, u32[]{:S(2)}, u32[]{:S(2)}) %collective-permute-start.13) | collective-permute-done | bytes 139296 | tf_op jit(solution)/shard_map/ppermute | solution.py:563
  93.5 2.7 %collective-permute-start.14 = (f32[16,2176]{1,0:T(8,128)S(1)}, f32[16,2176]{1,0:T(8,128)S(1)}, u32[]{:S(2)}, u32[]{:S(2)}) collective-permute-start(f32[16,2176]{1,0:T(8,128)S(1)} %add.23), channel_id=1, source_target_pairs={{0,16},{2,18},{4,20},{6,22},{8,24},{10,26},{12,28},{14,30},{16,0},... | collective-permute-start | bytes 417800 | tf_op jit(solution)/shard_map/ppermute | solution.py:563
  97.6 3.1 %collective-permute-start.16 = (bf16[256,1024]{1,0:T(8,128)(2,1)S(1)}, bf16[256,1024]{1,0:T(8,128)(2,1)S(1)}, u32[]{:S(2)}, u32[]{:S(2)}) collective-permute-start(bf16[256,1024]{1,0:T(8,128)(2,1)S(1)} %collective-permute-done.10.refs_4_), channel_id=1, source_target_pairs={{0,4},{4,8},{6,2},{8,12},{10,6},{12,16},{14,10},{16,20},{18,14},{2... | collective-permute-start | bytes 1572872 | tf_op jit(solution)/shard_map/ppermute | solution.py:555
  101.5 4.4 %collective-permute-start.17 = (bf16[256,1024]{1,0:T(8,128)(2,1)S(1)}, bf16[256,1024]{1,0:T(8,128)(2,1)S(1)}, u32[]{:S(2)}, u32[]{:S(2)}) collective-permute-start(bf16[256,1024]{1,0:T(8,128)(2,1)S(1)} %collective-permute-done.11.refs_5_), channel_id=1, source_target_pairs={{0,4},{4,8},{6,2},{8,12},{10,6},{12,16},{14,10},{16,20},{18,14},{2... | collective-permute-start | bytes 1572872 | tf_op jit(solution)/shard_map/ppermute | solution.py:555
  105.9 3.2 %collective-permute-done.15.refs_6_ = bf16[256,1024]{1,0:T(8,128)(2,1)S(1)} collective-permute-done((bf16[256,1024]{1,0:T(8,128)(2,1)S(1)}, bf16[256,1024]{1,0:T(8,128)(2,1)S(1)}, u32[]{:S(2)}, u32[]{:S(2)}) %collective-permute-start.15) | collective-permute-done | bytes 524320 | tf_op jit(solution)/shard_map/ppermute | solution.py:549
  109.1 4.0 %collective-permute-start.18 = (bf16[256,1024]{1,0:T(8,128)(2,1)S(1)}, bf16[256,1024]{1,0:T(8,128)(2,1)S(1)}, u32[]{:S(2)}, u32[]{:S(2)}) collective-permute-start(bf16[256,1024]{1,0:T(8,128)(2,1)S(1)} %collective-permute-done.15.refs_6_), channel_id=1, source_target_pairs={{0,4},{4,8},{6,2},{8,12},{10,6},{12,16},{14,10},{16,20},{18,14},{2... | collective-permute-start | bytes 1572872 | tf_op jit(solution)/shard_map/ppermute | solution.py:555
  113.0 3.1 %bands.3.band_ref = bf16[16,128,2432]{2,1,0:T(8,128)(2,1)S(1)} custom-call(f32[8,2,2304]{2,1,0:T(2,128)S(1)} %reshape.23.row_ref), custom_call_target="tpu_custom_call" | custom-call | flops 4718592 | bytes 9437184 | tf_op jit(solution)/shard_map/bands/pallas_call | solution.py:84
  116.1 4.6 %norm.1 = (bf16[1024,1024]{1,0:T(8,128)(2,1)}, bf16[1024,1024]{1,0:T(8,128)(2,1)}) custom-call(f32[2,1024]{1,0:T(2,128)S(1)} %add.22.sums_ref, f32[1024,1024]{1,0:T(8,128)S(1)} %get-tuple-element.49.mixed_ref, f32[256,1024]{1,0:T(8,128)S(1)} %get-tuple-element.52.first_ref, bf16[1024,1024]{1,0:T(8,128)(2,1)S(1)} %copy-done, ...), custom_call_target="tpu_custom_call" | custom-call | flops 14680064 | bytes 12582912 | tf_op jit(solution)/shard_map/norm/pallas_call | solution.py:398
  120.7 4.0 %collective-permute-start.12 = (bf16[256,1024]{1,0:T(8,128)(2,1)S(1)}, bf16[256,1024]{1,0:T(8,128)(2,1)S(1)}, u32[]{:S(2)}, u32[]{:S(2)}) collective-permute-start(bf16[256,1024]{1,0:T(8,128)(2,1)S(1)} %collective-permute-done.9.refs_7_), channel_id=1, source_target_pairs={{0,4},{4,8},{6,2},{8,12},{10,6},{12,16},{14,10},{16,20},{18,14},{2... | collective-permute-start | bytes 1572872 | tf_op jit(solution)/shard_map/ppermute | solution.py:555
  124.7 5.3 %collective-permute-start.21 = (f32[16,2176]{1,0:T(8,128)S(1)}, f32[16,2176]{1,0:T(8,128)S(1)}, u32[]{:S(2)}, u32[]{:S(2)}) collective-permute-start(f32[16,2176]{1,0:T(8,128)S(1)} %add.24), channel_id=1, source_target_pairs={{0,6},{2,4},{4,2},{6,0},{8,14},{10,12},{12,10},{14,8},{16,22},{18,... | collective-permute-start | bytes 417800 | tf_op jit(solution)/shard_map/ppermute | solution.py:563
  130.6 7.9 %collective-permute-done.18.refs_10_ = bf16[256,1024]{1,0:T(8,128)(2,1)S(1)} collective-permute-done((bf16[256,1024]{1,0:T(8,128)(2,1)S(1)}, bf16[256,1024]{1,0:T(8,128)(2,1)S(1)}, u32[]{:S(2)}, u32[]{:S(2)}) %collective-permute-start.18) | collective-permute-done | bytes 524320 | tf_op jit(solution)/shard_map/ppermute | solution.py:555
  138.5 10.3 %value_grad.1 = (bf16[1024,1024]{1,0:T(8,128)(2,1)}, f32[256,1024]{1,0:T(8,128)S(1)}) custom-call(bf16[16,128,2432]{2,1,0:T(8,128)(2,1)S(1)} %bands.3.band_ref, bf16[256,1024]{1,0:T(8,128)(2,1)S(1)} %get-tuple-element.54.refs_8_.refs_0_, bf16[256,1024]{1,0:T(8,128)(2,1)S(1)} %get-tuple-element.59.refs_9_.refs_1_, ...), custom_call_target="tpu_custom_call" | custom-call | flops 4831838208 | bytes 12582912 | tf_op jit(solution)/shard_map/value_grad/pallas_call | solution.py:501
  (52 shorter events, 24.9 us)
Async XLA Ops:
  3.0 16.0 %collective-permute-start.2 = (bf16[256,1024]{1,0:T(8,128)(2,1)}, bf16[256,1024]{1,0:T(8,128)(2,1)S(1)}, u32[]{:S(2)}, u32[]{:S(2)}) collective-permute-start(bf16[256,1024]{1,0:T(8,128)(2,1)} %get-tuple-element.46), channel_id=1, source_target_pairs={{0,2},{2,0},{4,6},{6,4},{8,10},{10,8},{12,14},{14,12},{16,18},{18,... | collective-permute-start | bytes 1572872 | tf_op jit(solution)/shard_map/ppermute | solution.py:549
  6.0 24.2 %collective-permute-start.3 = (bf16[256,1024]{1,0:T(8,128)(2,1)S(1)}, bf16[256,1024]{1,0:T(8,128)(2,1)S(1)}, u32[]{:S(2)}, u32[]{:S(2)}) collective-permute-start(bf16[256,1024]{1,0:T(8,128)(2,1)S(1)} %get-tuple-element.47), channel_id=1, source_target_pairs={{0,2},{2,0},{4,6},{6,4},{8,10},{10,8},{12,14},{14,12},{16,18},{18,... | collective-permute-start | bytes 1572872 | tf_op jit(solution)/shard_map/ppermute | solution.py:549
  6.1 35.4 %collective-permute-start.4 = (bf16[256,1024]{1,0:T(8,128)(2,1)S(1)}, bf16[256,1024]{1,0:T(8,128)(2,1)S(1)}, u32[]{:S(2)}, u32[]{:S(2)}) collective-permute-start(bf16[256,1024]{1,0:T(8,128)(2,1)S(1)} %get-tuple-element.48), channel_id=1, source_target_pairs={{0,2},{2,0},{4,6},{6,4},{8,10},{10,8},{12,14},{14,12},{16,18},{18,... | collective-permute-start | bytes 1572872 | tf_op jit(solution)/shard_map/ppermute | solution.py:549
  11.1 44.5 %copy-start = (bf16[1024,1024]{1,0:T(8,128)(2,1)S(1)}, bf16[1024,1024]{1,0:T(8,128)(2,1)}, u32[]{:S(2)}) copy-start(bf16[1024,1024]{1,0:T(8,128)(2,1)} %gate_ref.7) | copy-start | bytes 6291460
  11.1 44.5 %copy-start.1 = (bf16[1024,1024]{1,0:T(8,128)(2,1)S(1)}, bf16[1024,1024]{1,0:T(8,128)(2,1)}, u32[]{:S(2)}) copy-start(bf16[1024,1024]{1,0:T(8,128)(2,1)} %grad_ref.7) | copy-start | bytes 6291460
  14.3 37.6 %collective-permute-start = (bf16[256,1024]{1,0:T(8,128)(2,1)S(1)}, bf16[256,1024]{1,0:T(8,128)(2,1)S(1)}, u32[]{:S(2)}, u32[]{:S(2)}) collective-permute-start(bf16[256,1024]{1,0:T(8,128)(2,1)S(1)} %get-tuple-element.45), channel_id=1, source_target_pairs={{0,2},{2,0},{4,6},{6,4},{8,10},{10,8},{12,14},{14,12},{16,18},{18,... | collective-permute-start | bytes 1572872 | tf_op jit(solution)/shard_map/ppermute | solution.py:549
  19.0 36.6 %collective-permute-start.5 = (bf16[256,1024]{1,0:T(8,128)(2,1)S(1)}, bf16[256,1024]{1,0:T(8,128)(2,1)S(1)}, u32[]{:S(2)}, u32[]{:S(2)}) collective-permute-start(bf16[256,1024]{1,0:T(8,128)(2,1)S(1)} %collective-permute-done.2.refs_0_), channel_id=1, source_target_pairs={{0,4},{4,8},{6,2},{8,12},{10,6},{12,16},{14,10},{16,20},{18,14},{2... | collective-permute-start | bytes 1572872 | tf_op jit(solution)/shard_map/ppermute | solution.py:555
  30.2 25.4 %collective-permute-start.6 = (bf16[256,1024]{1,0:T(8,128)(2,1)S(1)}, bf16[256,1024]{1,0:T(8,128)(2,1)S(1)}, u32[]{:S(2)}, u32[]{:S(2)}) collective-permute-start(bf16[256,1024]{1,0:T(8,128)(2,1)S(1)} %collective-permute-done.3.refs_1_), channel_id=1, source_target_pairs={{0,4},{4,8},{6,2},{8,12},{10,6},{12,16},{14,10},{16,20},{18,14},{2... | collective-permute-start | bytes 1572872 | tf_op jit(solution)/shard_map/ppermute | solution.py:555
  41.5 14.1 %collective-permute-start.7 = (bf16[256,1024]{1,0:T(8,128)(2,1)S(1)}, bf16[256,1024]{1,0:T(8,128)(2,1)S(1)}, u32[]{:S(2)}, u32[]{:S(2)}) collective-permute-start(bf16[256,1024]{1,0:T(8,128)(2,1)S(1)} %collective-permute-done.4.refs_2_), channel_id=1, source_target_pairs={{0,4},{4,8},{6,2},{8,12},{10,6},{12,16},{14,10},{16,20},{18,14},{2... | collective-permute-start | bytes 1572872 | tf_op jit(solution)/shard_map/ppermute | solution.py:555
  51.9 14.7 %collective-permute-start.1 = (bf16[256,1024]{1,0:T(8,128)(2,1)S(1)}, bf16[256,1024]{1,0:T(8,128)(2,1)S(1)}, u32[]{:S(2)}, u32[]{:S(2)}) collective-permute-start(bf16[256,1024]{1,0:T(8,128)(2,1)S(1)} %collective-permute-done.refs_3_), channel_id=1, source_target_pairs={{0,4},{4,8},{6,2},{8,12},{10,6},{12,16},{14,10},{16,20},{18,14},{2... | collective-permute-start | bytes 1572872 | tf_op jit(solution)/shard_map/ppermute | solution.py:555
  68.7 1.2 collective-permute-start.8
  71.8 16.6 %collective-permute-start.10 = (bf16[256,1024]{1,0:T(8,128)(2,1)S(1)}, bf16[256,1024]{1,0:T(8,128)(2,1)S(1)}, u32[]{:S(2)}, u32[]{:S(2)}) collective-permute-start(bf16[256,1024]{1,0:T(8,128)(2,1)S(1)} %get-tuple-element.54.refs_8_.refs_0_), channel_id=1, source_target_pairs={{0,2},{2,0},{4,6},{6,4},{8,10},{10,8},{12,14},{14,12},{16,18},{18,... | collective-permute-start | bytes 1572872 | tf_op jit(solution)/shard_map/ppermute | solution.py:549
  73.5 28.0 %collective-permute-start.11 = (bf16[256,1024]{1,0:T(8,128)(2,1)S(1)}, bf16[256,1024]{1,0:T(8,128)(2,1)S(1)}, u32[]{:S(2)}, u32[]{:S(2)}) collective-permute-start(bf16[256,1024]{1,0:T(8,128)(2,1)S(1)} %get-tuple-element.59.refs_9_.refs_1_), channel_id=1, source_target_pairs={{0,2},{2,0},{4,6},{6,4},{8,10},{10,8},{12,14},{14,12},{16,18},{18,... | collective-permute-start | bytes 1572872 | tf_op jit(solution)/shard_map/ppermute | solution.py:549
  73.8 35.2 %collective-permute-start.15 = (bf16[256,1024]{1,0:T(8,128)(2,1)S(1)}, bf16[256,1024]{1,0:T(8,128)(2,1)S(1)}, u32[]{:S(2)}, u32[]{:S(2)}) collective-permute-start(bf16[256,1024]{1,0:T(8,128)(2,1)S(1)} %get-tuple-element.65.refs_10_.refs_2_), channel_id=1, source_target_pairs={{0,2},{2,0},{4,6},{6,4},{8,10},{10,8},{12,14},{14,12},{16,18},{18,... | collective-permute-start | bytes 1572872 | tf_op jit(solution)/shard_map/ppermute | solution.py:549
  88.4 5.1 %collective-permute-start.13 = (f32[16,2176]{1,0:T(8,128)S(1)}, f32[16,2176]{1,0:T(8,128)S(1)}, u32[]{:S(2)}, u32[]{:S(2)}) collective-permute-start(f32[16,2176]{1,0:T(8,128)S(1)} %kernel_grad.1), channel_id=1, source_target_pairs={{0,8},{2,10},{4,12},{6,14},{8,0},{10,2},{12,4},{14,6},{16,24},{18,... | collective-permute-start | bytes 417800 | tf_op jit(solution)/shard_map/ppermute | solution.py:563
  93.5 8.0 %collective-permute-start.14 = (f32[16,2176]{1,0:T(8,128)S(1)}, f32[16,2176]{1,0:T(8,128)S(1)}, u32[]{:S(2)}, u32[]{:S(2)}) collective-permute-start(f32[16,2176]{1,0:T(8,128)S(1)} %add.23), channel_id=1, source_target_pairs={{0,16},{2,18},{4,20},{6,22},{8,24},{10,26},{12,28},{14,30},{16,0},... | collective-permute-start | bytes 417800 | tf_op jit(solution)/shard_map/ppermute | solution.py:563
  96.2 24.6 %collective-permute-start.9 = (bf16[256,1024]{1,0:T(8,128)(2,1)S(1)}, bf16[256,1024]{1,0:T(8,128)(2,1)S(1)}, u32[]{:S(2)}, u32[]{:S(2)}) collective-permute-start(bf16[256,1024]{1,0:T(8,128)(2,1)S(1)} %get-tuple-element.53.refs_11_.refs_3_), channel_id=1, source_target_pairs={{0,2},{2,0},{4,6},{6,4},{8,10},{10,8},{12,14},{14,12},{16,18},{18,... | collective-permute-start | bytes 1572872 | tf_op jit(solution)/shard_map/ppermute | solution.py:549
  97.6 27.1 %collective-permute-start.16 = (bf16[256,1024]{1,0:T(8,128)(2,1)S(1)}, bf16[256,1024]{1,0:T(8,128)(2,1)S(1)}, u32[]{:S(2)}, u32[]{:S(2)}) collective-permute-start(bf16[256,1024]{1,0:T(8,128)(2,1)S(1)} %collective-permute-done.10.refs_4_), channel_id=1, source_target_pairs={{0,4},{4,8},{6,2},{8,12},{10,6},{12,16},{14,10},{16,20},{18,14},{2... | collective-permute-start | bytes 1572872 | tf_op jit(solution)/shard_map/ppermute | solution.py:555
  101.5 23.2 %collective-permute-start.17 = (bf16[256,1024]{1,0:T(8,128)(2,1)S(1)}, bf16[256,1024]{1,0:T(8,128)(2,1)S(1)}, u32[]{:S(2)}, u32[]{:S(2)}) collective-permute-start(bf16[256,1024]{1,0:T(8,128)(2,1)S(1)} %collective-permute-done.11.refs_5_), channel_id=1, source_target_pairs={{0,4},{4,8},{6,2},{8,12},{10,6},{12,16},{14,10},{16,20},{18,14},{2... | collective-permute-start | bytes 1572872 | tf_op jit(solution)/shard_map/ppermute | solution.py:555
  109.1 29.4 %collective-permute-start.18 = (bf16[256,1024]{1,0:T(8,128)(2,1)S(1)}, bf16[256,1024]{1,0:T(8,128)(2,1)S(1)}, u32[]{:S(2)}, u32[]{:S(2)}) collective-permute-start(bf16[256,1024]{1,0:T(8,128)(2,1)S(1)} %collective-permute-done.15.refs_6_), channel_id=1, source_target_pairs={{0,4},{4,8},{6,2},{8,12},{10,6},{12,16},{14,10},{16,20},{18,14},{2... | collective-permute-start | bytes 1572872 | tf_op jit(solution)/shard_map/ppermute | solution.py:555
  120.7 28.1 %collective-permute-start.12 = (bf16[256,1024]{1,0:T(8,128)(2,1)S(1)}, bf16[256,1024]{1,0:T(8,128)(2,1)S(1)}, u32[]{:S(2)}, u32[]{:S(2)}) collective-permute-start(bf16[256,1024]{1,0:T(8,128)(2,1)S(1)} %collective-permute-done.9.refs_7_), channel_id=1, source_target_pairs={{0,4},{4,8},{6,2},{8,12},{10,6},{12,16},{14,10},{16,20},{18,14},{2... | collective-permute-start | bytes 1572872 | tf_op jit(solution)/shard_map/ppermute | solution.py:555
  124.7 26.6 %collective-permute-start.21 = (f32[16,2176]{1,0:T(8,128)S(1)}, f32[16,2176]{1,0:T(8,128)S(1)}, u32[]{:S(2)}, u32[]{:S(2)}) collective-permute-start(f32[16,2176]{1,0:T(8,128)S(1)} %add.24), channel_id=1, source_target_pairs={{0,6},{2,4},{4,2},{6,0},{8,14},{10,12},{12,10},{14,8},{16,22},{18,... | collective-permute-start | bytes 417800 | tf_op jit(solution)/shard_map/ppermute | solution.py:563
  130.1 21.3 %collective-permute-start.20 = (f32[16,2176]{1,0:T(8,128)S(1)}, f32[16,2176]{1,0:T(8,128)S(1)}, u32[]{:S(2)}, u32[]{:S(2)}) collective-permute-start(f32[16,2176]{1,0:T(8,128)S(1)} %add.24), channel_id=1, source_target_pairs={{0,4},{2,6},{4,0},{6,2},{8,12},{10,14},{12,8},{14,10},{16,20},{18,... | collective-permute-start | bytes 417800 | tf_op jit(solution)/shard_map/ppermute | solution.py:563
  130.1 21.3 %collective-permute-start.19 = (f32[16,2176]{1,0:T(8,128)S(1)}, f32[16,2176]{1,0:T(8,128)S(1)}, u32[]{:S(2)}, u32[]{:S(2)}) collective-permute-start(f32[16,2176]{1,0:T(8,128)S(1)} %add.24), channel_id=1, source_target_pairs={{0,2},{2,0},{4,6},{6,4},{8,10},{10,8},{12,14},{14,12},{16,18},{18,... | collective-permute-start | bytes 417800 | tf_op jit(solution)/shard_map/ppermute | solution.py:563
  (3 other events, 96.4 us)

commit v4 on v3

--- a/solution.py
+++ b/solution.py
@@ -114,25 +114,25 @@
     return [ref[at : at + TILE, slab(pair)] for at in range(0, ref.shape[0], TILE)]
 
 
-def layout_scratch(rows, lag):
+def layout_scratch(rows, lag, heads=2):
     wide = (rows + 2 * lag) // TILE * HEAD
     return [
-        pltpu.VMEM((2, TILE, wide), jnp.bfloat16),
-        pltpu.VMEM((2, TILE, wide - LANES), jnp.bfloat16),
+        pltpu.VMEM((heads, TILE, wide), jnp.bfloat16),
+        pltpu.VMEM((heads, TILE, wide - LANES), jnp.bfloat16),
     ]
 
 
-def lay_out(blocks, even_ref, odd_ref):
+def lay_out(blocks, even_ref, odd_ref, base=0):
     low = lane_iota(TILE) < HEAD
     turned = [pltpu.roll(block, HEAD, 1) for block in blocks]
     for tile in range(len(blocks) // 2):
         cols = slice(tile * LANES, (tile + 1) * LANES)
         first, second = 2 * tile, 2 * tile + 1
-        even_ref[0, :, cols] = jnp.where(low, blocks[first], turned[second])
-        even_ref[1, :, cols] = jnp.where(low, turned[first], blocks[second])
+        even_ref[base, :, cols] = jnp.where(low, blocks[first], turned[second])
+        even_ref[base + 1, :, cols] = jnp.where(low, turned[first], blocks[second])
         if odd_ref is not None and second + 1 < len(blocks):
-            odd_ref[0, :, cols] = jnp.where(low, blocks[second], turned[second + 1])
-            odd_ref[1, :, cols] = jnp.where(low, turned[second], blocks[second + 1])
+            odd_ref[base, :, cols] = jnp.where(low, blocks[second], turned[second + 1])
+            odd_ref[base + 1, :, cols] = jnp.where(low, turned[second], blocks[second + 1])
 
 
 def window(even_ref, odd_ref, head, start, width):
@@ -230,6 +230,7 @@
     near_refs, far_refs, refs = refs[:CHUNKS], refs[CHUNKS : 2 * CHUNKS - 1], refs[2 * CHUNKS - 1 :]
     mixed_ref, sums_ref, even_ref, odd_ref, square_ref, inner_ref = refs
     pair = pl.program_id(0)
+    heads = (2 * pair, 2 * pair + 1)
 
     @pl.when(pair == 0)
     def _():
@@ -237,12 +238,9 @@
         inner_ref[...] = jnp.zeros_like(inner_ref)
 
     blocks = extended(rows_of(own_ref, pair), at_pair(near_refs, pair), at_pair(far_refs, pair))
-    lay_out(blocks, even_ref, odd_ref)
+    lay_out(blocks, even_ref, odd_ref, 2 * pair)
     width = mixed_ref.shape[0] // TILE * HEAD
-    results = [
-        band_product(band_ref, 2 * pair + half, even_ref, odd_ref, half, slots, width)
-        for half in range(2)
-    ]
+    results = [band_product(band_ref, h, even_ref, odd_ref, h, slots, width) for h in heads]
     lanes = slab(pair)
     for index, mixed in enumerate(token_blocks(*results)):
         at = slice(index * TILE, (index + 1) * TILE)
@@ -264,14 +262,14 @@
         functools.partial(forward_body, slots),
         grid=(width // LANES,),
         in_specs=[VMEM] * len(operands),
-        out_specs=[VMEM] * 2,
+        out_specs=[VMEM] * 4,
         out_shape=[
             pltpu.VMEM((rows, width), jnp.float32),
             pltpu.VMEM((2, rows), jnp.float32),
+            *layout_scratch(rows, lag, width // HEAD),
         ],
-        scratch_shapes=layout_scratch(rows, lag)
-        + [pltpu.VMEM((rows, LANES), jnp.float32)] * 2,
-        compiler_params=params(10),
+        scratch_shapes=[pltpu.VMEM((rows, LANES), jnp.float32)] * 2,
+        compiler_params=params(9),
         cost_estimate=cost(product_flops(rows, width, lag), 16 * rows * width),
         name="forward",
     )(*operands)
@@ -407,12 +405,25 @@
     )(*operands)
 
 
-def kernel_grad_body(slots, gain_ref, own_ref, *refs):
-    near_refs, far_refs, refs = refs[:CHUNKS], refs[CHUNKS : 2 * CHUNKS], refs[2 * CHUNKS :]
-    mix_refs, (out_ref, even_ref, odd_ref, mix_even_ref, cells_ref) = refs[:CHUNKS], refs[CHUNKS:]
+def patched(even_ref, head, half, slot, slots, width, last):
+    data = even_ref[head, :, slot * HEAD : slot * HEAD + width]
+    low = lane_iota(TILE) < HEAD
+    turned = pltpu.roll(last, HEAD, 1)
+    if slot == 0:
+        tile = data[:, :LANES]
+        put = jnp.where(low, last if half == 0 else turned, tile)
+        return jnp.concatenate([jnp.where(odd_device(), tile, put), data[:, LANES:]], axis=1)
+    if slot == slots - 1:
+        tile = data[:, width - LANES :]
+        put = jnp.where(low, tile, turned if half == 0 else last)
+        return jnp.concatenate([data[:, : width - LANES], jnp.where(odd_device(), put, tile)], axis=1)
+    return data
+
+
+def kernel_grad_body(slots, gain_ref, even_ref, odd_ref, last_ref, *refs):
+    mix_refs, (out_ref, mix_even_ref, cells_ref) = refs[:CHUNKS], refs[CHUNKS:]
     pair = pl.program_id(0)
-    blocks = extended(rows_of(own_ref, pair), at_pair(near_refs, pair), at_pair(far_refs, pair))
-    lay_out(blocks, even_ref, odd_ref)
+    last = last_ref[:, slab(pair)]
     blocks = natural(at_pair(mix_refs, pair))
     lay_out(blocks, mix_even_ref, None)
     width = len(blocks) * HEAD
@@ -423,11 +434,12 @@
         mix = mix_even_ref[half].T
         carry = None
         for lag_slot in range(slots):
-            cross = jnp.dot(
-                window(even_ref, odd_ref, half, slots - 1 - lag_slot, width),
-                mix,
-                preferred_element_type=jnp.float32,
-            )
+            slot, head = slots - 1 - lag_slot, 2 * pair + half
+            if slot % 2 == 0:
+                data = patched(even_ref, head, half, slot, slots, width, last)
+            else:
+                data = window(even_ref, odd_ref, head, slot, width)
+            cross = jnp.dot(data, mix, preferred_element_type=jnp.float32)
             at = 2 * lag_slot * LANES
             upper, lower = cross[:LANES], cross[LANES:]
             if carry is not None:
@@ -454,23 +466,22 @@
         out_ref[group, :] = jnp.where(here, sums, out_ref[group, :])
 
 
-def kernel_grad_local(gain_sums, own, near, far, mix_grad, lag):
-    rows, width = own.shape
+def kernel_grad_local(gain_sums, even, odd, last, mix_grad, lag):
+    rows, width = len(mix_grad) * TILE, last.shape[1]
     pairs = width // LANES
     slots = 1 + 2 * lag // TILE
-    operands = held(gain_sums, own, *near, *far, *mix_grad)
+    operands = held(gain_sums, even, odd, last, *mix_grad)
     return pl.pallas_call(
         functools.partial(kernel_grad_body, slots),
         grid=(pairs,),
         in_specs=[VMEM] * len(operands),
         out_specs=VMEM,
         out_shape=pltpu.VMEM((2 * pairs, 2 * lag + LANES), jnp.float32),
-        scratch_shapes=layout_scratch(rows, lag)
-        + [
+        scratch_shapes=[
             pltpu.VMEM((2, TILE, rows // TILE * HEAD), jnp.bfloat16),
             pltpu.VMEM((LANES, 2 * lag + LANES), jnp.float32),
         ],
-        compiler_params=params(10),
+        compiler_params=params(8),
         cost_estimate=cost(product_flops(rows, width, lag), 8 * rows * width),
         name="kernel_grad",
     )(*operands)
@@ -591,14 +602,16 @@
     *chunks, last = split(value_acts)
     near = [swapped(chunk) for chunk in [*chunks, after(last, band)]]
     far = [relayed(chunk) for chunk in near]
-    mixed, sums = forward(band, value_acts, near, far[:-1], gate_acts, out_grad, gain, lag)
+    mixed, sums, even, odd = forward(
+        band, value_acts, near, far[:-1], gate_acts, out_grad, gain, lag
+    )
     first, sums = forward_last(band, far[-1], gate_acts, out_grad, gain, mixed, sums)
     sums = sum_over(sums, "chan")
     args = (mixed, first, gate_acts, out_grad, gain)
     mix_grad, gain_sums = mix_grad_of(full_width, sums, *args)
 
     grad_near = [swapped(part) for part in mix_grad]
-    totals = kernel_grad_local(gain_sums, value_acts, near, far, mix_grad, lag)
+    totals = kernel_grad_local(gain_sums, even, odd, far[-1], mix_grad, lag)
     normed, gate_grad = norm(full_width, after(sums, grad_near[0]), *args)
     back_band = bands(after(behind, grad_near[1]))
     grad_near[0], totals = lax.optimization_barrier((grad_near[0], totals))

time: 154 us -> 153 us (level)
  waiting for transfers between devices: 41.9 us -> 45 us
  Pallas kernels: 53.7 us -> 51 us
    pallas_call x1, Pallas kernels: 12.8 us -> 10.4 us  [kernel_grad_local(): pl.pallas_call(functools.partial(kernel_grad_body, slots), grid=(pairs,),...]
    ppermute x8, waiting for transfers between devices: 28.6 us -> 30.9 us  [swapped(): return lax.ppermute(chunk, 'seq', [(i, i ^ 1) for i in range(count)])]
    ppermute x8, waiting for transfers between devices: 7.89 us -> 9.84 us  [relayed(): lax.ppermute(chunk, 'seq', [(i, j) for i, j in pairs if 0 <= j < count])]
  transfers between devices with their start and end apart: 22 -> 22, of which waited for: 9 -> 9; matrix products, arithmetic and copies ran while one was open for 2% -> 2% of each run, Pallas kernels for 31% -> 29%
where the time goes in v4:
time: 153 us; the launch traced here: 152 us
  Pallas kernels  51 us (33%)
  starting transfers between devices  51 us (33%)
  waiting for transfers between devices  45 us (29%)
  local copies, waits for them, and re-layouts  3.71 us (2%)
    ppermute x8, starting transfers between devices, relayed(): lax.ppermute(chunk, 'seq', [(i, j) for i, j in pairs if 0 <= j < count])  31.5 us
    ppermute x8, waiting for transfers between devices, swapped(): return lax.ppermute(chunk, 'seq', [(i, i ^ 1) for i in range(count)])  30.9 us
    pallas_call x1, Pallas kernels, forward(): pl.pallas_call(functools.partial(forward_body, slots), grid=(width // LAN...  10.6 us
    pallas_call x1, Pallas kernels, kernel_grad_local(): pl.pallas_call(functools.partial(kernel_grad_body, slots), grid=(pairs,),...  10.4 us
    pallas_call x1, Pallas kernels, value_grad_of(): pl.pallas_call(functools.partial(value_grad_body, slots), grid=(width //...  10.3 us
    ppermute x8, waiting for transfers between devices, relayed(): lax.ppermute(chunk, 'seq', [(i, j) for i, j in pairs if 0 <= j < count])  9.84 us
    ppermute x8, starting transfers between devices, swapped(): return lax.ppermute(chunk, 'seq', [(i, i ^ 1) for i in range(count)])  9.81 us
    ppermute x5, starting transfers between devices, terms_over_bits(): lax.ppermute(value, 'seq', [(i, i ^ flip) for i in range(count)])  9.63 us
  transfers between devices with their start and end apart: 22, of which 9 were waited for; matrix products, arithmetic and copies ran while one was open for 2% of the time, Pallas kernels for 29%

profile of v4, /device:TPU:0, one launch (start us, length us, event | category | flops | bytes accessed | tf_op | source)
XLA Modules:
  0.0 152.4 jit_solution(13703153574358964810)
XLA Ops:
  3.0 3.0 %collective-permute-start.2 = (bf16[256,1024]{1,0:T(8,128)(2,1)}, bf16[256,1024]{1,0:T(8,128)(2,1)S(1)}, u32[]{:S(2)}, u32[]{:S(2)}) collective-permute-start(bf16[256,1024]{1,0:T(8,128)(2,1)} %get-tuple-element.48), channel_id=1, source_target_pairs={{0,2},{2,0},{4,6},{6,4},{8,10},{10,8},{12,14},{14,12},{16,18},{18,... | collective-permute-start | bytes 1572872 | tf_op jit(solution)/shard_map/ppermute | solution.py:560
  11.2 3.1 %bands.2.band_ref = bf16[16,128,2432]{2,1,0:T(8,128)(2,1)S(1)} custom-call(f32[8,2,2304]{2,1,0:T(2,128)S(1)} %reshape.22.row_ref), custom_call_target="tpu_custom_call" | custom-call | flops 4718592 | bytes 9437184 | tf_op jit(solution)/shard_map/bands/pallas_call | solution.py:84
  14.4 4.6 %collective-permute-done.2.refs_0_ = bf16[256,1024]{1,0:T(8,128)(2,1)S(1)} collective-permute-done((bf16[256,1024]{1,0:T(8,128)(2,1)}, bf16[256,1024]{1,0:T(8,128)(2,1)S(1)}, u32[]{:S(2)}, u32[]{:S(2)}) %collective-permute-start.2) | collective-permute-done | bytes 524320 | tf_op jit(solution)/shard_map/ppermute | solution.py:560
  19.0 4.0 %collective-permute-start.5 = (bf16[256,1024]{1,0:T(8,128)(2,1)S(1)}, bf16[256,1024]{1,0:T(8,128)(2,1)S(1)}, u32[]{:S(2)}, u32[]{:S(2)}) collective-permute-start(bf16[256,1024]{1,0:T(8,128)(2,1)S(1)} %collective-permute-done.2.refs_0_), channel_id=1, source_target_pairs={{0,4},{4,8},{6,2},{8,12},{10,6},{12,16},{14,10},{16,20},{18,14},{2... | collective-permute-start | bytes 1572872 | tf_op jit(solution)/shard_map/ppermute | solution.py:566
  23.0 7.2 %collective-permute-done.3.refs_1_ = bf16[256,1024]{1,0:T(8,128)(2,1)S(1)} collective-permute-done((bf16[256,1024]{1,0:T(8,128)(2,1)S(1)}, bf16[256,1024]{1,0:T(8,128)(2,1)S(1)}, u32[]{:S(2)}, u32[]{:S(2)}) %collective-permute-start.3) | collective-permute-done | bytes 524320 | tf_op jit(solution)/shard_map/ppermute | solution.py:560
  30.2 4.0 %collective-permute-start.6 = (bf16[256,1024]{1,0:T(8,128)(2,1)S(1)}, bf16[256,1024]{1,0:T(8,128)(2,1)S(1)}, u32[]{:S(2)}, u32[]{:S(2)}) collective-permute-start(bf16[256,1024]{1,0:T(8,128)(2,1)S(1)} %collective-permute-done.3.refs_1_), channel_id=1, source_target_pairs={{0,4},{4,8},{6,2},{8,12},{10,6},{12,16},{14,10},{16,20},{18,14},{2... | collective-permute-start | bytes 1572872 | tf_op jit(solution)/shard_map/ppermute | solution.py:566
  34.3 7.2 %collective-permute-done.4.refs_2_ = bf16[256,1024]{1,0:T(8,128)(2,1)S(1)} collective-permute-done((bf16[256,1024]{1,0:T(8,128)(2,1)S(1)}, bf16[256,1024]{1,0:T(8,128)(2,1)S(1)}, u32[]{:S(2)}, u32[]{:S(2)}) %collective-permute-start.4) | collective-permute-done | bytes 524320 | tf_op jit(solution)/shard_map/ppermute | solution.py:560
  41.5 4.0 %collective-permute-start.7 = (bf16[256,1024]{1,0:T(8,128)(2,1)S(1)}, bf16[256,1024]{1,0:T(8,128)(2,1)S(1)}, u32[]{:S(2)}, u32[]{:S(2)}) collective-permute-start(bf16[256,1024]{1,0:T(8,128)(2,1)S(1)} %collective-permute-done.4.refs_2_), channel_id=1, source_target_pairs={{0,4},{4,8},{6,2},{8,12},{10,6},{12,16},{14,10},{16,20},{18,14},{2... | collective-permute-start | bytes 1572872 | tf_op jit(solution)/shard_map/ppermute | solution.py:566
  45.5 6.4 %collective-permute-done.refs_3_ = bf16[256,1024]{1,0:T(8,128)(2,1)S(1)} collective-permute-done((bf16[256,1024]{1,0:T(8,128)(2,1)S(1)}, bf16[256,1024]{1,0:T(8,128)(2,1)S(1)}, u32[]{:S(2)}, u32[]{:S(2)}) %collective-permute-start) | collective-permute-done | bytes 524320 | tf_op jit(solution)/shard_map/ppermute | solution.py:560
  51.9 3.7 %collective-permute-start.1 = (bf16[256,1024]{1,0:T(8,128)(2,1)S(1)}, bf16[256,1024]{1,0:T(8,128)(2,1)S(1)}, u32[]{:S(2)}, u32[]{:S(2)}) collective-permute-start(bf16[256,1024]{1,0:T(8,128)(2,1)S(1)} %collective-permute-done.refs_3_), channel_id=1, source_target_pairs={{0,4},{4,8},{6,2},{8,12},{10,6},{12,16},{14,10},{16,20},{18,14},{2... | collective-permute-start | bytes 1572872 | tf_op jit(solution)/shard_map/ppermute | solution.py:566
  55.7 10.6 %forward.1 = (f32[1024,1024]{1,0:T(8,128)S(1)}, f32[2,1024]{1,0:T(2,128)S(1)}, bf16[16,256,768]{2,1,0:T(8,128)(2,1)S(1)}, bf16[16,256,640]{2,1,0:T(8,128)(2,1)S(1)}) custom-call(bf16[16,128,2432]{2,1,0:T(8,128)(2,1)S(1)} %bands.2.band_ref, bf16[1024,1024]{1,0:T(8,128)(2,1)S(1)} %copy-done.2, bf16[1024,1024]{1,0:T(8,128)(2,1)S(1)} %copy-done, ...), custom_call_target="tpu_custom_call" | custom-call | flops 4831838208 | bytes 16777216 | tf_op jit(solution)/shard_map/forward/pallas_call | solution.py:261
  75.5 10.4 %kernel_grad.1 = f32[16,2176]{1,0:T(8,128)S(1)} custom-call(f32[1,1024]{1,0:T(1,128)S(1)} %get-tuple-element.68.gain_ref, bf16[16,256,768]{2,1,0:T(8,128)(2,1)S(1)} %get-tuple-element.69.even_ref, bf16[16,256,640]{2,1,0:T(8,128)(2,1)S(1)} %get-tuple-element.70.odd_ref, bf16[256,1024]{1,0:T(8,128)(2,1)S(1)} %collective-permute-done.1.last_ref, ...), custom_call_target="tpu_custom_call" | custom-call | flops 4831838208 | bytes 8388608 | tf_op jit(solution)/shard_map/kernel_grad/pallas_call | solution.py:474
  86.3 3.0 %collective-permute-start.13 = (f32[16,2176]{1,0:T(8,128)S(1)}, f32[16,2176]{1,0:T(8,128)S(1)}, u32[]{:S(2)}, u32[]{:S(2)}) collective-permute-start(f32[16,2176]{1,0:T(8,128)S(1)} %kernel_grad.1), channel_id=1, source_target_pairs={{0,8},{2,10},{4,12},{6,14},{8,0},{10,2},{12,4},{14,6},{16,24},{18,... | collective-permute-start | bytes 417800 | tf_op jit(solution)/shard_map/ppermute | solution.py:574
  89.3 3.0 %collective-permute-done.13 = f32[16,2176]{1,0:T(8,128)S(1)} collective-permute-done((f32[16,2176]{1,0:T(8,128)S(1)}, f32[16,2176]{1,0:T(8,128)S(1)}, u32[]{:S(2)}, u32[]{:S(2)}) %collective-permute-start.13) | collective-permute-done | bytes 139296 | tf_op jit(solution)/shard_map/ppermute | solution.py:574
  92.3 3.1 %collective-permute-start.14 = (f32[16,2176]{1,0:T(8,128)S(1)}, f32[16,2176]{1,0:T(8,128)S(1)}, u32[]{:S(2)}, u32[]{:S(2)}) collective-permute-start(f32[16,2176]{1,0:T(8,128)S(1)} %add.23), channel_id=1, source_target_pairs={{0,16},{2,18},{4,20},{6,22},{8,24},{10,26},{12,28},{14,30},{16,0},... | collective-permute-start | bytes 417800 | tf_op jit(solution)/shard_map/ppermute | solution.py:574
  96.0 4.3 %collective-permute-start.16 = (bf16[256,1024]{1,0:T(8,128)(2,1)S(1)}, bf16[256,1024]{1,0:T(8,128)(2,1)S(1)}, u32[]{:S(2)}, u32[]{:S(2)}) collective-permute-start(bf16[256,1024]{1,0:T(8,128)(2,1)S(1)} %collective-permute-done.10.refs_4_), channel_id=1, source_target_pairs={{0,4},{4,8},{6,2},{8,12},{10,6},{12,16},{14,10},{16,20},{18,14},{2... | collective-permute-start | bytes 1572872 | tf_op jit(solution)/shard_map/ppermute | solution.py:566
  100.4 3.1 %collective-permute-start.17 = (bf16[256,1024]{1,0:T(8,128)(2,1)S(1)}, bf16[256,1024]{1,0:T(8,128)(2,1)S(1)}, u32[]{:S(2)}, u32[]{:S(2)}) collective-permute-start(bf16[256,1024]{1,0:T(8,128)(2,1)S(1)} %collective-permute-done.11.refs_5_), channel_id=1, source_target_pairs={{0,4},{4,8},{6,2},{8,12},{10,6},{12,16},{14,10},{16,20},{18,14},{2... | collective-permute-start | bytes 1572872 | tf_op jit(solution)/shard_map/ppermute | solution.py:566
  103.5 5.2 %collective-permute-done.15.refs_6_ = bf16[256,1024]{1,0:T(8,128)(2,1)S(1)} collective-permute-done((bf16[256,1024]{1,0:T(8,128)(2,1)S(1)}, bf16[256,1024]{1,0:T(8,128)(2,1)S(1)}, u32[]{:S(2)}, u32[]{:S(2)}) %collective-permute-start.15) | collective-permute-done | bytes 524320 | tf_op jit(solution)/shard_map/ppermute | solution.py:560
  108.7 4.3 %collective-permute-start.18 = (bf16[256,1024]{1,0:T(8,128)(2,1)S(1)}, bf16[256,1024]{1,0:T(8,128)(2,1)S(1)}, u32[]{:S(2)}, u32[]{:S(2)}) collective-permute-start(bf16[256,1024]{1,0:T(8,128)(2,1)S(1)} %collective-permute-done.15.refs_6_), channel_id=1, source_target_pairs={{0,4},{4,8},{6,2},{8,12},{10,6},{12,16},{14,10},{16,20},{18,14},{2... | collective-permute-start | bytes 1572872 | tf_op jit(solution)/shard_map/ppermute | solution.py:566
  113.0 3.1 %bands.3.band_ref = bf16[16,128,2432]{2,1,0:T(8,128)(2,1)S(1)} custom-call(f32[8,2,2304]{2,1,0:T(2,128)S(1)} %reshape.23.row_ref), custom_call_target="tpu_custom_call" | custom-call | flops 4718592 | bytes 9437184 | tf_op jit(solution)/shard_map/bands/pallas_call | solution.py:84
  116.1 4.6 %norm.1 = (bf16[1024,1024]{1,0:T(8,128)(2,1)}, bf16[1024,1024]{1,0:T(8,128)(2,1)}) custom-call(f32[2,1024]{1,0:T(2,128)S(1)} %add.22.sums_ref, f32[1024,1024]{1,0:T(8,128)S(1)} %get-tuple-element.51.mixed_ref, f32[256,1024]{1,0:T(8,128)S(1)} %get-tuple-element.54.first_ref, bf16[1024,1024]{1,0:T(8,128)(2,1)S(1)} %copy-done, ...), custom_call_target="tpu_custom_call" | custom-call | flops 14680064 | bytes 12582912 | tf_op jit(solution)/shard_map/norm/pallas_call | solution.py:396
  120.7 4.0 %collective-permute-start.12 = (bf16[256,1024]{1,0:T(8,128)(2,1)S(1)}, bf16[256,1024]{1,0:T(8,128)(2,1)S(1)}, u32[]{:S(2)}, u32[]{:S(2)}) collective-permute-start(bf16[256,1024]{1,0:T(8,128)(2,1)S(1)} %collective-permute-done.9.refs_7_), channel_id=1, source_target_pairs={{0,4},{4,8},{6,2},{8,12},{10,6},{12,16},{14,10},{16,20},{18,14},{2... | collective-permute-start | bytes 1572872 | tf_op jit(solution)/shard_map/ppermute | solution.py:566
  128.3 9.8 %collective-permute-done.18.refs_10_ = bf16[256,1024]{1,0:T(8,128)(2,1)S(1)} collective-permute-done((bf16[256,1024]{1,0:T(8,128)(2,1)S(1)}, bf16[256,1024]{1,0:T(8,128)(2,1)S(1)}, u32[]{:S(2)}, u32[]{:S(2)}) %collective-permute-start.18) | collective-permute-done | bytes 524320 | tf_op jit(solution)/shard_map/ppermute | solution.py:566
  138.1 10.3 %value_grad.1 = (bf16[1024,1024]{1,0:T(8,128)(2,1)}, f32[256,1024]{1,0:T(8,128)S(1)}) custom-call(bf16[16,128,2432]{2,1,0:T(8,128)(2,1)S(1)} %bands.3.band_ref, bf16[256,1024]{1,0:T(8,128)(2,1)S(1)} %get-tuple-element.56.refs_0_, bf16[256,1024]{1,0:T(8,128)(2,1)S(1)} %get-tuple-element.61.refs_1_, bf16[256,1024]{1,0:T(8,128)(2,1)S(1)} %get-tuple-element.67.refs_2_, ...), custom_call_target="tpu_custom_call" | custom-call | flops 4831838208 | bytes 12582912 | tf_op jit(solution)/shard_map/value_grad/pallas_call | solution.py:512
  (52 shorter events, 25.3 us)
Async XLA Ops:
  3.0 16.0 %collective-permute-start.2 = (bf16[256,1024]{1,0:T(8,128)(2,1)}, bf16[256,1024]{1,0:T(8,128)(2,1)S(1)}, u32[]{:S(2)}, u32[]{:S(2)}) collective-permute-start(bf16[256,1024]{1,0:T(8,128)(2,1)} %get-tuple-element.48), channel_id=1, source_target_pairs={{0,2},{2,0},{4,6},{6,4},{8,10},{10,8},{12,14},{14,12},{16,18},{18,... | collective-permute-start | bytes 1572872 | tf_op jit(solution)/shard_map/ppermute | solution.py:560
  6.0 24.2 %collective-permute-start.3 = (bf16[256,1024]{1,0:T(8,128)(2,1)S(1)}, bf16[256,1024]{1,0:T(8,128)(2,1)S(1)}, u32[]{:S(2)}, u32[]{:S(2)}) collective-permute-start(bf16[256,1024]{1,0:T(8,128)(2,1)S(1)} %get-tuple-element.49), channel_id=1, source_target_pairs={{0,2},{2,0},{4,6},{6,4},{8,10},{10,8},{12,14},{14,12},{16,18},{18,... | collective-permute-start | bytes 1572872 | tf_op jit(solution)/shard_map/ppermute | solution.py:560
  6.1 35.4 %collective-permute-start.4 = (bf16[256,1024]{1,0:T(8,128)(2,1)S(1)}, bf16[256,1024]{1,0:T(8,128)(2,1)S(1)}, u32[]{:S(2)}, u32[]{:S(2)}) collective-permute-start(bf16[256,1024]{1,0:T(8,128)(2,1)S(1)} %get-tuple-element.50), channel_id=1, source_target_pairs={{0,2},{2,0},{4,6},{6,4},{8,10},{10,8},{12,14},{14,12},{16,18},{18,... | collective-permute-start | bytes 1572872 | tf_op jit(solution)/shard_map/ppermute | solution.py:560
  11.1 44.5 %copy-start = (bf16[1024,1024]{1,0:T(8,128)(2,1)S(1)}, bf16[1024,1024]{1,0:T(8,128)(2,1)}, u32[]{:S(2)}) copy-start(bf16[1024,1024]{1,0:T(8,128)(2,1)} %gate_ref.7) | copy-start | bytes 6291460
  11.1 44.5 %copy-start.1 = (bf16[1024,1024]{1,0:T(8,128)(2,1)S(1)}, bf16[1024,1024]{1,0:T(8,128)(2,1)}, u32[]{:S(2)}) copy-start(bf16[1024,1024]{1,0:T(8,128)(2,1)} %grad_ref.7) | copy-start | bytes 6291460
  14.3 37.6 %collective-permute-start = (bf16[256,1024]{1,0:T(8,128)(2,1)S(1)}, bf16[256,1024]{1,0:T(8,128)(2,1)S(1)}, u32[]{:S(2)}, u32[]{:S(2)}) collective-permute-start(bf16[256,1024]{1,0:T(8,128)(2,1)S(1)} %get-tuple-element.47), channel_id=1, source_target_pairs={{0,2},{2,0},{4,6},{6,4},{8,10},{10,8},{12,14},{14,12},{16,18},{18,... | collective-permute-start | bytes 1572872 | tf_op jit(solution)/shard_map/ppermute | solution.py:560
  19.0 36.6 %collective-permute-start.5 = (bf16[256,1024]{1,0:T(8,128)(2,1)S(1)}, bf16[256,1024]{1,0:T(8,128)(2,1)S(1)}, u32[]{:S(2)}, u32[]{:S(2)}) collective-permute-start(bf16[256,1024]{1,0:T(8,128)(2,1)S(1)} %collective-permute-done.2.refs_0_), channel_id=1, source_target_pairs={{0,4},{4,8},{6,2},{8,12},{10,6},{12,16},{14,10},{16,20},{18,14},{2... | collective-permute-start | bytes 1572872 | tf_op jit(solution)/shard_map/ppermute | solution.py:566
  30.2 25.4 %collective-permute-start.6 = (bf16[256,1024]{1,0:T(8,128)(2,1)S(1)}, bf16[256,1024]{1,0:T(8,128)(2,1)S(1)}, u32[]{:S(2)}, u32[]{:S(2)}) collective-permute-start(bf16[256,1024]{1,0:T(8,128)(2,1)S(1)} %collective-permute-done.3.refs_1_), channel_id=1, source_target_pairs={{0,4},{4,8},{6,2},{8,12},{10,6},{12,16},{14,10},{16,20},{18,14},{2... | collective-permute-start | bytes 1572872 | tf_op jit(solution)/shard_map/ppermute | solution.py:566
  41.5 14.1 %collective-permute-start.7 = (bf16[256,1024]{1,0:T(8,128)(2,1)S(1)}, bf16[256,1024]{1,0:T(8,128)(2,1)S(1)}, u32[]{:S(2)}, u32[]{:S(2)}) collective-permute-start(bf16[256,1024]{1,0:T(8,128)(2,1)S(1)} %collective-permute-done.4.refs_2_), channel_id=1, source_target_pairs={{0,4},{4,8},{6,2},{8,12},{10,6},{12,16},{14,10},{16,20},{18,14},{2... | collective-permute-start | bytes 1572872 | tf_op jit(solution)/shard_map/ppermute | solution.py:566
  51.9 14.4 %collective-permute-start.1 = (bf16[256,1024]{1,0:T(8,128)(2,1)S(1)}, bf16[256,1024]{1,0:T(8,128)(2,1)S(1)}, u32[]{:S(2)}, u32[]{:S(2)}) collective-permute-start(bf16[256,1024]{1,0:T(8,128)(2,1)S(1)} %collective-permute-done.refs_3_), channel_id=1, source_target_pairs={{0,4},{4,8},{6,2},{8,12},{10,6},{12,16},{14,10},{16,20},{18,14},{2... | collective-permute-start | bytes 1572872 | tf_op jit(solution)/shard_map/ppermute | solution.py:566
  68.4 1.2 collective-permute-start.8
  71.5 14.8 %collective-permute-start.10 = (bf16[256,1024]{1,0:T(8,128)(2,1)S(1)}, bf16[256,1024]{1,0:T(8,128)(2,1)S(1)}, u32[]{:S(2)}, u32[]{:S(2)}) collective-permute-start(bf16[256,1024]{1,0:T(8,128)(2,1)S(1)} %get-tuple-element.56.refs_0_), channel_id=1, source_target_pairs={{0,2},{2,0},{4,6},{6,4},{8,10},{10,8},{12,14},{14,12},{16,18},{18,... | collective-permute-start | bytes 1572872 | tf_op jit(solution)/shard_map/ppermute | solution.py:560
  73.5 26.9 %collective-permute-start.11 = (bf16[256,1024]{1,0:T(8,128)(2,1)S(1)}, bf16[256,1024]{1,0:T(8,128)(2,1)S(1)}, u32[]{:S(2)}, u32[]{:S(2)}) collective-permute-start(bf16[256,1024]{1,0:T(8,128)(2,1)S(1)} %get-tuple-element.61.refs_1_), channel_id=1, source_target_pairs={{0,2},{2,0},{4,6},{6,4},{8,10},{10,8},{12,14},{14,12},{16,18},{18,... | collective-permute-start | bytes 1572872 | tf_op jit(solution)/shard_map/ppermute | solution.py:560
  73.6 35.2 %collective-permute-start.15 = (bf16[256,1024]{1,0:T(8,128)(2,1)S(1)}, bf16[256,1024]{1,0:T(8,128)(2,1)S(1)}, u32[]{:S(2)}, u32[]{:S(2)}) collective-permute-start(bf16[256,1024]{1,0:T(8,128)(2,1)S(1)} %get-tuple-element.67.refs_2_), channel_id=1, source_target_pairs={{0,2},{2,0},{4,6},{6,4},{8,10},{10,8},{12,14},{14,12},{16,18},{18,... | collective-permute-start | bytes 1572872 | tf_op jit(solution)/shard_map/ppermute | solution.py:560
  86.3 6.0 %collective-permute-start.13 = (f32[16,2176]{1,0:T(8,128)S(1)}, f32[16,2176]{1,0:T(8,128)S(1)}, u32[]{:S(2)}, u32[]{:S(2)}) collective-permute-start(f32[16,2176]{1,0:T(8,128)S(1)} %kernel_grad.1), channel_id=1, source_target_pairs={{0,8},{2,10},{4,12},{6,14},{8,0},{10,2},{12,4},{14,6},{16,24},{18,... | collective-permute-start | bytes 417800 | tf_op jit(solution)/shard_map/ppermute | solution.py:574
  92.3 8.0 %collective-permute-start.14 = (f32[16,2176]{1,0:T(8,128)S(1)}, f32[16,2176]{1,0:T(8,128)S(1)}, u32[]{:S(2)}, u32[]{:S(2)}) collective-permute-start(f32[16,2176]{1,0:T(8,128)S(1)} %add.23), channel_id=1, source_target_pairs={{0,16},{2,18},{4,20},{6,22},{8,24},{10,26},{12,28},{14,30},{16,0},... | collective-permute-start | bytes 417800 | tf_op jit(solution)/shard_map/ppermute | solution.py:574
  95.4 25.3 %collective-permute-start.9 = (bf16[256,1024]{1,0:T(8,128)(2,1)S(1)}, bf16[256,1024]{1,0:T(8,128)(2,1)S(1)}, u32[]{:S(2)}, u32[]{:S(2)}) collective-permute-start(bf16[256,1024]{1,0:T(8,128)(2,1)S(1)} %get-tuple-element.55.refs_3_), channel_id=1, source_target_pairs={{0,2},{2,0},{4,6},{6,4},{8,10},{10,8},{12,14},{14,12},{16,18},{18,... | collective-permute-start | bytes 1572872 | tf_op jit(solution)/shard_map/ppermute | solution.py:560
  96.0 28.7 %collective-permute-start.16 = (bf16[256,1024]{1,0:T(8,128)(2,1)S(1)}, bf16[256,1024]{1,0:T(8,128)(2,1)S(1)}, u32[]{:S(2)}, u32[]{:S(2)}) collective-permute-start(bf16[256,1024]{1,0:T(8,128)(2,1)S(1)} %collective-permute-done.10.refs_4_), channel_id=1, source_target_pairs={{0,4},{4,8},{6,2},{8,12},{10,6},{12,16},{14,10},{16,20},{18,14},{2... | collective-permute-start | bytes 1572872 | tf_op jit(solution)/shard_map/ppermute | solution.py:566
  100.4 24.4 %collective-permute-start.17 = (bf16[256,1024]{1,0:T(8,128)(2,1)S(1)}, bf16[256,1024]{1,0:T(8,128)(2,1)S(1)}, u32[]{:S(2)}, u32[]{:S(2)}) collective-permute-start(bf16[256,1024]{1,0:T(8,128)(2,1)S(1)} %collective-permute-done.11.refs_5_), channel_id=1, source_target_pairs={{0,4},{4,8},{6,2},{8,12},{10,6},{12,16},{14,10},{16,20},{18,14},{2... | collective-permute-start | bytes 1572872 | tf_op jit(solution)/shard_map/ppermute | solution.py:566
  108.7 29.4 %collective-permute-start.18 = (bf16[256,1024]{1,0:T(8,128)(2,1)S(1)}, bf16[256,1024]{1,0:T(8,128)(2,1)S(1)}, u32[]{:S(2)}, u32[]{:S(2)}) collective-permute-start(bf16[256,1024]{1,0:T(8,128)(2,1)S(1)} %collective-permute-done.15.refs_6_), channel_id=1, source_target_pairs={{0,4},{4,8},{6,2},{8,12},{10,6},{12,16},{14,10},{16,20},{18,14},{2... | collective-permute-start | bytes 1572872 | tf_op jit(solution)/shard_map/ppermute | solution.py:566
  120.7 27.7 %collective-permute-start.12 = (bf16[256,1024]{1,0:T(8,128)(2,1)S(1)}, bf16[256,1024]{1,0:T(8,128)(2,1)S(1)}, u32[]{:S(2)}, u32[]{:S(2)}) collective-permute-start(bf16[256,1024]{1,0:T(8,128)(2,1)S(1)} %collective-permute-done.9.refs_7_), channel_id=1, source_target_pairs={{0,4},{4,8},{6,2},{8,12},{10,6},{12,16},{14,10},{16,20},{18,14},{2... | collective-permute-start | bytes 1572872 | tf_op jit(solution)/shard_map/ppermute | solution.py:566
  124.8 26.3 %collective-permute-start.19 = (f32[16,2176]{1,0:T(8,128)S(1)}, f32[16,2176]{1,0:T(8,128)S(1)}, u32[]{:S(2)}, u32[]{:S(2)}) collective-permute-start(f32[16,2176]{1,0:T(8,128)S(1)} %add.24), channel_id=1, source_target_pairs={{0,2},{2,0},{4,6},{6,4},{8,10},{10,8},{12,14},{14,12},{16,18},{18,... | collective-permute-start | bytes 417800 | tf_op jit(solution)/shard_map/ppermute | solution.py:574
  125.4 25.6 %collective-permute-start.20 = (f32[16,2176]{1,0:T(8,128)S(1)}, f32[16,2176]{1,0:T(8,128)S(1)}, u32[]{:S(2)}, u32[]{:S(2)}) collective-permute-start(f32[16,2176]{1,0:T(8,128)S(1)} %add.24), channel_id=1, source_target_pairs={{0,4},{2,6},{4,0},{6,2},{8,12},{10,14},{12,8},{14,10},{16,20},{18,... | collective-permute-start | bytes 417800 | tf_op jit(solution)/shard_map/ppermute | solution.py:574
  127.3 23.7 %collective-permute-start.21 = (f32[16,2176]{1,0:T(8,128)S(1)}, f32[16,2176]{1,0:T(8,128)S(1)}, u32[]{:S(2)}, u32[]{:S(2)}) collective-permute-start(f32[16,2176]{1,0:T(8,128)S(1)} %add.24), channel_id=1, source_target_pairs={{0,6},{2,4},{4,2},{6,0},{8,14},{10,12},{12,10},{14,8},{16,22},{18,... | collective-permute-start | bytes 417800 | tf_op jit(solution)/shard_map/ppermute | solution.py:574
  (3 other events, 96.4 us)

commit v5 on v4

--- a/solution.py
+++ b/solution.py
@@ -619,13 +619,16 @@
         (grad_near[3], normed, gate_grad, back_band)
     )
     bits = list(range(count.bit_length() - 1))
-    for bit in bits[2:]:
+    totals += terms_over_bits(totals, bits[2:3])[0]
+    for chunk in (1, 2):
+        grad_near[chunk], totals = lax.optimization_barrier((grad_near[chunk], totals))
+    for bit in bits[3:]:
         totals += terms_over_bits(totals, [bit])[0]
-    grad_near[1], totals = lax.optimization_barrier((grad_near[1], totals))
     grad_far = [relayed(chunk) for chunk in grad_near]
     totals, *grad_far[:2] = lax.optimization_barrier((totals, *grad_far[:2]))
+    value_grad, first = value_grad_of(back_band, mix_grad, grad_near, grad_far[:-1], lag)
+    totals, first = lax.optimization_barrier((totals, first))
     terms = [totals] + terms_over_bits(totals, bits[:2])
-    value_grad, first = value_grad_of(back_band, mix_grad, grad_near, grad_far[:-1], lag)
     value_grad = value_grad_last(back_band, grad_far[-1], first, value_grad)
     value_grad, *terms = lax.optimization_barrier((value_grad, *terms))
     totals = sum(terms[1:], terms[0])

time: 153 us -> 155 us (1.013)
  starting transfers between devices: 51 us -> 58.5 us
  waiting for transfers between devices: 45 us -> 39.6 us
    ppermute x8, waiting for transfers between devices: 9.84 us -> 0.02 us  [relayed(): lax.ppermute(chunk, 'seq', [(i, j) for i, j in pairs if 0 <= j < count])]
    ppermute x5, starting transfers between devices: 9.63 us -> 16 us  [terms_over_bits(): lax.ppermute(value, 'seq', [(i, i ^ flip) for i in range(count)])]
    ppermute x8, waiting for transfers between devices: 30.9 us -> 35.9 us  [swapped(): return lax.ppermute(chunk, 'seq', [(i, i ^ 1) for i in range(count)])]
where the time goes in v5:
time: 155 us
  starting transfers between devices  58.5 us (38%)
  Pallas kernels  51.1 us (33%)
  waiting for transfers between devices  39.6 us (26%)
  local copies, waits for them, and re-layouts  3.71 us (2%)
    ppermute x8, waiting for transfers between devices, swapped(): return lax.ppermute(chunk, 'seq', [(i, i ^ 1) for i in range(count)])  35.9 us
    ppermute x8, starting transfers between devices, relayed(): lax.ppermute(chunk, 'seq', [(i, j) for i, j in pairs if 0 <= j < count])  32.6 us
    ppermute x5, starting transfers between devices, terms_over_bits(): lax.ppermute(value, 'seq', [(i, i ^ flip) for i in range(count)])  16 us
    pallas_call x1, Pallas kernels, forward(): pl.pallas_call(functools.partial(forward_body, slots), grid=(width // LAN...  10.6 us
    pallas_call x1, Pallas kernels, kernel_grad_local(): pl.pallas_call(functools.partial(kernel_grad_body, slots), grid=(pairs,),...  10.4 us
    pallas_call x1, Pallas kernels, value_grad_of(): pl.pallas_call(functools.partial(value_grad_body, slots), grid=(width //...  10.3 us
    ppermute x8, starting transfers between devices, swapped(): return lax.ppermute(chunk, 'seq', [(i, i ^ 1) for i in range(count)])  9.81 us
    pallas_call x2, Pallas kernels, bands(): pl.pallas_call(band_body, grid=(heads // 2,), in_specs=[VMEM], out_specs=...  6.2 us
  transfers between devices with their start and end apart: 22, of which 9 were waited for; matrix products, arithmetic and copies ran while one was open for 2% of the time, Pallas kernels for 29%

profile of v5, /device:TPU:0, one launch (start us, length us, event | category | flops | bytes accessed | tf_op | source)
XLA Modules:
  0.0 154.6 jit_solution(12174863228943421344)
XLA Ops:
  3.0 3.0 %collective-permute-start.2 = (bf16[256,1024]{1,0:T(8,128)(2,1)}, bf16[256,1024]{1,0:T(8,128)(2,1)S(1)}, u32[]{:S(2)}, u32[]{:S(2)}) collective-permute-start(bf16[256,1024]{1,0:T(8,128)(2,1)} %get-tuple-element.52), channel_id=1, source_target_pairs={{0,2},{2,0},{4,6},{6,4},{8,10},{10,8},{12,14},{14,12},{16,18},{18,... | collective-permute-start | bytes 1572872 | tf_op jit(solution)/shard_map/ppermute | solution.py:560
  11.2 3.1 %bands.2.band_ref = bf16[16,128,2432]{2,1,0:T(8,128)(2,1)S(1)} custom-call(f32[8,2,2304]{2,1,0:T(2,128)S(1)} %reshape.22.row_ref), custom_call_target="tpu_custom_call" | custom-call | flops 4718592 | bytes 9437184 | tf_op jit(solution)/shard_map/bands/pallas_call | solution.py:84
  14.4 4.6 %collective-permute-done.2.refs_0_ = bf16[256,1024]{1,0:T(8,128)(2,1)S(1)} collective-permute-done((bf16[256,1024]{1,0:T(8,128)(2,1)}, bf16[256,1024]{1,0:T(8,128)(2,1)S(1)}, u32[]{:S(2)}, u32[]{:S(2)}) %collective-permute-start.2) | collective-permute-done | bytes 524320 | tf_op jit(solution)/shard_map/ppermute | solution.py:560
  19.0 4.0 %collective-permute-start.5 = (bf16[256,1024]{1,0:T(8,128)(2,1)S(1)}, bf16[256,1024]{1,0:T(8,128)(2,1)S(1)}, u32[]{:S(2)}, u32[]{:S(2)}) collective-permute-start(bf16[256,1024]{1,0:T(8,128)(2,1)S(1)} %collective-permute-done.2.refs_0_), channel_id=1, source_target_pairs={{0,4},{4,8},{6,2},{8,12},{10,6},{12,16},{14,10},{16,20},{18,14},{2... | collective-permute-start | bytes 1572872 | tf_op jit(solution)/shard_map/ppermute | solution.py:566
  23.0 7.2 %collective-permute-done.3.refs_1_ = bf16[256,1024]{1,0:T(8,128)(2,1)S(1)} collective-permute-done((bf16[256,1024]{1,0:T(8,128)(2,1)S(1)}, bf16[256,1024]{1,0:T(8,128)(2,1)S(1)}, u32[]{:S(2)}, u32[]{:S(2)}) %collective-permute-start.3) | collective-permute-done | bytes 524320 | tf_op jit(solution)/shard_map/ppermute | solution.py:560
  30.2 4.0 %collective-permute-start.6 = (bf16[256,1024]{1,0:T(8,128)(2,1)S(1)}, bf16[256,1024]{1,0:T(8,128)(2,1)S(1)}, u32[]{:S(2)}, u32[]{:S(2)}) collective-permute-start(bf16[256,1024]{1,0:T(8,128)(2,1)S(1)} %collective-permute-done.3.refs_1_), channel_id=1, source_target_pairs={{0,4},{4,8},{6,2},{8,12},{10,6},{12,16},{14,10},{16,20},{18,14},{2... | collective-permute-start | bytes 1572872 | tf_op jit(solution)/shard_map/ppermute | solution.py:566
  34.3 7.2 %collective-permute-done.4.refs_2_ = bf16[256,1024]{1,0:T(8,128)(2,1)S(1)} collective-permute-done((bf16[256,1024]{1,0:T(8,128)(2,1)S(1)}, bf16[256,1024]{1,0:T(8,128)(2,1)S(1)}, u32[]{:S(2)}, u32[]{:S(2)}) %collective-permute-start.4) | collective-permute-done | bytes 524320 | tf_op jit(solution)/shard_map/ppermute | solution.py:560
  41.5 4.0 %collective-permute-start.7 = (bf16[256,1024]{1,0:T(8,128)(2,1)S(1)}, bf16[256,1024]{1,0:T(8,128)(2,1)S(1)}, u32[]{:S(2)}, u32[]{:S(2)}) collective-permute-start(bf16[256,1024]{1,0:T(8,128)(2,1)S(1)} %collective-permute-done.4.refs_2_), channel_id=1, source_target_pairs={{0,4},{4,8},{6,2},{8,12},{10,6},{12,16},{14,10},{16,20},{18,14},{2... | collective-permute-start | bytes 1572872 | tf_op jit(solution)/shard_map/ppermute | solution.py:566
  45.5 6.4 %collective-permute-done.refs_3_ = bf16[256,1024]{1,0:T(8,128)(2,1)S(1)} collective-permute-done((bf16[256,1024]{1,0:T(8,128)(2,1)S(1)}, bf16[256,1024]{1,0:T(8,128)(2,1)S(1)}, u32[]{:S(2)}, u32[]{:S(2)}) %collective-permute-start) | collective-permute-done | bytes 524320 | tf_op jit(solution)/shard_map/ppermute | solution.py:560
  51.9 3.7 %collective-permute-start.1 = (bf16[256,1024]{1,0:T(8,128)(2,1)S(1)}, bf16[256,1024]{1,0:T(8,128)(2,1)S(1)}, u32[]{:S(2)}, u32[]{:S(2)}) collective-permute-start(bf16[256,1024]{1,0:T(8,128)(2,1)S(1)} %collective-permute-done.refs_3_), channel_id=1, source_target_pairs={{0,4},{4,8},{6,2},{8,12},{10,6},{12,16},{14,10},{16,20},{18,14},{2... | collective-permute-start | bytes 1572872 | tf_op jit(solution)/shard_map/ppermute | solution.py:566
  55.7 10.6 %forward.1 = (f32[1024,1024]{1,0:T(8,128)S(1)}, f32[2,1024]{1,0:T(2,128)S(1)}, bf16[16,256,768]{2,1,0:T(8,128)(2,1)S(1)}, bf16[16,256,640]{2,1,0:T(8,128)(2,1)S(1)}) custom-call(bf16[16,128,2432]{2,1,0:T(8,128)(2,1)S(1)} %bands.2.band_ref, bf16[1024,1024]{1,0:T(8,128)(2,1)S(1)} %copy-done.2, bf16[1024,1024]{1,0:T(8,128)(2,1)S(1)} %copy-done, ...), custom_call_target="tpu_custom_call" | custom-call | flops 4831838208 | bytes 16777216 | tf_op jit(solution)/shard_map/forward/pallas_call | solution.py:261
  75.5 10.4 %kernel_grad.1 = f32[16,2176]{1,0:T(8,128)S(1)} custom-call(f32[1,1024]{1,0:T(1,128)S(1)} %get-tuple-element.72.gain_ref, bf16[16,256,768]{2,1,0:T(8,128)(2,1)S(1)} %get-tuple-element.73.even_ref, bf16[16,256,640]{2,1,0:T(8,128)(2,1)S(1)} %get-tuple-element.74.odd_ref, bf16[256,1024]{1,0:T(8,128)(2,1)S(1)} %collective-permute-done.1.last_ref, ...), custom_call_target="tpu_custom_call" | custom-call | flops 4831838208 | bytes 8388608 | tf_op jit(solution)/shard_map/kernel_grad/pallas_call | solution.py:474
  86.3 3.0 %collective-permute-start.14 = (f32[16,2176]{1,0:T(8,128)S(1)}, f32[16,2176]{1,0:T(8,128)S(1)}, u32[]{:S(2)}, u32[]{:S(2)}) collective-permute-start(f32[16,2176]{1,0:T(8,128)S(1)} %kernel_grad.1), channel_id=1, source_target_pairs={{0,8},{2,10},{4,12},{6,14},{8,0},{10,2},{12,4},{14,6},{16,24},{18,... | collective-permute-start | bytes 417800 | tf_op jit(solution)/shard_map/ppermute | solution.py:574
  89.8 4.3 %collective-permute-start.16 = (bf16[256,1024]{1,0:T(8,128)(2,1)S(1)}, bf16[256,1024]{1,0:T(8,128)(2,1)S(1)}, u32[]{:S(2)}, u32[]{:S(2)}) collective-permute-start(bf16[256,1024]{1,0:T(8,128)(2,1)S(1)} %collective-permute-done.10.refs_4_), channel_id=1, source_target_pairs={{0,4},{4,8},{6,2},{8,12},{10,6},{12,16},{14,10},{16,20},{18,14},{2... | collective-permute-start | bytes 1572872 | tf_op jit(solution)/shard_map/ppermute | solution.py:566
  94.2 3.3 %collective-permute-done.11.refs_5_ = bf16[256,1024]{1,0:T(8,128)(2,1)S(1)} collective-permute-done((bf16[256,1024]{1,0:T(8,128)(2,1)S(1)}, bf16[256,1024]{1,0:T(8,128)(2,1)S(1)}, u32[]{:S(2)}, u32[]{:S(2)}) %collective-permute-start.11) | collective-permute-done | bytes 524320 | tf_op jit(solution)/shard_map/ppermute | solution.py:560
  97.5 4.3 %collective-permute-start.17 = (bf16[256,1024]{1,0:T(8,128)(2,1)S(1)}, bf16[256,1024]{1,0:T(8,128)(2,1)S(1)}, u32[]{:S(2)}, u32[]{:S(2)}) collective-permute-start(bf16[256,1024]{1,0:T(8,128)(2,1)S(1)} %collective-permute-done.11.refs_5_), channel_id=1, source_target_pairs={{0,4},{4,8},{6,2},{8,12},{10,6},{12,16},{14,10},{16,20},{18,14},{2... | collective-permute-start | bytes 1572872 | tf_op jit(solution)/shard_map/ppermute | solution.py:566
  101.8 7.0 %collective-permute-done.13.refs_6_ = bf16[256,1024]{1,0:T(8,128)(2,1)S(1)} collective-permute-done((bf16[256,1024]{1,0:T(8,128)(2,1)S(1)}, bf16[256,1024]{1,0:T(8,128)(2,1)S(1)}, u32[]{:S(2)}, u32[]{:S(2)}) %collective-permute-start.13) | collective-permute-done | bytes 524320 | tf_op jit(solution)/shard_map/ppermute | solution.py:560
  108.7 4.3 %collective-permute-start.18 = (bf16[256,1024]{1,0:T(8,128)(2,1)S(1)}, bf16[256,1024]{1,0:T(8,128)(2,1)S(1)}, u32[]{:S(2)}, u32[]{:S(2)}) collective-permute-start(bf16[256,1024]{1,0:T(8,128)(2,1)S(1)} %collective-permute-done.13.refs_6_), channel_id=1, source_target_pairs={{0,4},{4,8},{6,2},{8,12},{10,6},{12,16},{14,10},{16,20},{18,14},{2... | collective-permute-start | bytes 1572872 | tf_op jit(solution)/shard_map/ppermute | solution.py:566
  113.0 2.6 %collective-permute-start.15 = (f32[16,2176]{1,0:T(8,128)S(1)}, f32[16,2176]{1,0:T(8,128)S(1)}, u32[]{:S(2)}, u32[]{:S(2)}) collective-permute-start(f32[16,2176]{1,0:T(8,128)S(1)} %add.23), channel_id=1, source_target_pairs={{0,16},{2,18},{4,20},{6,22},{8,24},{10,26},{12,28},{14,30},{16,0},... | collective-permute-start | bytes 417800 | tf_op jit(solution)/shard_map/ppermute | solution.py:574
  115.7 3.1 %bands.3.band_ref = bf16[16,128,2432]{2,1,0:T(8,128)(2,1)S(1)} custom-call(f32[8,2,2304]{2,1,0:T(2,128)S(1)} %reshape.23.row_ref), custom_call_target="tpu_custom_call" | custom-call | flops 4718592 | bytes 9437184 | tf_op jit(solution)/shard_map/bands/pallas_call | solution.py:84
  118.8 4.6 %norm.1 = (bf16[1024,1024]{1,0:T(8,128)(2,1)}, bf16[1024,1024]{1,0:T(8,128)(2,1)}) custom-call(f32[2,1024]{1,0:T(2,128)S(1)} %add.22.sums_ref, f32[1024,1024]{1,0:T(8,128)S(1)} %get-tuple-element.55.mixed_ref, f32[256,1024]{1,0:T(8,128)S(1)} %get-tuple-element.58.first_ref, bf16[1024,1024]{1,0:T(8,128)(2,1)S(1)} %copy-done, ...), custom_call_target="tpu_custom_call" | custom-call | flops 14680064 | bytes 12582912 | tf_op jit(solution)/shard_map/norm/pallas_call | solution.py:396
  123.4 4.0 %collective-permute-start.12 = (bf16[256,1024]{1,0:T(8,128)(2,1)S(1)}, bf16[256,1024]{1,0:T(8,128)(2,1)S(1)}, u32[]{:S(2)}, u32[]{:S(2)}) collective-permute-start(bf16[256,1024]{1,0:T(8,128)(2,1)S(1)} %collective-permute-done.9.refs_7_), channel_id=1, source_target_pairs={{0,4},{4,8},{6,2},{8,12},{10,6},{12,16},{14,10},{16,20},{18,14},{2... | collective-permute-start | bytes 1572872 | tf_op jit(solution)/shard_map/ppermute | solution.py:566
  127.4 10.3 %value_grad.1 = (bf16[1024,1024]{1,0:T(8,128)(2,1)}, f32[256,1024]{1,0:T(8,128)S(1)}) custom-call(bf16[16,128,2432]{2,1,0:T(8,128)(2,1)S(1)} %bands.3.band_ref, bf16[256,1024]{1,0:T(8,128)(2,1)S(1)} %get-tuple-element.60.refs_0_, bf16[256,1024]{1,0:T(8,128)(2,1)S(1)} %get-tuple-element.65.refs_1_, bf16[256,1024]{1,0:T(8,128)(2,1)S(1)} %get-tuple-element.71.refs_2_, ...), custom_call_target="tpu_custom_call" | custom-call | flops 4831838208 | bytes 12582912 | tf_op jit(solution)/shard_map/value_grad/pallas_call | solution.py:512
  137.8 8.9 %collective-permute-start.19 = (f32[16,2176]{1,0:T(8,128)S(1)}, f32[16,2176]{1,0:T(8,128)S(1)}, u32[]{:S(2)}, u32[]{:S(2)}) collective-permute-start(f32[16,2176]{1,0:T(8,128)S(1)} %add.24), channel_id=1, source_target_pairs={{0,2},{2,0},{4,6},{6,4},{8,10},{10,8},{12,14},{14,12},{16,18},{18,... | collective-permute-start | bytes 417800 | tf_op jit(solution)/shard_map/ppermute | solution.py:574
  (52 shorter events, 25.6 us)
Async XLA Ops:
  3.0 16.0 %collective-permute-start.2 = (bf16[256,1024]{1,0:T(8,128)(2,1)}, bf16[256,1024]{1,0:T(8,128)(2,1)S(1)}, u32[]{:S(2)}, u32[]{:S(2)}) collective-permute-start(bf16[256,1024]{1,0:T(8,128)(2,1)} %get-tuple-element.52), channel_id=1, source_target_pairs={{0,2},{2,0},{4,6},{6,4},{8,10},{10,8},{12,14},{14,12},{16,18},{18,... | collective-permute-start | bytes 1572872 | tf_op jit(solution)/shard_map/ppermute | solution.py:560
  6.0 24.2 %collective-permute-start.3 = (bf16[256,1024]{1,0:T(8,128)(2,1)S(1)}, bf16[256,1024]{1,0:T(8,128)(2,1)S(1)}, u32[]{:S(2)}, u32[]{:S(2)}) collective-permute-start(bf16[256,1024]{1,0:T(8,128)(2,1)S(1)} %get-tuple-element.53), channel_id=1, source_target_pairs={{0,2},{2,0},{4,6},{6,4},{8,10},{10,8},{12,14},{14,12},{16,18},{18,... | collective-permute-start | bytes 1572872 | tf_op jit(solution)/shard_map/ppermute | solution.py:560
  6.1 35.4 %collective-permute-start.4 = (bf16[256,1024]{1,0:T(8,128)(2,1)S(1)}, bf16[256,1024]{1,0:T(8,128)(2,1)S(1)}, u32[]{:S(2)}, u32[]{:S(2)}) collective-permute-start(bf16[256,1024]{1,0:T(8,128)(2,1)S(1)} %get-tuple-element.54), channel_id=1, source_target_pairs={{0,2},{2,0},{4,6},{6,4},{8,10},{10,8},{12,14},{14,12},{16,18},{18,... | collective-permute-start | bytes 1572872 | tf_op jit(solution)/shard_map/ppermute | solution.py:560
  11.1 44.5 %copy-start = (bf16[1024,1024]{1,0:T(8,128)(2,1)S(1)}, bf16[1024,1024]{1,0:T(8,128)(2,1)}, u32[]{:S(2)}) copy-start(bf16[1024,1024]{1,0:T(8,128)(2,1)} %gate_ref.7) | copy-start | bytes 6291460
  11.1 44.5 %copy-start.1 = (bf16[1024,1024]{1,0:T(8,128)(2,1)S(1)}, bf16[1024,1024]{1,0:T(8,128)(2,1)}, u32[]{:S(2)}) copy-start(bf16[1024,1024]{1,0:T(8,128)(2,1)} %grad_ref.7) | copy-start | bytes 6291460
  14.3 37.6 %collective-permute-start = (bf16[256,1024]{1,0:T(8,128)(2,1)S(1)}, bf16[256,1024]{1,0:T(8,128)(2,1)S(1)}, u32[]{:S(2)}, u32[]{:S(2)}) collective-permute-start(bf16[256,1024]{1,0:T(8,128)(2,1)S(1)} %get-tuple-element.51), channel_id=1, source_target_pairs={{0,2},{2,0},{4,6},{6,4},{8,10},{10,8},{12,14},{14,12},{16,18},{18,... | collective-permute-start | bytes 1572872 | tf_op jit(solution)/shard_map/ppermute | solution.py:560
  19.0 36.6 %collective-permute-start.5 = (bf16[256,1024]{1,0:T(8,128)(2,1)S(1)}, bf16[256,1024]{1,0:T(8,128)(2,1)S(1)}, u32[]{:S(2)}, u32[]{:S(2)}) collective-permute-start(bf16[256,1024]{1,0:T(8,128)(2,1)S(1)} %collective-permute-done.2.refs_0_), channel_id=1, source_target_pairs={{0,4},{4,8},{6,2},{8,12},{10,6},{12,16},{14,10},{16,20},{18,14},{2... | collective-permute-start | bytes 1572872 | tf_op jit(solution)/shard_map/ppermute | solution.py:566
  30.2 25.4 %collective-permute-start.6 = (bf16[256,1024]{1,0:T(8,128)(2,1)S(1)}, bf16[256,1024]{1,0:T(8,128)(2,1)S(1)}, u32[]{:S(2)}, u32[]{:S(2)}) collective-permute-start(bf16[256,1024]{1,0:T(8,128)(2,1)S(1)} %collective-permute-done.3.refs_1_), channel_id=1, source_target_pairs={{0,4},{4,8},{6,2},{8,12},{10,6},{12,16},{14,10},{16,20},{18,14},{2... | collective-permute-start | bytes 1572872 | tf_op jit(solution)/shard_map/ppermute | solution.py:566
  41.5 14.1 %collective-permute-start.7 = (bf16[256,1024]{1,0:T(8,128)(2,1)S(1)}, bf16[256,1024]{1,0:T(8,128)(2,1)S(1)}, u32[]{:S(2)}, u32[]{:S(2)}) collective-permute-start(bf16[256,1024]{1,0:T(8,128)(2,1)S(1)} %collective-permute-done.4.refs_2_), channel_id=1, source_target_pairs={{0,4},{4,8},{6,2},{8,12},{10,6},{12,16},{14,10},{16,20},{18,14},{2... | collective-permute-start | bytes 1572872 | tf_op jit(solution)/shard_map/ppermute | solution.py:566
  51.9 14.4 %collective-permute-start.1 = (bf16[256,1024]{1,0:T(8,128)(2,1)S(1)}, bf16[256,1024]{1,0:T(8,128)(2,1)S(1)}, u32[]{:S(2)}, u32[]{:S(2)}) collective-permute-start(bf16[256,1024]{1,0:T(8,128)(2,1)S(1)} %collective-permute-done.refs_3_), channel_id=1, source_target_pairs={{0,4},{4,8},{6,2},{8,12},{10,6},{12,16},{14,10},{16,20},{18,14},{2... | collective-permute-start | bytes 1572872 | tf_op jit(solution)/shard_map/ppermute | solution.py:566
  68.4 1.2 collective-permute-start.8
  71.5 14.8 %collective-permute-start.10 = (bf16[256,1024]{1,0:T(8,128)(2,1)S(1)}, bf16[256,1024]{1,0:T(8,128)(2,1)S(1)}, u32[]{:S(2)}, u32[]{:S(2)}) collective-permute-start(bf16[256,1024]{1,0:T(8,128)(2,1)S(1)} %get-tuple-element.60.refs_0_), channel_id=1, source_target_pairs={{0,2},{2,0},{4,6},{6,4},{8,10},{10,8},{12,14},{14,12},{16,18},{18,... | collective-permute-start | bytes 1572872 | tf_op jit(solution)/shard_map/ppermute | solution.py:560
  73.5 24.0 %collective-permute-start.11 = (bf16[256,1024]{1,0:T(8,128)(2,1)S(1)}, bf16[256,1024]{1,0:T(8,128)(2,1)S(1)}, u32[]{:S(2)}, u32[]{:S(2)}) collective-permute-start(bf16[256,1024]{1,0:T(8,128)(2,1)S(1)} %get-tuple-element.65.refs_1_), channel_id=1, source_target_pairs={{0,2},{2,0},{4,6},{6,4},{8,10},{10,8},{12,14},{14,12},{16,18},{18,... | collective-permute-start | bytes 1572872 | tf_op jit(solution)/shard_map/ppermute | solution.py:560
  73.6 35.2 %collective-permute-start.13 = (bf16[256,1024]{1,0:T(8,128)(2,1)S(1)}, bf16[256,1024]{1,0:T(8,128)(2,1)S(1)}, u32[]{:S(2)}, u32[]{:S(2)}) collective-permute-start(bf16[256,1024]{1,0:T(8,128)(2,1)S(1)} %get-tuple-element.71.refs_2_), channel_id=1, source_target_pairs={{0,2},{2,0},{4,6},{6,4},{8,10},{10,8},{12,14},{14,12},{16,18},{18,... | collective-permute-start | bytes 1572872 | tf_op jit(solution)/shard_map/ppermute | solution.py:560
  86.3 7.9 %collective-permute-start.14 = (f32[16,2176]{1,0:T(8,128)S(1)}, f32[16,2176]{1,0:T(8,128)S(1)}, u32[]{:S(2)}, u32[]{:S(2)}) collective-permute-start(f32[16,2176]{1,0:T(8,128)S(1)} %kernel_grad.1), channel_id=1, source_target_pairs={{0,8},{2,10},{4,12},{6,14},{8,0},{10,2},{12,4},{14,6},{16,24},{18,... | collective-permute-start | bytes 417800 | tf_op jit(solution)/shard_map/ppermute | solution.py:574
  89.3 34.1 %collective-permute-start.9 = (bf16[256,1024]{1,0:T(8,128)(2,1)S(1)}, bf16[256,1024]{1,0:T(8,128)(2,1)S(1)}, u32[]{:S(2)}, u32[]{:S(2)}) collective-permute-start(bf16[256,1024]{1,0:T(8,128)(2,1)S(1)} %get-tuple-element.59.refs_3_), channel_id=1, source_target_pairs={{0,2},{2,0},{4,6},{6,4},{8,10},{10,8},{12,14},{14,12},{16,18},{18,... | collective-permute-start | bytes 1572872 | tf_op jit(solution)/shard_map/ppermute | solution.py:560
  89.8 37.6 %collective-permute-start.16 = (bf16[256,1024]{1,0:T(8,128)(2,1)S(1)}, bf16[256,1024]{1,0:T(8,128)(2,1)S(1)}, u32[]{:S(2)}, u32[]{:S(2)}) collective-permute-start(bf16[256,1024]{1,0:T(8,128)(2,1)S(1)} %collective-permute-done.10.refs_4_), channel_id=1, source_target_pairs={{0,4},{4,8},{6,2},{8,12},{10,6},{12,16},{14,10},{16,20},{18,14},{2... | collective-permute-start | bytes 1572872 | tf_op jit(solution)/shard_map/ppermute | solution.py:566
  97.5 29.9 %collective-permute-start.17 = (bf16[256,1024]{1,0:T(8,128)(2,1)S(1)}, bf16[256,1024]{1,0:T(8,128)(2,1)S(1)}, u32[]{:S(2)}, u32[]{:S(2)}) collective-permute-start(bf16[256,1024]{1,0:T(8,128)(2,1)S(1)} %collective-permute-done.11.refs_5_), channel_id=1, source_target_pairs={{0,4},{4,8},{6,2},{8,12},{10,6},{12,16},{14,10},{16,20},{18,14},{2... | collective-permute-start | bytes 1572872 | tf_op jit(solution)/shard_map/ppermute | solution.py:566
  108.7 18.7 %collective-permute-start.18 = (bf16[256,1024]{1,0:T(8,128)(2,1)S(1)}, bf16[256,1024]{1,0:T(8,128)(2,1)S(1)}, u32[]{:S(2)}, u32[]{:S(2)}) collective-permute-start(bf16[256,1024]{1,0:T(8,128)(2,1)S(1)} %collective-permute-done.13.refs_6_), channel_id=1, source_target_pairs={{0,4},{4,8},{6,2},{8,12},{10,6},{12,16},{14,10},{16,20},{18,14},{2... | collective-permute-start | bytes 1572872 | tf_op jit(solution)/shard_map/ppermute | solution.py:566
  113.0 14.3 %collective-permute-start.15 = (f32[16,2176]{1,0:T(8,128)S(1)}, f32[16,2176]{1,0:T(8,128)S(1)}, u32[]{:S(2)}, u32[]{:S(2)}) collective-permute-start(f32[16,2176]{1,0:T(8,128)S(1)} %add.23), channel_id=1, source_target_pairs={{0,16},{2,18},{4,20},{6,22},{8,24},{10,26},{12,28},{14,30},{16,0},... | collective-permute-start | bytes 417800 | tf_op jit(solution)/shard_map/ppermute | solution.py:574
  123.4 24.8 %collective-permute-start.12 = (bf16[256,1024]{1,0:T(8,128)(2,1)S(1)}, bf16[256,1024]{1,0:T(8,128)(2,1)S(1)}, u32[]{:S(2)}, u32[]{:S(2)}) collective-permute-start(bf16[256,1024]{1,0:T(8,128)(2,1)S(1)} %collective-permute-done.9.refs_7_), channel_id=1, source_target_pairs={{0,4},{4,8},{6,2},{8,12},{10,6},{12,16},{14,10},{16,20},{18,14},{2... | collective-permute-start | bytes 1572872 | tf_op jit(solution)/shard_map/ppermute | solution.py:566
  137.8 13.0 %collective-permute-start.19 = (f32[16,2176]{1,0:T(8,128)S(1)}, f32[16,2176]{1,0:T(8,128)S(1)}, u32[]{:S(2)}, u32[]{:S(2)}) collective-permute-start(f32[16,2176]{1,0:T(8,128)S(1)} %add.24), channel_id=1, source_target_pairs={{0,2},{2,0},{4,6},{6,4},{8,10},{10,8},{12,14},{14,12},{16,18},{18,... | collective-permute-start | bytes 417800 | tf_op jit(solution)/shard_map/ppermute | solution.py:574
  146.7 6.5 %collective-permute-start.20 = (f32[16,2176]{1,0:T(8,128)S(1)}, f32[16,2176]{1,0:T(8,128)S(1)}, u32[]{:S(2)}, u32[]{:S(2)}) collective-permute-start(f32[16,2176]{1,0:T(8,128)S(1)} %add.24), channel_id=1, source_target_pairs={{0,4},{2,6},{4,0},{6,2},{8,12},{10,14},{12,8},{14,10},{16,20},{18,... | collective-permute-start | bytes 417800 | tf_op jit(solution)/shard_map/ppermute | solution.py:574
  146.7 6.5 %collective-permute-start.21 = (f32[16,2176]{1,0:T(8,128)S(1)}, f32[16,2176]{1,0:T(8,128)S(1)}, u32[]{:S(2)}, u32[]{:S(2)}) collective-permute-start(f32[16,2176]{1,0:T(8,128)S(1)} %add.24), channel_id=1, source_target_pairs={{0,6},{2,4},{4,2},{6,0},{8,14},{10,12},{12,10},{14,8},{16,22},{18,... | collective-permute-start | bytes 417800 | tf_op jit(solution)/shard_map/ppermute | solution.py:574
  (3 other events, 96.4 us)

commit v6 on v5

--- a/solution.py
+++ b/solution.py
@@ -627,10 +627,9 @@
     grad_far = [relayed(chunk) for chunk in grad_near]
     totals, *grad_far[:2] = lax.optimization_barrier((totals, *grad_far[:2]))
     value_grad, first = value_grad_of(back_band, mix_grad, grad_near, grad_far[:-1], lag)
-    totals, first = lax.optimization_barrier((totals, first))
+    value_grad = value_grad_last(back_band, grad_far[-1], first, value_grad)
+    totals, value_grad = lax.optimization_barrier((totals, value_grad))
     terms = [totals] + terms_over_bits(totals, bits[:2])
-    value_grad = value_grad_last(back_band, grad_far[-1], first, value_grad)
-    value_grad, *terms = lax.optimization_barrier((value_grad, *terms))
     totals = sum(terms[1:], terms[0])
     tokens = rows * count
     kernel_grad = totals[:, : 2 * lag] / math.sqrt(tokens * HEAD)

time: 155 us -> 158 us (1.019)
  waiting for transfers between devices: 39.6 us -> 42.1 us
    ppermute x5, waiting for transfers between devices: 2.51 us -> 5.01 us  [terms_over_bits(): lax.ppermute(value, 'seq', [(i, i ^ flip) for i in range(count)])]
  transfers between devices with their start and end apart: 22 -> 22, of which waited for: 9 -> 10; matrix products, arithmetic and copies ran while one was open for 2% -> 2% of each run, Pallas kernels for 29% -> 27%
where the time goes in v6:
time: 158 us; the launch traced here: 157 us
  starting transfers between devices  58.7 us (37%)
  Pallas kernels  51.1 us (32%)
  waiting for transfers between devices  42.1 us (27%)
  local copies, waits for them, and re-layouts  3.71 us (2%)
    ppermute x8, waiting for transfers between devices, swapped(): return lax.ppermute(chunk, 'seq', [(i, i ^ 1) for i in range(count)])  35.9 us
    ppermute x8, starting transfers between devices, relayed(): lax.ppermute(chunk, 'seq', [(i, j) for i, j in pairs if 0 <= j < count])  32.6 us
    ppermute x5, starting transfers between devices, terms_over_bits(): lax.ppermute(value, 'seq', [(i, i ^ flip) for i in range(count)])  16.1 us
    pallas_call x1, Pallas kernels, forward(): pl.pallas_call(functools.partial(forward_body, slots), grid=(width // LAN...  10.6 us
    pallas_call x1, Pallas kernels, kernel_grad_local(): pl.pallas_call(functools.partial(kernel_grad_body, slots), grid=(pairs,),...  10.4 us
    pallas_call x1, Pallas kernels, value_grad_of(): pl.pallas_call(functools.partial(value_grad_body, slots), grid=(width //...  10.3 us
    ppermute x8, starting transfers between devices, swapped(): return lax.ppermute(chunk, 'seq', [(i, i ^ 1) for i in range(count)])  9.81 us
    pallas_call x2, Pallas kernels, bands(): pl.pallas_call(band_body, grid=(heads // 2,), in_specs=[VMEM], out_specs=...  6.2 us
  transfers between devices with their start and end apart: 22, of which 10 were waited for; matrix products, arithmetic and copies ran while one was open for 2% of the time, Pallas kernels for 27%

profile of v6, /device:TPU:0, one launch (start us, length us, event | category | flops | bytes accessed | tf_op | source)
XLA Modules:
  0.0 157.3 jit_solution(618956856836245276)
XLA Ops:
  3.0 3.0 %collective-permute-start.2 = (bf16[256,1024]{1,0:T(8,128)(2,1)}, bf16[256,1024]{1,0:T(8,128)(2,1)S(1)}, u32[]{:S(2)}, u32[]{:S(2)}) collective-permute-start(bf16[256,1024]{1,0:T(8,128)(2,1)} %get-tuple-element.47), channel_id=1, source_target_pairs={{0,2},{2,0},{4,6},{6,4},{8,10},{10,8},{12,14},{14,12},{16,18},{18,... | collective-permute-start | bytes 1572872 | tf_op jit(solution)/shard_map/ppermute | solution.py:560
  11.2 3.1 %bands.2.band_ref = bf16[16,128,2432]{2,1,0:T(8,128)(2,1)S(1)} custom-call(f32[8,2,2304]{2,1,0:T(2,128)S(1)} %reshape.22.row_ref), custom_call_target="tpu_custom_call" | custom-call | flops 4718592 | bytes 9437184 | tf_op jit(solution)/shard_map/bands/pallas_call | solution.py:84
  14.4 4.6 %collective-permute-done.2.refs_0_ = bf16[256,1024]{1,0:T(8,128)(2,1)S(1)} collective-permute-done((bf16[256,1024]{1,0:T(8,128)(2,1)}, bf16[256,1024]{1,0:T(8,128)(2,1)S(1)}, u32[]{:S(2)}, u32[]{:S(2)}) %collective-permute-start.2) | collective-permute-done | bytes 524320 | tf_op jit(solution)/shard_map/ppermute | solution.py:560
  19.0 4.0 %collective-permute-start.5 = (bf16[256,1024]{1,0:T(8,128)(2,1)S(1)}, bf16[256,1024]{1,0:T(8,128)(2,1)S(1)}, u32[]{:S(2)}, u32[]{:S(2)}) collective-permute-start(bf16[256,1024]{1,0:T(8,128)(2,1)S(1)} %collective-permute-done.2.refs_0_), channel_id=1, source_target_pairs={{0,4},{4,8},{6,2},{8,12},{10,6},{12,16},{14,10},{16,20},{18,14},{2... | collective-permute-start | bytes 1572872 | tf_op jit(solution)/shard_map/ppermute | solution.py:566
  23.0 7.2 %collective-permute-done.3.refs_1_ = bf16[256,1024]{1,0:T(8,128)(2,1)S(1)} collective-permute-done((bf16[256,1024]{1,0:T(8,128)(2,1)S(1)}, bf16[256,1024]{1,0:T(8,128)(2,1)S(1)}, u32[]{:S(2)}, u32[]{:S(2)}) %collective-permute-start.3) | collective-permute-done | bytes 524320 | tf_op jit(solution)/shard_map/ppermute | solution.py:560
  30.2 4.0 %collective-permute-start.6 = (bf16[256,1024]{1,0:T(8,128)(2,1)S(1)}, bf16[256,1024]{1,0:T(8,128)(2,1)S(1)}, u32[]{:S(2)}, u32[]{:S(2)}) collective-permute-start(bf16[256,1024]{1,0:T(8,128)(2,1)S(1)} %collective-permute-done.3.refs_1_), channel_id=1, source_target_pairs={{0,4},{4,8},{6,2},{8,12},{10,6},{12,16},{14,10},{16,20},{18,14},{2... | collective-permute-start | bytes 1572872 | tf_op jit(solution)/shard_map/ppermute | solution.py:566
  34.3 7.2 %collective-permute-done.4.refs_2_ = bf16[256,1024]{1,0:T(8,128)(2,1)S(1)} collective-permute-done((bf16[256,1024]{1,0:T(8,128)(2,1)S(1)}, bf16[256,1024]{1,0:T(8,128)(2,1)S(1)}, u32[]{:S(2)}, u32[]{:S(2)}) %collective-permute-start.4) | collective-permute-done | bytes 524320 | tf_op jit(solution)/shard_map/ppermute | solution.py:560
  41.5 4.0 %collective-permute-start.7 = (bf16[256,1024]{1,0:T(8,128)(2,1)S(1)}, bf16[256,1024]{1,0:T(8,128)(2,1)S(1)}, u32[]{:S(2)}, u32[]{:S(2)}) collective-permute-start(bf16[256,1024]{1,0:T(8,128)(2,1)S(1)} %collective-permute-done.4.refs_2_), channel_id=1, source_target_pairs={{0,4},{4,8},{6,2},{8,12},{10,6},{12,16},{14,10},{16,20},{18,14},{2... | collective-permute-start | bytes 1572872 | tf_op jit(solution)/shard_map/ppermute | solution.py:566
  45.5 6.4 %collective-permute-done.refs_3_ = bf16[256,1024]{1,0:T(8,128)(2,1)S(1)} collective-permute-done((bf16[256,1024]{1,0:T(8,128)(2,1)S(1)}, bf16[256,1024]{1,0:T(8,128)(2,1)S(1)}, u32[]{:S(2)}, u32[]{:S(2)}) %collective-permute-start) | collective-permute-done | bytes 524320 | tf_op jit(solution)/shard_map/ppermute | solution.py:560
  51.9 3.7 %collective-permute-start.1 = (bf16[256,1024]{1,0:T(8,128)(2,1)S(1)}, bf16[256,1024]{1,0:T(8,128)(2,1)S(1)}, u32[]{:S(2)}, u32[]{:S(2)}) collective-permute-start(bf16[256,1024]{1,0:T(8,128)(2,1)S(1)} %collective-permute-done.refs_3_), channel_id=1, source_target_pairs={{0,4},{4,8},{6,2},{8,12},{10,6},{12,16},{14,10},{16,20},{18,14},{2... | collective-permute-start | bytes 1572872 | tf_op jit(solution)/shard_map/ppermute | solution.py:566
  55.7 10.6 %forward.1 = (f32[1024,1024]{1,0:T(8,128)S(1)}, f32[2,1024]{1,0:T(2,128)S(1)}, bf16[16,256,768]{2,1,0:T(8,128)(2,1)S(1)}, bf16[16,256,640]{2,1,0:T(8,128)(2,1)S(1)}) custom-call(bf16[16,128,2432]{2,1,0:T(8,128)(2,1)S(1)} %bands.2.band_ref, bf16[1024,1024]{1,0:T(8,128)(2,1)S(1)} %copy-done.2, bf16[1024,1024]{1,0:T(8,128)(2,1)S(1)} %copy-done, ...), custom_call_target="tpu_custom_call" | custom-call | flops 4831838208 | bytes 16777216 | tf_op jit(solution)/shard_map/forward/pallas_call | solution.py:261
  75.5 10.4 %kernel_grad.1 = f32[16,2176]{1,0:T(8,128)S(1)} custom-call(f32[1,1024]{1,0:T(1,128)S(1)} %get-tuple-element.65.gain_ref, bf16[16,256,768]{2,1,0:T(8,128)(2,1)S(1)} %get-tuple-element.66.even_ref, bf16[16,256,640]{2,1,0:T(8,128)(2,1)S(1)} %get-tuple-element.67.odd_ref, bf16[256,1024]{1,0:T(8,128)(2,1)S(1)} %collective-permute-done.1.last_ref, ...), custom_call_target="tpu_custom_call" | custom-call | flops 4831838208 | bytes 8388608 | tf_op jit(solution)/shard_map/kernel_grad/pallas_call | solution.py:474
  86.3 3.0 %collective-permute-start.13 = (f32[16,2176]{1,0:T(8,128)S(1)}, f32[16,2176]{1,0:T(8,128)S(1)}, u32[]{:S(2)}, u32[]{:S(2)}) collective-permute-start(f32[16,2176]{1,0:T(8,128)S(1)} %kernel_grad.1), channel_id=1, source_target_pairs={{0,8},{2,10},{4,12},{6,14},{8,0},{10,2},{12,4},{14,6},{16,24},{18,... | collective-permute-start | bytes 417800 | tf_op jit(solution)/shard_map/ppermute | solution.py:574
  89.8 4.3 %collective-permute-start.15 = (bf16[256,1024]{1,0:T(8,128)(2,1)S(1)}, bf16[256,1024]{1,0:T(8,128)(2,1)S(1)}, u32[]{:S(2)}, u32[]{:S(2)}) collective-permute-start(bf16[256,1024]{1,0:T(8,128)(2,1)S(1)} %collective-permute-done.10.refs_4_), channel_id=1, source_target_pairs={{0,4},{4,8},{6,2},{8,12},{10,6},{12,16},{14,10},{16,20},{18,14},{2... | collective-permute-start | bytes 1572872 | tf_op jit(solution)/shard_map/ppermute | solution.py:566
  94.2 3.3 %collective-permute-done.11.refs_5_ = bf16[256,1024]{1,0:T(8,128)(2,1)S(1)} collective-permute-done((bf16[256,1024]{1,0:T(8,128)(2,1)S(1)}, bf16[256,1024]{1,0:T(8,128)(2,1)S(1)}, u32[]{:S(2)}, u32[]{:S(2)}) %collective-permute-start.11) | collective-permute-done | bytes 524320 | tf_op jit(solution)/shard_map/ppermute | solution.py:560
  97.5 4.3 %collective-permute-start.16 = (bf16[256,1024]{1,0:T(8,128)(2,1)S(1)}, bf16[256,1024]{1,0:T(8,128)(2,1)S(1)}, u32[]{:S(2)}, u32[]{:S(2)}) collective-permute-start(bf16[256,1024]{1,0:T(8,128)(2,1)S(1)} %collective-permute-done.11.refs_5_), channel_id=1, source_target_pairs={{0,4},{4,8},{6,2},{8,12},{10,6},{12,16},{14,10},{16,20},{18,14},{2... | collective-permute-start | bytes 1572872 | tf_op jit(solution)/shard_map/ppermute | solution.py:566
  101.8 7.0 %collective-permute-done.12.refs_6_ = bf16[256,1024]{1,0:T(8,128)(2,1)S(1)} collective-permute-done((bf16[256,1024]{1,0:T(8,128)(2,1)S(1)}, bf16[256,1024]{1,0:T(8,128)(2,1)S(1)}, u32[]{:S(2)}, u32[]{:S(2)}) %collective-permute-start.12) | collective-permute-done | bytes 524320 | tf_op jit(solution)/shard_map/ppermute | solution.py:560
  108.7 4.3 %collective-permute-start.18 = (bf16[256,1024]{1,0:T(8,128)(2,1)S(1)}, bf16[256,1024]{1,0:T(8,128)(2,1)S(1)}, u32[]{:S(2)}, u32[]{:S(2)}) collective-permute-start(bf16[256,1024]{1,0:T(8,128)(2,1)S(1)} %collective-permute-done.12.refs_6_), channel_id=1, source_target_pairs={{0,4},{4,8},{6,2},{8,12},{10,6},{12,16},{14,10},{16,20},{18,14},{2... | collective-permute-start | bytes 1572872 | tf_op jit(solution)/shard_map/ppermute | solution.py:566
  115.7 3.1 %bands.3.band_ref = bf16[16,128,2432]{2,1,0:T(8,128)(2,1)S(1)} custom-call(f32[8,2,2304]{2,1,0:T(2,128)S(1)} %reshape.23.row_ref), custom_call_target="tpu_custom_call" | custom-call | flops 4718592 | bytes 9437184 | tf_op jit(solution)/shard_map/bands/pallas_call | solution.py:84
  118.8 4.6 %norm.1 = (bf16[1024,1024]{1,0:T(8,128)(2,1)}, bf16[1024,1024]{1,0:T(8,128)(2,1)}) custom-call(f32[2,1024]{1,0:T(2,128)S(1)} %add.22.sums_ref, f32[1024,1024]{1,0:T(8,128)S(1)} %get-tuple-element.50.mixed_ref, f32[256,1024]{1,0:T(8,128)S(1)} %get-tuple-element.53.first_ref, bf16[1024,1024]{1,0:T(8,128)(2,1)S(1)} %copy-done, ...), custom_call_target="tpu_custom_call" | custom-call | flops 14680064 | bytes 12582912 | tf_op jit(solution)/shard_map/norm/pallas_call | solution.py:396
  123.4 4.0 %collective-permute-start.17 = (bf16[256,1024]{1,0:T(8,128)(2,1)S(1)}, bf16[256,1024]{1,0:T(8,128)(2,1)S(1)}, u32[]{:S(2)}, u32[]{:S(2)}) collective-permute-start(bf16[256,1024]{1,0:T(8,128)(2,1)S(1)} %collective-permute-done.9.refs_7_), channel_id=1, source_target_pairs={{0,4},{4,8},{6,2},{8,12},{10,6},{12,16},{14,10},{16,20},{18,14},{2... | collective-permute-start | bytes 1572872 | tf_op jit(solution)/shard_map/ppermute | solution.py:566
  127.4 10.3 %value_grad.1 = (bf16[1024,1024]{1,0:T(8,128)(2,1)}, f32[256,1024]{1,0:T(8,128)S(1)}) custom-call(bf16[16,128,2432]{2,1,0:T(8,128)(2,1)S(1)} %bands.3.band_ref, bf16[256,1024]{1,0:T(8,128)(2,1)S(1)} %get-tuple-element.55.refs_0_, bf16[256,1024]{1,0:T(8,128)(2,1)S(1)} %get-tuple-element.60.refs_1_, bf16[256,1024]{1,0:T(8,128)(2,1)S(1)} %get-tuple-element.64.refs_2_, ...), custom_call_target="tpu_custom_call" | custom-call | flops 4831838208 | bytes 12582912 | tf_op jit(solution)/shard_map/value_grad/pallas_call | solution.py:512
  140.4 9.0 %collective-permute-start.19 = (f32[16,2176]{1,0:T(8,128)S(1)}, f32[16,2176]{1,0:T(8,128)S(1)}, u32[]{:S(2)}, u32[]{:S(2)}) collective-permute-start(f32[16,2176]{1,0:T(8,128)S(1)} %add.24), channel_id=1, source_target_pairs={{0,2},{2,0},{4,6},{6,4},{8,10},{10,8},{12,14},{14,12},{16,18},{18,... | collective-permute-start | bytes 417800 | tf_op jit(solution)/shard_map/ppermute | solution.py:574
  152.4 3.5 %collective-permute-done.20 = f32[16,2176]{1,0:T(8,128)S(1)} collective-permute-done((f32[16,2176]{1,0:T(8,128)S(1)}, f32[16,2176]{1,0:T(8,128)S(1)}, u32[]{:S(2)}, u32[]{:S(2)}) %collective-permute-start.20) | collective-permute-done | bytes 139296 | tf_op jit(solution)/shard_map/ppermute | solution.py:574
  (52 shorter events, 27.3 us)
Async XLA Ops:
  3.0 16.0 %collective-permute-start.2 = (bf16[256,1024]{1,0:T(8,128)(2,1)}, bf16[256,1024]{1,0:T(8,128)(2,1)S(1)}, u32[]{:S(2)}, u32[]{:S(2)}) collective-permute-start(bf16[256,1024]{1,0:T(8,128)(2,1)} %get-tuple-element.47), channel_id=1, source_target_pairs={{0,2},{2,0},{4,6},{6,4},{8,10},{10,8},{12,14},{14,12},{16,18},{18,... | collective-permute-start | bytes 1572872 | tf_op jit(solution)/shard_map/ppermute | solution.py:560
  6.0 24.2 %collective-permute-start.3 = (bf16[256,1024]{1,0:T(8,128)(2,1)S(1)}, bf16[256,1024]{1,0:T(8,128)(2,1)S(1)}, u32[]{:S(2)}, u32[]{:S(2)}) collective-permute-start(bf16[256,1024]{1,0:T(8,128)(2,1)S(1)} %get-tuple-element.48), channel_id=1, source_target_pairs={{0,2},{2,0},{4,6},{6,4},{8,10},{10,8},{12,14},{14,12},{16,18},{18,... | collective-permute-start | bytes 1572872 | tf_op jit(solution)/shard_map/ppermute | solution.py:560
  6.1 35.4 %collective-permute-start.4 = (bf16[256,1024]{1,0:T(8,128)(2,1)S(1)}, bf16[256,1024]{1,0:T(8,128)(2,1)S(1)}, u32[]{:S(2)}, u32[]{:S(2)}) collective-permute-start(bf16[256,1024]{1,0:T(8,128)(2,1)S(1)} %get-tuple-element.49), channel_id=1, source_target_pairs={{0,2},{2,0},{4,6},{6,4},{8,10},{10,8},{12,14},{14,12},{16,18},{18,... | collective-permute-start | bytes 1572872 | tf_op jit(solution)/shard_map/ppermute | solution.py:560
  11.1 44.5 %copy-start = (bf16[1024,1024]{1,0:T(8,128)(2,1)S(1)}, bf16[1024,1024]{1,0:T(8,128)(2,1)}, u32[]{:S(2)}) copy-start(bf16[1024,1024]{1,0:T(8,128)(2,1)} %gate_ref.7) | copy-start | bytes 6291460
  11.1 44.5 %copy-start.1 = (bf16[1024,1024]{1,0:T(8,128)(2,1)S(1)}, bf16[1024,1024]{1,0:T(8,128)(2,1)}, u32[]{:S(2)}) copy-start(bf16[1024,1024]{1,0:T(8,128)(2,1)} %grad_ref.7) | copy-start | bytes 6291460
  14.3 37.6 %collective-permute-start = (bf16[256,1024]{1,0:T(8,128)(2,1)S(1)}, bf16[256,1024]{1,0:T(8,128)(2,1)S(1)}, u32[]{:S(2)}, u32[]{:S(2)}) collective-permute-start(bf16[256,1024]{1,0:T(8,128)(2,1)S(1)} %get-tuple-element.46), channel_id=1, source_target_pairs={{0,2},{2,0},{4,6},{6,4},{8,10},{10,8},{12,14},{14,12},{16,18},{18,... | collective-permute-start | bytes 1572872 | tf_op jit(solution)/shard_map/ppermute | solution.py:560
  19.0 36.6 %collective-permute-start.5 = (bf16[256,1024]{1,0:T(8,128)(2,1)S(1)}, bf16[256,1024]{1,0:T(8,128)(2,1)S(1)}, u32[]{:S(2)}, u32[]{:S(2)}) collective-permute-start(bf16[256,1024]{1,0:T(8,128)(2,1)S(1)} %collective-permute-done.2.refs_0_), channel_id=1, source_target_pairs={{0,4},{4,8},{6,2},{8,12},{10,6},{12,16},{14,10},{16,20},{18,14},{2... | collective-permute-start | bytes 1572872 | tf_op jit(solution)/shard_map/ppermute | solution.py:566
  30.2 25.4 %collective-permute-start.6 = (bf16[256,1024]{1,0:T(8,128)(2,1)S(1)}, bf16[256,1024]{1,0:T(8,128)(2,1)S(1)}, u32[]{:S(2)}, u32[]{:S(2)}) collective-permute-start(bf16[256,1024]{1,0:T(8,128)(2,1)S(1)} %collective-permute-done.3.refs_1_), channel_id=1, source_target_pairs={{0,4},{4,8},{6,2},{8,12},{10,6},{12,16},{14,10},{16,20},{18,14},{2... | collective-permute-start | bytes 1572872 | tf_op jit(solution)/shard_map/ppermute | solution.py:566
  41.5 14.1 %collective-permute-start.7 = (bf16[256,1024]{1,0:T(8,128)(2,1)S(1)}, bf16[256,1024]{1,0:T(8,128)(2,1)S(1)}, u32[]{:S(2)}, u32[]{:S(2)}) collective-permute-start(bf16[256,1024]{1,0:T(8,128)(2,1)S(1)} %collective-permute-done.4.refs_2_), channel_id=1, source_target_pairs={{0,4},{4,8},{6,2},{8,12},{10,6},{12,16},{14,10},{16,20},{18,14},{2... | collective-permute-start | bytes 1572872 | tf_op jit(solution)/shard_map/ppermute | solution.py:566
  51.9 14.4 %collective-permute-start.1 = (bf16[256,1024]{1,0:T(8,128)(2,1)S(1)}, bf16[256,1024]{1,0:T(8,128)(2,1)S(1)}, u32[]{:S(2)}, u32[]{:S(2)}) collective-permute-start(bf16[256,1024]{1,0:T(8,128)(2,1)S(1)} %collective-permute-done.refs_3_), channel_id=1, source_target_pairs={{0,4},{4,8},{6,2},{8,12},{10,6},{12,16},{14,10},{16,20},{18,14},{2... | collective-permute-start | bytes 1572872 | tf_op jit(solution)/shard_map/ppermute | solution.py:566
  68.4 1.2 collective-permute-start.8
  71.5 14.8 %collective-permute-start.10 = (bf16[256,1024]{1,0:T(8,128)(2,1)S(1)}, bf16[256,1024]{1,0:T(8,128)(2,1)S(1)}, u32[]{:S(2)}, u32[]{:S(2)}) collective-permute-start(bf16[256,1024]{1,0:T(8,128)(2,1)S(1)} %get-tuple-element.55.refs_0_), channel_id=1, source_target_pairs={{0,2},{2,0},{4,6},{6,4},{8,10},{10,8},{12,14},{14,12},{16,18},{18,... | collective-permute-start | bytes 1572872 | tf_op jit(solution)/shard_map/ppermute | solution.py:560
  73.5 24.0 %collective-permute-start.11 = (bf16[256,1024]{1,0:T(8,128)(2,1)S(1)}, bf16[256,1024]{1,0:T(8,128)(2,1)S(1)}, u32[]{:S(2)}, u32[]{:S(2)}) collective-permute-start(bf16[256,1024]{1,0:T(8,128)(2,1)S(1)} %get-tuple-element.60.refs_1_), channel_id=1, source_target_pairs={{0,2},{2,0},{4,6},{6,4},{8,10},{10,8},{12,14},{14,12},{16,18},{18,... | collective-permute-start | bytes 1572872 | tf_op jit(solution)/shard_map/ppermute | solution.py:560
  73.6 35.2 %collective-permute-start.12 = (bf16[256,1024]{1,0:T(8,128)(2,1)S(1)}, bf16[256,1024]{1,0:T(8,128)(2,1)S(1)}, u32[]{:S(2)}, u32[]{:S(2)}) collective-permute-start(bf16[256,1024]{1,0:T(8,128)(2,1)S(1)} %get-tuple-element.64.refs_2_), channel_id=1, source_target_pairs={{0,2},{2,0},{4,6},{6,4},{8,10},{10,8},{12,14},{14,12},{16,18},{18,... | collective-permute-start | bytes 1572872 | tf_op jit(solution)/shard_map/ppermute | solution.py:560
  86.3 7.9 %collective-permute-start.13 = (f32[16,2176]{1,0:T(8,128)S(1)}, f32[16,2176]{1,0:T(8,128)S(1)}, u32[]{:S(2)}, u32[]{:S(2)}) collective-permute-start(f32[16,2176]{1,0:T(8,128)S(1)} %kernel_grad.1), channel_id=1, source_target_pairs={{0,8},{2,10},{4,12},{6,14},{8,0},{10,2},{12,4},{14,6},{16,24},{18,... | collective-permute-start | bytes 417800 | tf_op jit(solution)/shard_map/ppermute | solution.py:574
  89.3 34.1 %collective-permute-start.9 = (bf16[256,1024]{1,0:T(8,128)(2,1)S(1)}, bf16[256,1024]{1,0:T(8,128)(2,1)S(1)}, u32[]{:S(2)}, u32[]{:S(2)}) collective-permute-start(bf16[256,1024]{1,0:T(8,128)(2,1)S(1)} %get-tuple-element.54.refs_3_), channel_id=1, source_target_pairs={{0,2},{2,0},{4,6},{6,4},{8,10},{10,8},{12,14},{14,12},{16,18},{18,... | collective-permute-start | bytes 1572872 | tf_op jit(solution)/shard_map/ppermute | solution.py:560
  89.8 37.6 %collective-permute-start.15 = (bf16[256,1024]{1,0:T(8,128)(2,1)S(1)}, bf16[256,1024]{1,0:T(8,128)(2,1)S(1)}, u32[]{:S(2)}, u32[]{:S(2)}) collective-permute-start(bf16[256,1024]{1,0:T(8,128)(2,1)S(1)} %collective-permute-done.10.refs_4_), channel_id=1, source_target_pairs={{0,4},{4,8},{6,2},{8,12},{10,6},{12,16},{14,10},{16,20},{18,14},{2... | collective-permute-start | bytes 1572872 | tf_op jit(solution)/shard_map/ppermute | solution.py:566
  97.5 29.9 %collective-permute-start.16 = (bf16[256,1024]{1,0:T(8,128)(2,1)S(1)}, bf16[256,1024]{1,0:T(8,128)(2,1)S(1)}, u32[]{:S(2)}, u32[]{:S(2)}) collective-permute-start(bf16[256,1024]{1,0:T(8,128)(2,1)S(1)} %collective-permute-done.11.refs_5_), channel_id=1, source_target_pairs={{0,4},{4,8},{6,2},{8,12},{10,6},{12,16},{14,10},{16,20},{18,14},{2... | collective-permute-start | bytes 1572872 | tf_op jit(solution)/shard_map/ppermute | solution.py:566
  108.7 18.7 %collective-permute-start.18 = (bf16[256,1024]{1,0:T(8,128)(2,1)S(1)}, bf16[256,1024]{1,0:T(8,128)(2,1)S(1)}, u32[]{:S(2)}, u32[]{:S(2)}) collective-permute-start(bf16[256,1024]{1,0:T(8,128)(2,1)S(1)} %collective-permute-done.12.refs_6_), channel_id=1, source_target_pairs={{0,4},{4,8},{6,2},{8,12},{10,6},{12,16},{14,10},{16,20},{18,14},{2... | collective-permute-start | bytes 1572872 | tf_op jit(solution)/shard_map/ppermute | solution.py:566
  113.0 14.3 %collective-permute-start.14 = (f32[16,2176]{1,0:T(8,128)S(1)}, f32[16,2176]{1,0:T(8,128)S(1)}, u32[]{:S(2)}, u32[]{:S(2)}) collective-permute-start(f32[16,2176]{1,0:T(8,128)S(1)} %add.23), channel_id=1, source_target_pairs={{0,16},{2,18},{4,20},{6,22},{8,24},{10,26},{12,28},{14,30},{16,0},... | collective-permute-start | bytes 417800 | tf_op jit(solution)/shard_map/ppermute | solution.py:574
  123.4 14.4 %collective-permute-start.17 = (bf16[256,1024]{1,0:T(8,128)(2,1)S(1)}, bf16[256,1024]{1,0:T(8,128)(2,1)S(1)}, u32[]{:S(2)}, u32[]{:S(2)}) collective-permute-start(bf16[256,1024]{1,0:T(8,128)(2,1)S(1)} %collective-permute-done.9.refs_7_), channel_id=1, source_target_pairs={{0,4},{4,8},{6,2},{8,12},{10,6},{12,16},{14,10},{16,20},{18,14},{2... | collective-permute-start | bytes 1572872 | tf_op jit(solution)/shard_map/ppermute | solution.py:566
  140.4 12.0 %collective-permute-start.19 = (f32[16,2176]{1,0:T(8,128)S(1)}, f32[16,2176]{1,0:T(8,128)S(1)}, u32[]{:S(2)}, u32[]{:S(2)}) collective-permute-start(f32[16,2176]{1,0:T(8,128)S(1)} %add.24), channel_id=1, source_target_pairs={{0,2},{2,0},{4,6},{6,4},{8,10},{10,8},{12,14},{14,12},{16,18},{18,... | collective-permute-start | bytes 417800 | tf_op jit(solution)/shard_map/ppermute | solution.py:574
  149.3 6.5 %collective-permute-start.20 = (f32[16,2176]{1,0:T(8,128)S(1)}, f32[16,2176]{1,0:T(8,128)S(1)}, u32[]{:S(2)}, u32[]{:S(2)}) collective-permute-start(f32[16,2176]{1,0:T(8,128)S(1)} %add.24), channel_id=1, source_target_pairs={{0,4},{2,6},{4,0},{6,2},{8,12},{10,14},{12,8},{14,10},{16,20},{18,... | collective-permute-start | bytes 417800 | tf_op jit(solution)/shard_map/ppermute | solution.py:574
  149.4 6.5 %collective-permute-start.21 = (f32[16,2176]{1,0:T(8,128)S(1)}, f32[16,2176]{1,0:T(8,128)S(1)}, u32[]{:S(2)}, u32[]{:S(2)}) collective-permute-start(f32[16,2176]{1,0:T(8,128)S(1)} %add.24), channel_id=1, source_target_pairs={{0,6},{2,4},{4,2},{6,0},{8,14},{10,12},{12,10},{14,8},{16,22},{18,... | collective-permute-start | bytes 417800 | tf_op jit(solution)/shard_map/ppermute | solution.py:574
  (3 other events, 96.4 us)

commit v7 on v4

--- a/solution.py
+++ b/solution.py
@@ -620,7 +620,9 @@
     )
     bits = list(range(count.bit_length() - 1))
     for bit in bits[2:]:
-        totals += terms_over_bits(totals, [bit])[0]
+        half = lax.optimization_barrier(totals.astype(jnp.bfloat16))
+        other = terms_over_bits(half, [bit])[0]
+        totals = half.astype(jnp.float32) + other.astype(jnp.float32)
     grad_near[1], totals = lax.optimization_barrier((grad_near[1], totals))
     grad_far = [relayed(chunk) for chunk in grad_near]
     totals, *grad_far[:2] = lax.optimization_barrier((totals, *grad_far[:2]))

time: 153 us -> 161 us (1.052)
  waiting for transfers between devices: 45 us -> 54.7 us
    ppermute x8, waiting for transfers between devices: 30.9 us -> 51.2 us  [swapped(): return lax.ppermute(chunk, 'seq', [(i, i ^ 1) for i in range(count)])]
    ppermute x8, waiting for transfers between devices: 9.84 us -> 0.02 us  [relayed(): lax.ppermute(chunk, 'seq', [(i, j) for i, j in pairs if 0 <= j < count])]
  transfers between devices with their start and end apart: 22 -> 22, of which waited for: 9 -> 9; matrix products, arithmetic and copies ran while one was open for 2% -> 2% of each run, Pallas kernels for 29% -> 28%
where the time goes in v7:
time: 161 us
  waiting for transfers between devices  54.7 us (34%)
  Pallas kernels  51 us (32%)
  starting transfers between devices  49.5 us (31%)
  local copies, waits for them, and re-layouts  3.71 us (2%)
    ppermute x8, waiting for transfers between devices, swapped(): return lax.ppermute(chunk, 'seq', [(i, i ^ 1) for i in range(count)])  51.2 us
    ppermute x8, starting transfers between devices, relayed(): lax.ppermute(chunk, 'seq', [(i, j) for i, j in pairs if 0 <= j < count])  30.1 us
    pallas_call x1, Pallas kernels, forward(): pl.pallas_call(functools.partial(forward_body, slots), grid=(width // LAN...  10.6 us
    pallas_call x1, Pallas kernels, kernel_grad_local(): pl.pallas_call(functools.partial(kernel_grad_body, slots), grid=(pairs,),...  10.4 us
    pallas_call x1, Pallas kernels, value_grad_of(): pl.pallas_call(functools.partial(value_grad_body, slots), grid=(width //...  10.3 us
    ppermute x8, starting transfers between devices, swapped(): return lax.ppermute(chunk, 'seq', [(i, i ^ 1) for i in range(count)])  9.82 us
    ppermute x5, starting transfers between devices, terms_over_bits(): lax.ppermute(value, 'seq', [(i, i ^ flip) for i in range(count)])  9.43 us
    pallas_call x2, Pallas kernels, bands(): pl.pallas_call(band_body, grid=(heads // 2,), in_specs=[VMEM], out_specs=...  6.21 us
  transfers between devices with their start and end apart: 22, of which 9 were waited for; matrix products, arithmetic and copies ran while one was open for 2% of the time, Pallas kernels for 28%

profile of v7, /device:TPU:0, one launch (start us, length us, event | category | flops | bytes accessed | tf_op | source)
XLA Modules:
  0.0 160.6 jit_solution(11696780125399060012)
XLA Ops:
  3.0 3.0 %collective-permute-start.2 = (bf16[256,1024]{1,0:T(8,128)(2,1)}, bf16[256,1024]{1,0:T(8,128)(2,1)S(1)}, u32[]{:S(2)}, u32[]{:S(2)}) collective-permute-start(bf16[256,1024]{1,0:T(8,128)(2,1)} %get-tuple-element.48), channel_id=1, source_target_pairs={{0,2},{2,0},{4,6},{6,4},{8,10},{10,8},{12,14},{14,12},{16,18},{18,... | collective-permute-start | bytes 1572872 | tf_op jit(solution)/shard_map/ppermute | solution.py:560
  11.2 3.1 %bands.2.band_ref = bf16[16,128,2432]{2,1,0:T(8,128)(2,1)S(1)} custom-call(f32[8,2,2304]{2,1,0:T(2,128)S(1)} %reshape.22.row_ref), custom_call_target="tpu_custom_call" | custom-call | flops 4718592 | bytes 9437184 | tf_op jit(solution)/shard_map/bands/pallas_call | solution.py:84
  14.4 4.6 %collective-permute-done.2.refs_0_ = bf16[256,1024]{1,0:T(8,128)(2,1)S(1)} collective-permute-done((bf16[256,1024]{1,0:T(8,128)(2,1)}, bf16[256,1024]{1,0:T(8,128)(2,1)S(1)}, u32[]{:S(2)}, u32[]{:S(2)}) %collective-permute-start.2) | collective-permute-done | bytes 524320 | tf_op jit(solution)/shard_map/ppermute | solution.py:560
  19.0 4.0 %collective-permute-start.5 = (bf16[256,1024]{1,0:T(8,128)(2,1)S(1)}, bf16[256,1024]{1,0:T(8,128)(2,1)S(1)}, u32[]{:S(2)}, u32[]{:S(2)}) collective-permute-start(bf16[256,1024]{1,0:T(8,128)(2,1)S(1)} %collective-permute-done.2.refs_0_), channel_id=1, source_target_pairs={{0,4},{4,8},{6,2},{8,12},{10,6},{12,16},{14,10},{16,20},{18,14},{2... | collective-permute-start | bytes 1572872 | tf_op jit(solution)/shard_map/ppermute | solution.py:566
  23.0 7.2 %collective-permute-done.3.refs_1_ = bf16[256,1024]{1,0:T(8,128)(2,1)S(1)} collective-permute-done((bf16[256,1024]{1,0:T(8,128)(2,1)S(1)}, bf16[256,1024]{1,0:T(8,128)(2,1)S(1)}, u32[]{:S(2)}, u32[]{:S(2)}) %collective-permute-start.3) | collective-permute-done | bytes 524320 | tf_op jit(solution)/shard_map/ppermute | solution.py:560
  30.2 4.0 %collective-permute-start.6 = (bf16[256,1024]{1,0:T(8,128)(2,1)S(1)}, bf16[256,1024]{1,0:T(8,128)(2,1)S(1)}, u32[]{:S(2)}, u32[]{:S(2)}) collective-permute-start(bf16[256,1024]{1,0:T(8,128)(2,1)S(1)} %collective-permute-done.3.refs_1_), channel_id=1, source_target_pairs={{0,4},{4,8},{6,2},{8,12},{10,6},{12,16},{14,10},{16,20},{18,14},{2... | collective-permute-start | bytes 1572872 | tf_op jit(solution)/shard_map/ppermute | solution.py:566
  34.3 7.2 %collective-permute-done.4.refs_2_ = bf16[256,1024]{1,0:T(8,128)(2,1)S(1)} collective-permute-done((bf16[256,1024]{1,0:T(8,128)(2,1)S(1)}, bf16[256,1024]{1,0:T(8,128)(2,1)S(1)}, u32[]{:S(2)}, u32[]{:S(2)}) %collective-permute-start.4) | collective-permute-done | bytes 524320 | tf_op jit(solution)/shard_map/ppermute | solution.py:560
  41.5 4.0 %collective-permute-start.7 = (bf16[256,1024]{1,0:T(8,128)(2,1)S(1)}, bf16[256,1024]{1,0:T(8,128)(2,1)S(1)}, u32[]{:S(2)}, u32[]{:S(2)}) collective-permute-start(bf16[256,1024]{1,0:T(8,128)(2,1)S(1)} %collective-permute-done.4.refs_2_), channel_id=1, source_target_pairs={{0,4},{4,8},{6,2},{8,12},{10,6},{12,16},{14,10},{16,20},{18,14},{2... | collective-permute-start | bytes 1572872 | tf_op jit(solution)/shard_map/ppermute | solution.py:566
  45.5 6.4 %collective-permute-done.refs_3_ = bf16[256,1024]{1,0:T(8,128)(2,1)S(1)} collective-permute-done((bf16[256,1024]{1,0:T(8,128)(2,1)S(1)}, bf16[256,1024]{1,0:T(8,128)(2,1)S(1)}, u32[]{:S(2)}, u32[]{:S(2)}) %collective-permute-start) | collective-permute-done | bytes 524320 | tf_op jit(solution)/shard_map/ppermute | solution.py:560
  51.9 3.7 %collective-permute-start.1 = (bf16[256,1024]{1,0:T(8,128)(2,1)S(1)}, bf16[256,1024]{1,0:T(8,128)(2,1)S(1)}, u32[]{:S(2)}, u32[]{:S(2)}) collective-permute-start(bf16[256,1024]{1,0:T(8,128)(2,1)S(1)} %collective-permute-done.refs_3_), channel_id=1, source_target_pairs={{0,4},{4,8},{6,2},{8,12},{10,6},{12,16},{14,10},{16,20},{18,14},{2... | collective-permute-start | bytes 1572872 | tf_op jit(solution)/shard_map/ppermute | solution.py:566
  55.7 10.6 %forward.1 = (f32[1024,1024]{1,0:T(8,128)S(1)}, f32[2,1024]{1,0:T(2,128)S(1)}, bf16[16,256,768]{2,1,0:T(8,128)(2,1)S(1)}, bf16[16,256,640]{2,1,0:T(8,128)(2,1)S(1)}) custom-call(bf16[16,128,2432]{2,1,0:T(8,128)(2,1)S(1)} %bands.2.band_ref, bf16[1024,1024]{1,0:T(8,128)(2,1)S(1)} %copy-done.2, bf16[1024,1024]{1,0:T(8,128)(2,1)S(1)} %copy-done, ...), custom_call_target="tpu_custom_call" | custom-call | flops 4831838208 | bytes 16777216 | tf_op jit(solution)/shard_map/forward/pallas_call | solution.py:261
  73.5 10.4 %kernel_grad.1 = f32[16,2176]{1,0:T(8,128)S(1)} custom-call(f32[1,1024]{1,0:T(1,128)S(1)} %get-tuple-element.68.gain_ref, bf16[16,256,768]{2,1,0:T(8,128)(2,1)S(1)} %get-tuple-element.69.even_ref, bf16[16,256,640]{2,1,0:T(8,128)(2,1)S(1)} %get-tuple-element.70.odd_ref, bf16[256,1024]{1,0:T(8,128)(2,1)S(1)} %collective-permute-done.1.last_ref, ...), custom_call_target="tpu_custom_call" | custom-call | flops 4831838208 | bytes 8388608 | tf_op jit(solution)/shard_map/kernel_grad/pallas_call | solution.py:474
  85.8 2.8 %collective-permute-start.13 = (bf16[16,2176]{1,0:T(8,128)(2,1)S(1)}, bf16[16,2176]{1,0:T(8,128)(2,1)S(1)}, u32[]{:S(2)}, u32[]{:S(2)}) collective-permute-start(bf16[16,2176]{1,0:T(8,128)(2,1)S(1)} %convert_element_type.26), channel_id=1, source_target_pairs={{0,8},{2,10},{4,12},{6,14},{8,0},{10,2},{12,4},{14,6},{16,24},{18,... | collective-permute-start | bytes 208904 | tf_op jit(solution)/shard_map/ppermute | solution.py:574
  90.9 3.1 %collective-permute-start.14 = (bf16[16,2176]{1,0:T(8,128)(2,1)S(1)}, bf16[16,2176]{1,0:T(8,128)(2,1)S(1)}, u32[]{:S(2)}, u32[]{:S(2)}) collective-permute-start(bf16[16,2176]{1,0:T(8,128)(2,1)S(1)} %add_convert_fusion), channel_id=1, source_target_pairs={{0,16},{2,18},{4,20},{6,22},{8,24},{10,26},{12,28},{14,30},{16,0},... | collective-permute-start | bytes 208904 | tf_op jit(solution)/shard_map/ppermute | solution.py:574
  96.6 4.3 %collective-permute-start.16 = (bf16[256,1024]{1,0:T(8,128)(2,1)S(1)}, bf16[256,1024]{1,0:T(8,128)(2,1)S(1)}, u32[]{:S(2)}, u32[]{:S(2)}) collective-permute-start(bf16[256,1024]{1,0:T(8,128)(2,1)S(1)} %collective-permute-done.10.refs_4_), channel_id=1, source_target_pairs={{0,4},{4,8},{6,2},{8,12},{10,6},{12,16},{14,10},{16,20},{18,14},{2... | collective-permute-start | bytes 1572872 | tf_op jit(solution)/shard_map/ppermute | solution.py:566
  101.0 7.9 %collective-permute-done.11.refs_5_ = bf16[256,1024]{1,0:T(8,128)(2,1)S(1)} collective-permute-done((bf16[256,1024]{1,0:T(8,128)(2,1)S(1)}, bf16[256,1024]{1,0:T(8,128)(2,1)S(1)}, u32[]{:S(2)}, u32[]{:S(2)}) %collective-permute-start.11) | collective-permute-done | bytes 524320 | tf_op jit(solution)/shard_map/ppermute | solution.py:560
  108.8 3.2 %collective-permute-start.17 = (bf16[256,1024]{1,0:T(8,128)(2,1)S(1)}, bf16[256,1024]{1,0:T(8,128)(2,1)S(1)}, u32[]{:S(2)}, u32[]{:S(2)}) collective-permute-start(bf16[256,1024]{1,0:T(8,128)(2,1)S(1)} %collective-permute-done.11.refs_5_), channel_id=1, source_target_pairs={{0,4},{4,8},{6,2},{8,12},{10,6},{12,16},{14,10},{16,20},{18,14},{2... | collective-permute-start | bytes 1572872 | tf_op jit(solution)/shard_map/ppermute | solution.py:566
  112.0 16.1 %collective-permute-done.15.refs_6_ = bf16[256,1024]{1,0:T(8,128)(2,1)S(1)} collective-permute-done((bf16[256,1024]{1,0:T(8,128)(2,1)S(1)}, bf16[256,1024]{1,0:T(8,128)(2,1)S(1)}, u32[]{:S(2)}, u32[]{:S(2)}) %collective-permute-start.15) | collective-permute-done | bytes 524320 | tf_op jit(solution)/shard_map/ppermute | solution.py:560
  128.2 3.5 %collective-permute-start.18 = (bf16[256,1024]{1,0:T(8,128)(2,1)S(1)}, bf16[256,1024]{1,0:T(8,128)(2,1)S(1)}, u32[]{:S(2)}, u32[]{:S(2)}) collective-permute-start(bf16[256,1024]{1,0:T(8,128)(2,1)S(1)} %collective-permute-done.15.refs_6_), channel_id=1, source_target_pairs={{0,4},{4,8},{6,2},{8,12},{10,6},{12,16},{14,10},{16,20},{18,14},{2... | collective-permute-start | bytes 1572872 | tf_op jit(solution)/shard_map/ppermute | solution.py:566
  131.7 3.1 %bands.3.band_ref = bf16[16,128,2432]{2,1,0:T(8,128)(2,1)S(1)} custom-call(f32[8,2,2304]{2,1,0:T(2,128)S(1)} %reshape.23.row_ref), custom_call_target="tpu_custom_call" | custom-call | flops 4718592 | bytes 9437184 | tf_op jit(solution)/shard_map/bands/pallas_call | solution.py:84
  134.8 4.6 %norm.1 = (bf16[1024,1024]{1,0:T(8,128)(2,1)}, bf16[1024,1024]{1,0:T(8,128)(2,1)}) custom-call(f32[2,1024]{1,0:T(2,128)S(1)} %add.22.sums_ref, f32[1024,1024]{1,0:T(8,128)S(1)} %get-tuple-element.51.mixed_ref, f32[256,1024]{1,0:T(8,128)S(1)} %get-tuple-element.54.first_ref, bf16[1024,1024]{1,0:T(8,128)(2,1)S(1)} %copy-done, ...), custom_call_target="tpu_custom_call" | custom-call | flops 14680064 | bytes 12582912 | tf_op jit(solution)/shard_map/norm/pallas_call | solution.py:396
  139.4 3.3 %collective-permute-start.12 = (bf16[256,1024]{1,0:T(8,128)(2,1)S(1)}, bf16[256,1024]{1,0:T(8,128)(2,1)S(1)}, u32[]{:S(2)}, u32[]{:S(2)}) collective-permute-start(bf16[256,1024]{1,0:T(8,128)(2,1)S(1)} %collective-permute-done.9.refs_7_), channel_id=1, source_target_pairs={{0,4},{4,8},{6,2},{8,12},{10,6},{12,16},{14,10},{16,20},{18,14},{2... | collective-permute-start | bytes 1572872 | tf_op jit(solution)/shard_map/ppermute | solution.py:566
  143.5 2.8 %collective-permute-start.21 = (f32[16,2176]{1,0:T(8,128)S(1)}, f32[16,2176]{1,0:T(8,128)S(1)}, u32[]{:S(2)}, u32[]{:S(2)}) collective-permute-start(f32[16,2176]{1,0:T(8,128)S(1)} %convert_add_fusion), channel_id=1, source_target_pairs={{0,6},{2,4},{4,2},{6,0},{8,14},{10,12},{12,10},{14,8},{16,22},{18,... | collective-permute-start | bytes 417800 | tf_op jit(solution)/shard_map/ppermute | solution.py:574
  146.3 10.3 %value_grad.1 = (bf16[1024,1024]{1,0:T(8,128)(2,1)}, f32[256,1024]{1,0:T(8,128)S(1)}) custom-call(bf16[16,128,2432]{2,1,0:T(8,128)(2,1)S(1)} %bands.3.band_ref, bf16[256,1024]{1,0:T(8,128)(2,1)S(1)} %get-tuple-element.56.refs_0_, bf16[256,1024]{1,0:T(8,128)(2,1)S(1)} %get-tuple-element.61.refs_1_, bf16[256,1024]{1,0:T(8,128)(2,1)S(1)} %get-tuple-element.67.refs_2_, ...), custom_call_target="tpu_custom_call" | custom-call | flops 4831838208 | bytes 12582912 | tf_op jit(solution)/shard_map/value_grad/pallas_call | solution.py:512
  (53 shorter events, 26.2 us)
Async XLA Ops:
  3.0 16.0 %collective-permute-start.2 = (bf16[256,1024]{1,0:T(8,128)(2,1)}, bf16[256,1024]{1,0:T(8,128)(2,1)S(1)}, u32[]{:S(2)}, u32[]{:S(2)}) collective-permute-start(bf16[256,1024]{1,0:T(8,128)(2,1)} %get-tuple-element.48), channel_id=1, source_target_pairs={{0,2},{2,0},{4,6},{6,4},{8,10},{10,8},{12,14},{14,12},{16,18},{18,... | collective-permute-start | bytes 1572872 | tf_op jit(solution)/shard_map/ppermute | solution.py:560
  6.0 24.2 %collective-permute-start.3 = (bf16[256,1024]{1,0:T(8,128)(2,1)S(1)}, bf16[256,1024]{1,0:T(8,128)(2,1)S(1)}, u32[]{:S(2)}, u32[]{:S(2)}) collective-permute-start(bf16[256,1024]{1,0:T(8,128)(2,1)S(1)} %get-tuple-element.49), channel_id=1, source_target_pairs={{0,2},{2,0},{4,6},{6,4},{8,10},{10,8},{12,14},{14,12},{16,18},{18,... | collective-permute-start | bytes 1572872 | tf_op jit(solution)/shard_map/ppermute | solution.py:560
  6.1 35.4 %collective-permute-start.4 = (bf16[256,1024]{1,0:T(8,128)(2,1)S(1)}, bf16[256,1024]{1,0:T(8,128)(2,1)S(1)}, u32[]{:S(2)}, u32[]{:S(2)}) collective-permute-start(bf16[256,1024]{1,0:T(8,128)(2,1)S(1)} %get-tuple-element.50), channel_id=1, source_target_pairs={{0,2},{2,0},{4,6},{6,4},{8,10},{10,8},{12,14},{14,12},{16,18},{18,... | collective-permute-start | bytes 1572872 | tf_op jit(solution)/shard_map/ppermute | solution.py:560
  11.1 44.5 %copy-start = (bf16[1024,1024]{1,0:T(8,128)(2,1)S(1)}, bf16[1024,1024]{1,0:T(8,128)(2,1)}, u32[]{:S(2)}) copy-start(bf16[1024,1024]{1,0:T(8,128)(2,1)} %gate_ref.7) | copy-start | bytes 6291460
  11.1 44.5 %copy-start.1 = (bf16[1024,1024]{1,0:T(8,128)(2,1)S(1)}, bf16[1024,1024]{1,0:T(8,128)(2,1)}, u32[]{:S(2)}) copy-start(bf16[1024,1024]{1,0:T(8,128)(2,1)} %grad_ref.7) | copy-start | bytes 6291460
  14.3 37.6 %collective-permute-start = (bf16[256,1024]{1,0:T(8,128)(2,1)S(1)}, bf16[256,1024]{1,0:T(8,128)(2,1)S(1)}, u32[]{:S(2)}, u32[]{:S(2)}) collective-permute-start(bf16[256,1024]{1,0:T(8,128)(2,1)S(1)} %get-tuple-element.47), channel_id=1, source_target_pairs={{0,2},{2,0},{4,6},{6,4},{8,10},{10,8},{12,14},{14,12},{16,18},{18,... | collective-permute-start | bytes 1572872 | tf_op jit(solution)/shard_map/ppermute | solution.py:560
  19.0 36.6 %collective-permute-start.5 = (bf16[256,1024]{1,0:T(8,128)(2,1)S(1)}, bf16[256,1024]{1,0:T(8,128)(2,1)S(1)}, u32[]{:S(2)}, u32[]{:S(2)}) collective-permute-start(bf16[256,1024]{1,0:T(8,128)(2,1)S(1)} %collective-permute-done.2.refs_0_), channel_id=1, source_target_pairs={{0,4},{4,8},{6,2},{8,12},{10,6},{12,16},{14,10},{16,20},{18,14},{2... | collective-permute-start | bytes 1572872 | tf_op jit(solution)/shard_map/ppermute | solution.py:566
  30.2 25.4 %collective-permute-start.6 = (bf16[256,1024]{1,0:T(8,128)(2,1)S(1)}, bf16[256,1024]{1,0:T(8,128)(2,1)S(1)}, u32[]{:S(2)}, u32[]{:S(2)}) collective-permute-start(bf16[256,1024]{1,0:T(8,128)(2,1)S(1)} %collective-permute-done.3.refs_1_), channel_id=1, source_target_pairs={{0,4},{4,8},{6,2},{8,12},{10,6},{12,16},{14,10},{16,20},{18,14},{2... | collective-permute-start | bytes 1572872 | tf_op jit(solution)/shard_map/ppermute | solution.py:566
  41.5 14.1 %collective-permute-start.7 = (bf16[256,1024]{1,0:T(8,128)(2,1)S(1)}, bf16[256,1024]{1,0:T(8,128)(2,1)S(1)}, u32[]{:S(2)}, u32[]{:S(2)}) collective-permute-start(bf16[256,1024]{1,0:T(8,128)(2,1)S(1)} %collective-permute-done.4.refs_2_), channel_id=1, source_target_pairs={{0,4},{4,8},{6,2},{8,12},{10,6},{12,16},{14,10},{16,20},{18,14},{2... | collective-permute-start | bytes 1572872 | tf_op jit(solution)/shard_map/ppermute | solution.py:566
  51.9 14.4 %collective-permute-start.1 = (bf16[256,1024]{1,0:T(8,128)(2,1)S(1)}, bf16[256,1024]{1,0:T(8,128)(2,1)S(1)}, u32[]{:S(2)}, u32[]{:S(2)}) collective-permute-start(bf16[256,1024]{1,0:T(8,128)(2,1)S(1)} %collective-permute-done.refs_3_), channel_id=1, source_target_pairs={{0,4},{4,8},{6,2},{8,12},{10,6},{12,16},{14,10},{16,20},{18,14},{2... | collective-permute-start | bytes 1572872 | tf_op jit(solution)/shard_map/ppermute | solution.py:566
  68.4 1.2 collective-permute-start.8
  71.5 14.3 %collective-permute-start.10 = (bf16[256,1024]{1,0:T(8,128)(2,1)S(1)}, bf16[256,1024]{1,0:T(8,128)(2,1)S(1)}, u32[]{:S(2)}, u32[]{:S(2)}) collective-permute-start(bf16[256,1024]{1,0:T(8,128)(2,1)S(1)} %get-tuple-element.56.refs_0_), channel_id=1, source_target_pairs={{0,2},{2,0},{4,6},{6,4},{8,10},{10,8},{12,14},{14,12},{16,18},{18,... | collective-permute-start | bytes 1572872 | tf_op jit(solution)/shard_map/ppermute | solution.py:560
  85.8 5.1 %collective-permute-start.13 = (bf16[16,2176]{1,0:T(8,128)(2,1)S(1)}, bf16[16,2176]{1,0:T(8,128)(2,1)S(1)}, u32[]{:S(2)}, u32[]{:S(2)}) collective-permute-start(bf16[16,2176]{1,0:T(8,128)(2,1)S(1)} %convert_element_type.26), channel_id=1, source_target_pairs={{0,8},{2,10},{4,12},{6,14},{8,0},{10,2},{12,4},{14,6},{16,24},{18,... | collective-permute-start | bytes 208904 | tf_op jit(solution)/shard_map/ppermute | solution.py:574
  90.9 10.1 %collective-permute-start.14 = (bf16[16,2176]{1,0:T(8,128)(2,1)S(1)}, bf16[16,2176]{1,0:T(8,128)(2,1)S(1)}, u32[]{:S(2)}, u32[]{:S(2)}) collective-permute-start(bf16[16,2176]{1,0:T(8,128)(2,1)S(1)} %add_convert_fusion), channel_id=1, source_target_pairs={{0,16},{2,18},{4,20},{6,22},{8,24},{10,26},{12,28},{14,30},{16,0},... | collective-permute-start | bytes 208904 | tf_op jit(solution)/shard_map/ppermute | solution.py:574
  94.0 14.9 %collective-permute-start.11 = (bf16[256,1024]{1,0:T(8,128)(2,1)S(1)}, bf16[256,1024]{1,0:T(8,128)(2,1)S(1)}, u32[]{:S(2)}, u32[]{:S(2)}) collective-permute-start(bf16[256,1024]{1,0:T(8,128)(2,1)S(1)} %get-tuple-element.61.refs_1_), channel_id=1, source_target_pairs={{0,2},{2,0},{4,6},{6,4},{8,10},{10,8},{12,14},{14,12},{16,18},{18,... | collective-permute-start | bytes 1572872 | tf_op jit(solution)/shard_map/ppermute | solution.py:560
  94.6 44.8 %collective-permute-start.9 = (bf16[256,1024]{1,0:T(8,128)(2,1)S(1)}, bf16[256,1024]{1,0:T(8,128)(2,1)S(1)}, u32[]{:S(2)}, u32[]{:S(2)}) collective-permute-start(bf16[256,1024]{1,0:T(8,128)(2,1)S(1)} %get-tuple-element.55.refs_3_), channel_id=1, source_target_pairs={{0,2},{2,0},{4,6},{6,4},{8,10},{10,8},{12,14},{14,12},{16,18},{18,... | collective-permute-start | bytes 1572872 | tf_op jit(solution)/shard_map/ppermute | solution.py:560
  96.0 32.2 %collective-permute-start.15 = (bf16[256,1024]{1,0:T(8,128)(2,1)S(1)}, bf16[256,1024]{1,0:T(8,128)(2,1)S(1)}, u32[]{:S(2)}, u32[]{:S(2)}) collective-permute-start(bf16[256,1024]{1,0:T(8,128)(2,1)S(1)} %get-tuple-element.67.refs_2_), channel_id=1, source_target_pairs={{0,2},{2,0},{4,6},{6,4},{8,10},{10,8},{12,14},{14,12},{16,18},{18,... | collective-permute-start | bytes 1572872 | tf_op jit(solution)/shard_map/ppermute | solution.py:560
  96.6 46.2 %collective-permute-start.16 = (bf16[256,1024]{1,0:T(8,128)(2,1)S(1)}, bf16[256,1024]{1,0:T(8,128)(2,1)S(1)}, u32[]{:S(2)}, u32[]{:S(2)}) collective-permute-start(bf16[256,1024]{1,0:T(8,128)(2,1)S(1)} %collective-permute-done.10.refs_4_), channel_id=1, source_target_pairs={{0,4},{4,8},{6,2},{8,12},{10,6},{12,16},{14,10},{16,20},{18,14},{2... | collective-permute-start | bytes 1572872 | tf_op jit(solution)/shard_map/ppermute | solution.py:566
  108.8 33.9 %collective-permute-start.17 = (bf16[256,1024]{1,0:T(8,128)(2,1)S(1)}, bf16[256,1024]{1,0:T(8,128)(2,1)S(1)}, u32[]{:S(2)}, u32[]{:S(2)}) collective-permute-start(bf16[256,1024]{1,0:T(8,128)(2,1)S(1)} %collective-permute-done.11.refs_5_), channel_id=1, source_target_pairs={{0,4},{4,8},{6,2},{8,12},{10,6},{12,16},{14,10},{16,20},{18,14},{2... | collective-permute-start | bytes 1572872 | tf_op jit(solution)/shard_map/ppermute | solution.py:566
  128.2 18.2 %collective-permute-start.18 = (bf16[256,1024]{1,0:T(8,128)(2,1)S(1)}, bf16[256,1024]{1,0:T(8,128)(2,1)S(1)}, u32[]{:S(2)}, u32[]{:S(2)}) collective-permute-start(bf16[256,1024]{1,0:T(8,128)(2,1)S(1)} %collective-permute-done.15.refs_6_), channel_id=1, source_target_pairs={{0,4},{4,8},{6,2},{8,12},{10,6},{12,16},{14,10},{16,20},{18,14},{2... | collective-permute-start | bytes 1572872 | tf_op jit(solution)/shard_map/ppermute | solution.py:566
  139.4 17.2 %collective-permute-start.12 = (bf16[256,1024]{1,0:T(8,128)(2,1)S(1)}, bf16[256,1024]{1,0:T(8,128)(2,1)S(1)}, u32[]{:S(2)}, u32[]{:S(2)}) collective-permute-start(bf16[256,1024]{1,0:T(8,128)(2,1)S(1)} %collective-permute-done.9.refs_7_), channel_id=1, source_target_pairs={{0,4},{4,8},{6,2},{8,12},{10,6},{12,16},{14,10},{16,20},{18,14},{2... | collective-permute-start | bytes 1572872 | tf_op jit(solution)/shard_map/ppermute | solution.py:566
  142.8 16.4 %collective-permute-start.19 = (f32[16,2176]{1,0:T(8,128)S(1)}, f32[16,2176]{1,0:T(8,128)S(1)}, u32[]{:S(2)}, u32[]{:S(2)}) collective-permute-start(f32[16,2176]{1,0:T(8,128)S(1)} %convert_add_fusion), channel_id=1, source_target_pairs={{0,2},{2,0},{4,6},{6,4},{8,10},{10,8},{12,14},{14,12},{16,18},{18,... | collective-permute-start | bytes 417800 | tf_op jit(solution)/shard_map/ppermute | solution.py:574
  142.8 16.4 %collective-permute-start.20 = (f32[16,2176]{1,0:T(8,128)S(1)}, f32[16,2176]{1,0:T(8,128)S(1)}, u32[]{:S(2)}, u32[]{:S(2)}) collective-permute-start(f32[16,2176]{1,0:T(8,128)S(1)} %convert_add_fusion), channel_id=1, source_target_pairs={{0,4},{2,6},{4,0},{6,2},{8,12},{10,14},{12,8},{14,10},{16,20},{18,... | collective-permute-start | bytes 417800 | tf_op jit(solution)/shard_map/ppermute | solution.py:574
  143.5 15.7 %collective-permute-start.21 = (f32[16,2176]{1,0:T(8,128)S(1)}, f32[16,2176]{1,0:T(8,128)S(1)}, u32[]{:S(2)}, u32[]{:S(2)}) collective-permute-start(f32[16,2176]{1,0:T(8,128)S(1)} %convert_add_fusion), channel_id=1, source_target_pairs={{0,6},{2,4},{4,2},{6,0},{8,14},{10,12},{12,10},{14,8},{16,22},{18,... | collective-permute-start | bytes 417800 | tf_op jit(solution)/shard_map/ppermute | solution.py:574
  (3 other events, 96.4 us)
